TPU v7x, 32 devices: a whole 2x2x4 slice. The times are simulated.
32 devices in a mesh: fsdp: 8 (over z, y), seq: 4 (over x, core).
Axes of the slice: x: 2, y: 2, z: 4, core: 2. Of those that a mesh axis runs over, the one named last changes fastest.
Arguments:
- latents: bfloat16 [16, 512, 1152], P('fsdp', 'seq'), may hold values from -6 to 6
- condition: bfloat16 [16, 1152], P('fsdp'), may hold values from -6 to 6
- mod_weight: bfloat16 [1152, 6912], P('fsdp'), may hold values from -0.1875 to 0.1875
- mod_bias: bfloat16 [6912], P('fsdp'), may hold values from -4 to 4
- qkv_weight: bfloat16 [1152, 3456], P('fsdp'), may hold values from -0.1875 to 0.1875
- qv_bias: bfloat16 [2304], P('fsdp'), may hold values from -4 to 4
- out_weight: bfloat16 [1152, 1152], P('fsdp'), may hold values from -1.5 to 1.5
- out_bias: bfloat16 [1152], P('fsdp'), may hold values from -4 to 4
- up_weight: bfloat16 [1152, 4608], P('fsdp'), may hold values from -0.1875 to 0.1875
- up_bias: bfloat16 [4608], P('fsdp'), may hold values from -4 to 4
- down_weight: bfloat16 [4608, 1152], P('fsdp'), may hold values from -0.09375 to 0.09375
- down_bias: bfloat16 [1152], P('fsdp'), may hold values from -4 to 4
- cotangent: bfloat16 [16, 512, 1152], P('fsdp', 'seq'), may hold values from -6 to 6
Outputs:
- mixed: bfloat16 [16, 512, 1152], P('fsdp', 'seq')
- grad_latents: float32 [16, 512, 1152], P('fsdp', 'seq')
- grad_condition: float32 [16, 1152], P('fsdp')
- grad_mod_weight: float32 [1152, 6912], P('fsdp')
- grad_mod_bias: float32 [6912], P('fsdp')
- grad_qkv_weight: float32 [1152, 3456], P('fsdp')
- grad_qv_bias: float32 [2304], P('fsdp')
- grad_out_weight: float32 [1152, 1152], P('fsdp')
- grad_out_bias: float32 [1152], P('fsdp')
- grad_up_weight: float32 [1152, 4608], P('fsdp')
- grad_up_bias: float32 [4608], P('fsdp')
- grad_down_weight: float32 [4608, 1152], P('fsdp')
- grad_down_bias: float32 [1152], P('fsdp')
All inputs are finite; a program needn't handle non-finite values.
Results may differ from a plain program's by a relative error of at most 0.015.
The roundings to bfloat16 on the way count: a program that leaves them out, or rounds other values in their place, can miss the bound.
Values may be sent and summed in bfloat16 or wider, within the bound.
No kernel may reach another device: no remote copies, remote signals or barrier semaphores. Data moves between devices by JAX's collectives and lax.ppermute only.
A program may use at most 256 MiB of HBM per device.

v0:
```python
import jax
import jax.numpy as jnp
from jax import lax
from jax.experimental import pallas as pl
from jax.experimental.pallas import tpu as pltpu
from jax.sharding import PartitionSpec as P

H = 16
HD = 72
GELU_ROOT = (2.0 / 3.141592653589793) ** 0.5
GELU_CUBE = 0.044715
SEAT, CORE, PAIR, LINE = range(4)
HEAD = 16

SCALARS = pl.BlockSpec(memory_space=pltpu.SMEM)
WHOLE = pl.BlockSpec(memory_space=pltpu.VMEM)
ANY = pl.BlockSpec(memory_space=pl.ANY)
ROOM = pltpu.CompilerParams(vmem_limit_bytes=20 << 20)
SHORT = pl.CostEstimate(flops=1, transcendentals=0, bytes_accessed=1)


def low(values):
    return values.astype(jnp.bfloat16)


def wide(values):
    return values.astype(jnp.float32)


def struct(shape, dtype):
    return jax.ShapeDtypeStruct(shape, dtype)


def whole(shape):
    return pl.BlockSpec(shape, lambda step: (0,) * len(shape))


def column_block(shape, columns):
    return pl.BlockSpec(shape[:-1] + (columns,), lambda step: (0,) * (len(shape) - 1) + (step,))


def row_block(shape, rows):
    return pl.BlockSpec((rows,) + shape[1:], lambda step: (step,) + (0,) * (len(shape) - 1))


def dot(left_side, right_side, left_dim, right_dim):
    return lax.dot_general(
        left_side,
        right_side,
        (((left_dim,), (right_dim,)), ((), ())),
        preferred_element_type=jnp.float32,
    )


def normalize_back(normed, inverse, grad):
    inner = jnp.mean(grad * normed, axis=-1, keepdims=True)
    return (grad - jnp.mean(grad, axis=-1, keepdims=True) - normed * inner) * inverse


def soft_columns(queries, keys):
    scores = dot(keys, queries, 0, 0) * HD ** (-0.5)
    raised = jnp.exp(scores - jnp.max(scores, axis=0, keepdims=True))
    return raised * (1.0 / jnp.sum(raised, axis=0, keepdims=True))


def pick(values, index, axis):
    return lax.dynamic_index_in_dim(values, index, axis, keepdims=False)


class Order:
    def __init__(self, place):
        self.place = place
        self.token = jnp.zeros((8, 128), jnp.float32)

    def wait(self, *values):
        self.token, values = lax.optimization_barrier((self.token, values))
        return values if len(values) > 1 else values[0]

    def run(self, kernel, outs, *args, grid=(), in_specs=None, out_specs=None, scratch=()):
        count, given = len(outs), len(args)

        def body(place, *refs):
            kernel(place, *refs[:given], *refs[given + 1 : given + 1 + count], *refs[given + 2 + count :])

        results = pl.pallas_call(
            body,
            out_shape=tuple(outs) + (struct(self.token.shape, self.token.dtype),),
            grid=grid,
            in_specs=[SCALARS] + list(in_specs or [WHOLE] * given) + [ANY],
            out_specs=tuple(out_specs or [WHOLE] * count) + (ANY,),
            scratch_shapes=scratch,
            input_output_aliases={given + 1: count},
            compiler_params=ROOM,
            cost_estimate=SHORT,
        )(self.place, *args, self.token)
        self.token = results[-1]
        return results[:-1] if count > 1 else results[0]

    def pass_on(self, blocks, step, sums):
        lines, rows, columns = blocks[0].shape
        count = len(blocks)

        def kernel(place, *refs):
            outs = refs[-1 - count : -1]
            for index in range(count):
                result = refs[index][0]
                if sums:
                    result = low(wide(result) + wide(refs[count + index][...]))
                outs[index][...] = result

        def block_at(unused, place):
            return (lax.rem(place[LINE] + (lines - step), lines), 0, 0)

        piece = pl.BlockSpec((rows, columns), lambda unused, place: (0, 0))
        spec = pltpu.PrefetchScalarGridSpec(
            num_scalar_prefetch=1,
            grid=(1,),
            in_specs=[pl.BlockSpec((1, rows, columns), block_at)] * count
            + [piece] * len(sums)
            + [ANY],
            out_specs=(piece,) * count + (ANY,),
        )
        results = pl.pallas_call(
            kernel,
            grid_spec=spec,
            out_shape=(struct((rows, columns), jnp.bfloat16),) * count
            + (struct(self.token.shape, self.token.dtype),),
            input_output_aliases={1 + count + len(sums): count},
            compiler_params=ROOM,
            cost_estimate=SHORT,
        )(self.place, *blocks, *sums, self.token)
        self.token = results[-1]
        return results[:-1]


class Place:
    def __init__(self):
        self.shards = lax.axis_size("fsdp")
        self.seats = lax.axis_size("seq")
        self.line_size = self.shards // 2
        self.shard = lax.axis_index("fsdp")
        self.seat = lax.axis_index("seq")
        self.core = self.seat % 2
        places = [self.seat, self.core, self.shard % 2, self.shard // 2]
        self.place = jnp.stack(places).astype(jnp.int32)

    def to_core(self, values):
        return lax.ppermute(values, "seq", [(i, i ^ 1) for i in range(self.seats)])

    def to_side(self, values):
        return lax.ppermute(values, "seq", [(i, i ^ 2) for i in range(self.seats)])

    def to_pair(self, values):
        return lax.ppermute(values, "fsdp", [(i, i ^ 1) for i in range(self.shards)])

    def to_line(self, values):
        return lax.ppermute(
            values, "fsdp", [(i, (i + 2) % self.shards) for i in range(self.shards)]
        )

    def exchange(self, values):
        results = [values[0]]
        for step in range(1, self.shards):
            shift = [(i, (i + step) % self.shards) for i in range(self.shards)]
            results.append(lax.ppermute(values[step], "fsdp", shift))
        return results


class Gather:
    def __init__(self, here, order, piece, near=False, hold=False):
        self.here, self.order, self.near = here, order, near
        self.pieces, self.copies = [], []
        self.steps, self.pending = 0, []
        self.send([piece], hold)

    def send(self, pieces, hold=False):
        here = self.here
        self.pieces += pieces
        sent = []
        if self.steps < here.line_size:
            if self.steps + 1 < here.line_size:
                sent.append(here.to_line(pieces[0]))
            if not hold:
                sent.append(here.to_pair(pieces[0]))
        self.steps += 1
        self.copied = [here.to_core(piece) for piece in pieces] if self.near else []
        self.pending = sent

    def release(self):
        self.pending.append(self.here.to_pair(self.order.wait(self.pieces[0])))

    def turn(self):
        if self.pending:
            arrived = self.order.wait(*self.pending, *self.copied)
            arrived = list(arrived) if len(self.pending) + len(self.copied) > 1 else [arrived]
            count = len(self.pending)
            self.copies += arrived[count:]
            self.send(arrived[:count])

    def finish(self, widths, head=0, keep_head=False):
        while self.pending:
            self.turn()
        return self.place(self.pieces, widths, head, keep_head)

    def finish_near(self, widths, head=0):
        return self.place(self.copies + [self.order.wait(*self.copied)], widths, head, False)

    def place(self, pieces, widths, head, keep_head):
        shards, lines = self.here.shards, self.here.line_size
        rows, total = pieces[0].shape
        rows -= head

        def kernel(place, *refs):
            targets = refs[shards:]
            for index in range(shards):
                near = index > 0 and (index % 2 == 0 or index == shards - 1)
                back = (index - 1) // 2 if near else (index + 1) // 2
                line = lax.rem(place[LINE] + (lines - back), lines)
                pair = 1 - place[PAIR] if near else place[PAIR]
                shard = 2 * line + pair
                start = 0
                for target, columns in zip(targets, widths):
                    target[shard] = refs[index][head:, start : start + columns]
                    start += columns
                if keep_head:
                    targets[-1][shard] = refs[index][:head, :]

        outs = [struct((shards, rows, columns), pieces[0].dtype) for columns in widths]
        if keep_head:
            outs.append(struct((shards, head, total), pieces[0].dtype))
        return self.order.run(kernel, outs, *pieces)


class Scatter:
    def __init__(self, here, order, give, mine):
        self.here, self.order, self.mine = here, order, mine
        self.got = here.to_pair(give)
        self.step = 0

    def join(self):
        got = self.order.wait(self.got)

        def kernel(place, got_ref, mine_ref, out):
            out[...] = low(wide(mine_ref[...]) + wide(got_ref[...]))

        shape = struct(self.mine.shape, jnp.bfloat16)
        self.kept = [self.order.run(kernel, [shape], got, self.mine)]
        self.sums = []
        self.send()

    def send(self):
        self.step += 1
        sums = self.order.pass_on(self.kept, self.step, self.sums)
        if self.step < self.here.line_size:
            sums = [self.here.to_line(total) for total in sums]
        self.sums = sums

    def turn(self):
        if self.step < self.here.line_size:
            sums = self.order.wait(*self.sums)
            self.sums = list(sums) if len(self.kept) > 1 else [sums]
            self.send()

    def finish(self):
        while self.step < self.here.line_size:
            self.turn()
        return self.sums[0]


class ScatterLines(Scatter):
    def __init__(self, here, order, both):
        self.here, self.order, self.step = here, order, 0
        self.kept, self.sums = [both], []
        self.send()

    def join(self):
        while self.step < self.here.line_size:
            self.turn()
        total = self.sums[0]
        rows = total.shape[0] // 2
        self.mine = total[rows:]
        self.got = self.here.to_pair(total[:rows])

    def finish(self):
        got = self.order.wait(self.got)

        def kernel(place, got_ref, mine_ref, out):
            out[...] = low(wide(mine_ref[...]) + wide(got_ref[...]))

        shape = struct(got.shape, jnp.bfloat16)
        return self.order.run(kernel, [shape], got, self.mine)


def cut_columns(place, source, target, offset, index, parts, groups):
    part = source.shape[1] // groups // parts
    for choice in range(parts):

        @pl.when(index == choice)
        def _():
            for group in range(groups):
                start = (group * parts + choice) * part
                goal = offset + group * part
                target[:, goal : goal + part] = source[:, start : start + part]


def cut_attention(order, condition, biases, qkv_weight, out_weight):
    rows, width = out_weight.shape
    columns = qkv_weight.shape[1] // 4
    total = columns + width // 2
    micros = condition.shape[0]

    def kernel(place, condition_ref, biases_ref, qkv_ref, out_ref, target, held):
        held[...] = jnp.zeros(held.shape, jnp.float32)
        held[:micros, :width] = wide(condition_ref[...])
        for row, start in enumerate(range(0, biases.shape[1], total)):
            count = min(total, biases.shape[1] - start)
            held[micros + row : micros + row + 1, :count] = wide(
                biases_ref[:, start : start + count]
            )
        target[:HEAD, :] = low(held[...])
        rest = target.at[HEAD:, :]
        cut_columns(place, qkv_ref, rest, 0, place[SEAT], 4, 3)
        cut_columns(place, out_ref, rest, columns, place[CORE], 2, 1)

    return order.run(
        kernel,
        [struct((HEAD + rows, total), qkv_weight.dtype)],
        condition,
        biases,
        qkv_weight,
        out_weight,
        scratch=(pltpu.VMEM((HEAD, total), jnp.float32),),
    )


def modulation_parts(order, heads, mod_weight, micros, width, hidden):
    shards, head, total = heads.shape
    rows, columns = mod_weight.shape
    part = H // 4 * HD
    block = hidden // shards // 4
    sizes = {"mod": columns, "qv": 2 * width, "out": width, "up": hidden, "down": width}

    def kernel(place, heads_ref, weight_ref, *refs):
        cond_rows, mod_bias, qkv_mine, qkv_near, out_bias, up_mine, up_near, down_bias = refs[:8]
        parts, (cond, mine, products) = refs[8 : 8 + shards], refs[8 + shards :]
        shard = 2 * place[LINE] + place[PAIR]
        for index in range(shards):
            values = wide(heads_ref[index, :micros, :width])
            values = wide(low(values / (1.0 + jnp.exp(-values))))
            cond[index * micros : (index + 1) * micros, :] = values
        for index in range(shards):

            @pl.when(shard == index)
            def _():
                mine[...] = low(cond[:, index * rows : (index + 1) * rows])

        cond_rows[...] = mine[...]
        products[...] = dot(mine[...], weight_ref[...], 1, 0)
        for step in range(shards):
            row = lax.rem(shard + step, shards) * micros + place[CORE]
            parts[step][...] = products[pl.ds(row, 1), :]

        def copy(target, row, column, name, start, count):
            base = 0
            for other, size in sizes.items():
                if other == name:
                    break
                base += size // shards
            share = sizes[name] // shards
            while count > 0:
                index, offset = divmod(start, share)
                line, lane = divmod(base + offset, total)
                length = min(count, share - offset, total - lane)
                source = heads_ref[index, micros + line : micros + line + 1, lane : lane + length]
                target[row : row + 1, column : column + length] = wide(source)
                start, column, count = start + length, column + length, count - length

        for row in range(6):
            copy(mod_bias, row, 0, "mod", row * width, width)
        copy(out_bias, 0, 0, "out", 0, width)
        copy(down_bias, 0, 0, "down", 0, width)
        for own in range(4):

            @pl.when(place[SEAT] == own)
            def _():
                for seat, qkv, up in ((own, qkv_mine, up_mine), (own ^ 1, qkv_near, up_near)):
                    copy(qkv, 0, 0, "qv", seat * part, part)
                    qkv[:, part : 2 * part] = jnp.zeros((1, part), jnp.float32)
                    copy(qkv, 0, 2 * part, "qv", width + seat * part, part)
                    for index in range(shards):
                        start = (index * 4 + seat) * block
                        copy(up, 0, index * block, "up", start, block)

    row = lambda count: struct((1, count), jnp.float32)
    outs = [
        struct((shards * micros, rows), jnp.bfloat16),
        struct((6, width), jnp.float32),
        row(3 * part),
        row(3 * part),
        row(width),
        row(shards * block),
        row(shards * block),
        row(width),
    ] + [row(columns)] * shards
    scratch = (
        pltpu.VMEM((shards * micros, width), jnp.float32),
        pltpu.VMEM((shards * micros, rows), jnp.bfloat16),
        pltpu.VMEM((shards * micros, columns), jnp.float32),
    )
    return order.run(kernel, outs, heads, mod_weight, scratch=scratch)


def token_sums(order, shards, attn, middle, mixed, down, qv_mine, qv_near, up_mine, up_near):
    width = attn.shape[1]
    part = qv_mine.shape[1] // 3
    hidden = 4 * up_mine.shape[1]
    block = hidden // shards // 4
    sizes = (2 * width // shards, width // shards, hidden // shards, width // shards)
    starts = [sum(sizes[:index]) for index in range(4)]

    def kernel(
        place, attn_ref, middle_ref, mixed_ref, down_ref, qv_mine_ref, qv_near_ref, up_mine_ref,
        up_near_ref, mods, biases,
    ):
        mods[0:2, :] = attn_ref[...]
        mods[2:3, :] = middle_ref[2:3, :]
        mods[3:5, :] = middle_ref[0:2, :]
        mods[5:6, :] = mixed_ref[...]
        biases[...] = jnp.zeros(biases.shape, jnp.float32)

        def copy(source, row, column, which, start, count):
            while count > 0:
                index, offset = divmod(start, sizes[which])
                length = min(count, sizes[which] - offset)
                goal = starts[which] + offset
                biases[index : index + 1, goal : goal + length] = source[
                    row : row + 1, column : column + length
                ]
                start, column, count = start + length, column + length, count - length

        copy(middle_ref, 3, 0, 1, 0, width)
        copy(down_ref, 0, 0, 3, 0, width)
        for own in range(4):

            @pl.when(place[SEAT] == own)
            def _():
                for seat, qv, up in (
                    (own, qv_mine_ref, up_mine_ref),
                    (own ^ 1, qv_near_ref, up_near_ref),
                ):
                    copy(qv, 0, 0, 0, seat * part, part)
                    copy(qv, 0, 2 * part, 0, width + seat * part, part)
                    for index in range(shards):
                        start = (index * 4 + seat) * block
                        copy(up, 0, index * block, 2, start, block)

    outs = (struct((6, width), jnp.float32), struct((shards, sum(sizes)), jnp.float32))
    return order.run(
        kernel, outs, attn, middle, mixed, down, qv_mine, qv_near, up_mine, up_near
    )


def add_sums(order, mods, biases, mods_far, biases_far):
    def kernel(place, mods_ref, biases_ref, mods_far_ref, biases_far_ref, mods_out, biases_out):
        mods_out[...] = mods_ref[...] + mods_far_ref[...]
        biases_out[...] = biases_ref[...] + biases_far_ref[...]

    outs = (struct(mods.shape, mods.dtype), struct(biases.shape, biases.dtype))
    return order.run(kernel, outs, mods, biases, mods_far, biases_far)


def sums_to_send(order, mods, biases, mods_near, biases_near):
    rows, width = mods.shape
    shards, columns = biases.shape

    def kernel(place, mods_ref, biases_ref, mods_near_ref, biases_near_ref, *refs):
        outs, (pair, total) = refs[:shards], refs[shards:]
        pair[place[CORE]] = wide(low(mods_ref[...]))
        pair[1 - place[CORE]] = wide(low(mods_near_ref[...]))
        total[...] = biases_ref[...] + biases_near_ref[...]
        shard = 2 * place[LINE] + place[PAIR]
        for step in range(shards):
            outs[step][:rows, :] = pair[0]
            outs[step][rows : 2 * rows, :] = pair[1]
            row = lax.rem(shard + step, shards)
            outs[step][2 * rows :, :] = jnp.zeros((HEAD - 2 * rows, width), jnp.float32)
            outs[step][2 * rows : 2 * rows + 1, :columns] = total[pl.ds(row, 1), :]

    outs = [struct((HEAD, width), jnp.float32)] * shards
    scratch = (
        pltpu.VMEM((2, rows, width), jnp.float32),
        pltpu.VMEM((shards, columns), jnp.float32),
    )
    return order.run(kernel, outs, mods, biases, mods_near, biases_near, scratch=scratch)


def modulation_back(order, received, mod_weight, hidden):
    shards, width = len(received), received[0].shape[1]
    rows, columns = mod_weight.shape
    sizes = (2 * width // shards, width // shards, hidden // shards, width // shards)

    def kernel(place, weight_ref, *refs):
        sources, refs = refs[:shards], refs[shards:]
        mod_all, biases, parts, (held, products) = refs[0], refs[1:5], refs[5:-2], refs[-2:]
        shard = 2 * place[LINE] + place[PAIR]
        total = jnp.zeros((1, sum(sizes)), jnp.float32)
        for step in range(shards):
            source = sources[step]
            index = lax.rem(shard + (shards - step), shards)
            for latent in range(2):
                for row in range(6):
                    held[pl.ds(2 * index + latent, 1), row * width : (row + 1) * width] = source[
                        6 * latent + row : 6 * latent + row + 1, :
                    ]
            total = total + source[12:13, : sum(sizes)]
        start = 0
        for target, size in zip(biases, sizes):
            target[...] = total[:, start : start + size]
            start += size
        mod_all[...] = low(held[...])
        products[...] = dot(mod_all[...], weight_ref[...], 1, 1)
        for step in range(shards):
            row = 2 * lax.rem(shard + step, shards)
            parts[step][0:1, :] = products[pl.ds(row, 1), :]
            parts[step][1:2, :] = products[pl.ds(row + 1, 1), :]

    outs = [struct((2 * shards, columns), jnp.bfloat16)]
    outs += [struct((1, size), jnp.float32) for size in sizes]
    outs += [struct((2, rows), jnp.float32)] * shards
    scratch = (
        pltpu.VMEM((2 * shards, columns), jnp.float32),
        pltpu.VMEM((2 * shards, rows), jnp.float32),
    )
    return order.run(kernel, outs, mod_weight, *received, scratch=scratch)


def condition_back(order, received, condition):
    shards, (micros, rows) = len(received), received[0].shape

    def kernel(place, condition_ref, *refs):
        out, held = refs[shards:]
        shard = 2 * place[LINE] + place[PAIR]
        for step in range(shards):
            held[lax.rem(shard + (shards - step), shards)] = refs[step][...]
        values = wide(condition_ref[...])
        sigma = 1.0 / (1.0 + jnp.exp(-values))
        slope = sigma * (1.0 + values * (1.0 - sigma))
        for index in range(shards):
            span = slice(index * rows, (index + 1) * rows)
            out[:, span] = held[index] * slope[:, span]

    outs = [struct(condition.shape, jnp.float32)]
    scratch = (pltpu.VMEM((shards, micros, rows), jnp.float32),)
    return order.run(kernel, outs, condition, *received, scratch=scratch)


def cut_feed(order, up_weight, down_weight, shards):
    hidden, width = down_weight.shape
    rows, columns = up_weight.shape

    def kernel(place, up_ref, down_ref, target):
        cut_columns(place, up_ref, target, 0, place[SEAT], 4, shards)
        target[:, columns // 4 :] = down_ref[place[SEAT]]

    shape = struct((rows, columns // 4 + width), up_weight.dtype)
    return order.run(
        kernel, [shape], up_weight, down_weight.reshape(4, hidden // 4, width)
    )


def cut_tokens(order, tokens):
    shape = struct(tokens.shape[1:], tokens.dtype)

    def kernel(place, source, mine, give):
        mine[...] = source[place[CORE]]
        give[...] = source[1 - place[CORE]]

    return order.run(kernel, [shape, shape], tokens)


def lay_columns(order, quarters, *parts):
    rows = quarters[0].shape[0]

    def kernel(place, *refs):
        for own in range(4):

            @pl.when(place[SEAT] == own)
            def _():
                offset = 0
                for target, (columns, groups) in zip(refs[4:], parts):
                    part = columns // groups
                    for group in range(groups):
                        for other in range(4):
                            start = (group * 4 + (own ^ other)) * part
                            block = refs[other][:, offset : offset + part]
                            target[:, start : start + part] = wide(block)
                        offset += part

    outs = [struct((rows, 4 * columns), jnp.float32) for columns, groups in parts]
    return order.run(kernel, outs, *quarters)


def lay_rows(order, quarters):
    rows, columns = quarters[0].shape

    def kernel(place, *refs):
        for other in range(4):
            refs[4][place[SEAT] ^ other] = wide(refs[other][...])

    result = order.run(kernel, [struct((4, rows, columns), jnp.float32)], *quarters)
    return result.reshape(4 * rows, columns)


def lay_tokens(order, *pairs):
    def kernel(place, *refs):
        for index in range(len(pairs)):
            target = refs[2 * len(pairs) + index]
            target[place[CORE]] = refs[2 * index][...]
            target[1 - place[CORE]] = refs[2 * index + 1][...]

    outs = [struct((2,) + mine.shape, mine.dtype) for mine, near in pairs]
    return order.run(kernel, outs, *(value for values in pairs for value in values))


def norm_tokens(order, pieces, parts, mod_bias):
    tokens, width = pieces[0].shape
    length = 4 * tokens

    def kernel(place, *refs):
        sources, refs = refs[: len(parts)], refs[len(parts) :]
        bias_ref, (mod, out, turned, means, inverses) = refs[0], refs[5:]
        for row in range(6):
            span = slice(row * width, (row + 1) * width)
            total = bias_ref[row : row + 1, :]
            for source in sources:
                total = total + source[:, span]
            mod[row : row + 1, :] = total
        for index in range(4):
            span = slice(index * tokens, (index + 1) * tokens)
            values = wide(refs[1 + index][...])
            mean = jnp.mean(values, axis=1, keepdims=True)
            centre = values - mean
            inverse = lax.rsqrt(jnp.mean(centre * centre, axis=1, keepdims=True) + 1e-06)
            result = centre * inverse * (1.0 + mod[1:2, :]) + mod[0:1, :]
            out[span, :] = low(result)
            turned[:, span] = low(result.T)
            means[span, :] = mean
            inverses[span, :] = inverse

    outs = (
        struct((6, width), jnp.float32),
        struct((length, width), jnp.bfloat16),
        struct((width, length), jnp.bfloat16),
        struct((length, 1), jnp.float32),
        struct((length, 1), jnp.float32),
    )
    return order.run(kernel, outs, *parts, mod_bias, *pieces)


def attend(order, attn_in, weight, bias):
    length = attn_in.shape[0]
    heads = H // 4

    def kernel(place, in_ref, weight_ref, bias_ref, parts, result):
        values = (dot(in_ref[...], weight_ref[...], 1, 0) + bias_ref[...]).T
        for index in range(3 * heads):
            parts[index] = low(values[index * HD : (index + 1) * HD])
        results = []
        for head in range(heads):
            probs = soft_columns(parts[head], parts[heads + head])
            results.append(dot(parts[2 * heads + head], low(probs), 1, 0))
        result[...] = low(jnp.concatenate(results, axis=0))

    outs = (
        struct((3 * heads, HD, length), jnp.bfloat16),
        struct((heads * HD, length), jnp.bfloat16),
    )
    return order.run(kernel, outs, attn_in, weight, bias)


def attend_back(order, other, parts, out_weight, grad_attn):
    length = grad_attn.shape[0]
    heads = H // 4
    part = heads * HD
    factor = HD ** (-0.5)

    def kernel(place, parts_ref, weight_ref, grad_ref, out, sums):
        rows = pl.ds(pl.multiple_of((place[SEAT] ^ other) * part, part), part)
        grad_heads = dot(weight_ref[rows, :], grad_ref[...], 1, 1)
        grads = [None] * (3 * heads)
        for head in range(heads):
            queries, keys = parts_ref[head], parts_ref[heads + head]
            contents = parts_ref[2 * heads + head]
            grad = low(grad_heads[head * HD : (head + 1) * HD])
            probs = soft_columns(queries, keys)
            grad_probs = dot(contents, grad, 0, 0)
            inner = jnp.sum(probs * grad_probs, axis=0, keepdims=True)
            grad_scores = low(probs * (grad_probs - inner))
            grads[head] = factor * dot(keys, grad_scores, 1, 0)
            grads[heads + head] = factor * dot(queries, grad_scores, 1, 1)
            grads[2 * heads + head] = dot(grad, low(probs), 1, 1)
        result = low(jnp.concatenate(grads, axis=0).T)
        out[...] = result
        sums[...] = jnp.sum(wide(result), axis=0, keepdims=True)

    outs = (
        struct((length, 3 * part), jnp.bfloat16),
        struct((1, 3 * part), jnp.float32),
    )
    return order.run(kernel, outs, parts, out_weight, grad_attn)


def attention_out(order, quarters, out_mine, out_near, out_bias, pieces, mod):
    tokens, width = pieces[0].shape
    half, length = 2 * tokens, 4 * tokens
    part = quarters[0].shape[0]
    columns = width // 2

    def kernel(place, *refs):
        out_mine_ref, out_near_ref, bias_ref = refs[4:7]
        mod_ref, heads, weight, branch, normed, inverses, mlp_in = refs[11:]
        for other in range(4):
            rows = pl.ds(pl.multiple_of((place[SEAT] ^ other) * part, part), part)
            if other < 2:
                heads[rows, :] = refs[other][...]
            else:
                heads[rows, :half] = refs[other][:, half:]
                heads[rows, half:] = refs[other][:, :half]
        for own in range(2):

            @pl.when(place[CORE] == own)
            def _():
                weight[:, own * columns : (own + 1) * columns] = out_mine_ref[...]
                weight[:, (1 - own) * columns : (2 - own) * columns] = out_near_ref[...]

        result = dot(heads[...], weight[...], 0, 0) + bias_ref[...]
        branch[...] = result[:half]
        shift, scale = mod_ref[3:4, :], 1.0 + mod_ref[4:5, :]
        for index in range(4):
            span = slice(index * tokens, (index + 1) * tokens)
            values = wide(refs[7 + index][...]) + mod_ref[2:3, :] * result[span]
            centre = values - jnp.mean(values, axis=1, keepdims=True)
            inverse = lax.rsqrt(jnp.mean(centre * centre, axis=1, keepdims=True) + 1e-06)
            centre = centre * inverse
            normed[span, :] = centre
            inverses[span, :] = inverse
            mlp_in[span, :] = low(centre * scale + shift)

    outs = (
        struct((width, length), jnp.bfloat16),
        struct((width, width), jnp.bfloat16),
        struct((half, width), jnp.float32),
        struct((length, width), jnp.float32),
        struct((length, 1), jnp.float32),
        struct((length, width), jnp.bfloat16),
    )
    return order.run(kernel, outs, *quarters, out_mine, out_near, out_bias, *pieces, mod)


def gate_grad(order, pieces, mod):
    tokens, width = pieces[0].shape

    def kernel(place, *refs):
        mod_ref, out, sums = refs[4:]
        total = jnp.zeros(sums.shape, jnp.float32)
        for index in range(4):
            result = low(mod_ref[5:6, :] * wide(refs[index][...]))
            out[index * tokens : (index + 1) * tokens, :] = result
            if index < 2:
                total = total + jnp.sum(wide(result), axis=0, keepdims=True)
        sums[...] = total

    outs = (struct((4 * tokens, width), jnp.bfloat16), struct((1, width), jnp.float32))
    return order.run(kernel, outs, *pieces, mod)


def feed(order, mlp_in, weight, bias):
    length, width = mlp_in.shape
    hidden = weight.shape[1]
    step = hidden // 3

    def kernel(place, in_ref, weight_ref, bias_ref, act, slope):
        pre_act = dot(in_ref[...], weight_ref[...], 1, 0) + bias_ref[...]
        squared = pre_act * pre_act
        bent = jnp.tanh(GELU_ROOT * pre_act * (1.0 + GELU_CUBE * squared))
        raised = 0.5 + 0.5 * bent
        act[...] = low(pre_act * raised)
        slope[...] = raised + pre_act * (1.0 - bent * bent) * (
            0.5 * GELU_ROOT + (1.5 * GELU_ROOT * GELU_CUBE) * squared
        )

    return order.run(
        kernel,
        (
            struct((length, hidden), jnp.bfloat16),
            struct((length, hidden), jnp.float32),
        ),
        mlp_in, weight, bias,
        grid=(3,),
        in_specs=[
            whole((length, width)),
            column_block((width, hidden), step),
            column_block((1, hidden), step),
        ],
        out_specs=(
            column_block((length, hidden), step),
            column_block((length, hidden), step),
        ),
    )


def feed_back(order, grad_mlp, weight, slope):
    length, width = grad_mlp.shape
    hidden = weight.shape[0]
    step = hidden // 3

    def kernel(place, grad_ref, weight_ref, slope_ref, out, sums):
        result = low(dot(grad_ref[...], weight_ref[...], 1, 1) * slope_ref[...])
        out[...] = result
        sums[...] = jnp.sum(wide(result), axis=0, keepdims=True)

    return order.run(
        kernel,
        (struct((length, hidden), jnp.bfloat16), struct((1, hidden), jnp.float32)),
        grad_mlp, weight, slope,
        grid=(3,),
        in_specs=[
            whole((length, width)),
            row_block((hidden, width), step),
            column_block((length, hidden), step),
        ],
        out_specs=(column_block((length, hidden), step), column_block((1, hidden), step)),
    )


def feed_in_back(order, pre_mine, up_mine, pre_near, up_near):
    length, hidden = pre_mine.shape
    width = up_mine.shape[0]
    step = width // 3

    def kernel(place, pre_mine_ref, up_mine_ref, pre_near_ref, up_near_ref, out):
        out[...] = low(
            dot(pre_mine_ref[...], up_mine_ref[...], 1, 1)
            + dot(pre_near_ref[...], up_near_ref[...], 1, 1)
        )

    return order.run(
        kernel,
        [struct((length, width), jnp.bfloat16)],
        pre_mine, up_mine, pre_near, up_near,
        grid=(3,),
        in_specs=[
            whole((length, hidden)),
            row_block((width, hidden), step),
            whole((length, hidden)),
            row_block((width, hidden), step),
        ],
        out_specs=[column_block((length, width), step)],
    )


def feed_out(order, act_mine, down_mine, act_near, down_near):
    length, hidden = act_mine.shape
    width = down_mine.shape[1]
    half, step = length // 2, width // 3

    def kernel(place, act_mine_ref, down_mine_ref, act_near_ref, down_near_ref, own, give):
        result = dot(act_mine_ref[...], down_mine_ref[...], 1, 0) + dot(
            act_near_ref[...], down_near_ref[...], 1, 0
        )
        own[...] = result[:half]
        give[...] = low(result[half:])

    return order.run(
        kernel,
        (struct((half, width), jnp.float32), struct((half, width), jnp.bfloat16)),
        act_mine, down_mine, act_near, down_near,
        grid=(3,),
        in_specs=[
            whole((length, hidden)),
            column_block((hidden, width), step),
            whole((length, hidden)),
            column_block((hidden, width), step),
        ],
        out_specs=(column_block((half, width), step), column_block((half, width), step)),
    )


def weight_grad(order, shards, left_side, right_side, chunks):
    length, rows = left_side.shape
    columns = right_side.shape[1]

    def kernel(place, left_ref, right_ref, *refs):
        total = low(dot(left_ref[...], right_ref[...], 0, 0))
        give_chunks(total, shards, refs, 0)

    return order.run(kernel, chunks_of(shards, rows, columns, chunks), left_side, right_side)


def chunks_of(shards, rows, columns, chunks):
    return [struct((shards // chunks, rows // shards, columns), jnp.bfloat16)] * chunks


def give_chunks(total, shards, refs, start):
    piece = total.shape[0] // shards
    share = shards // len(refs)
    span = slice(start, start + total.shape[1])
    for shard in range(shards):
        block = total[shard * piece : (shard + 1) * piece]
        refs[shard // share][shard % share, :, span] = block


def attention_grad(order, shards, attn_turned, qkv_grad, heads_out, grad_attn, chunks):
    rows = attn_turned.shape[0]
    columns, part = qkv_grad.shape[1], grad_attn.shape[1] // 4

    def kernel(place, turned_ref, qkv_ref, heads_ref, grad_ref, *refs):
        held = refs[chunks]
        take_quarter(place, grad_ref, held, 1)
        give_chunks(low(dot(turned_ref[...], qkv_ref[...], 1, 0)), shards, refs[:chunks], 0)
        total = low(dot(heads_ref[...], held[...], 1, 0))
        give_chunks(total, shards, refs[:chunks], columns)

    return order.run(
        kernel,
        chunks_of(shards, rows, columns + part, chunks),
        attn_turned,
        qkv_grad,
        heads_out,
        grad_attn,
        scratch=(pltpu.VMEM((grad_attn.shape[0], part), grad_attn.dtype),),
    )


def take_quarter(place, source, target, other):
    columns = target.shape[1]
    for index in range(4):

        @pl.when((place[SEAT] ^ other) == index)
        def _():
            target[...] = source[:, index * columns : (index + 1) * columns]


def split_pairs(place, total, shards, met_refs, start, write):
    piece = total.shape[0] // shards
    share = shards // len(met_refs)
    span = slice(start, start + total.shape[1])
    for own in range(2):

        @pl.when(place[PAIR] == own)
        def _():
            for shard in range(shards):
                part = total[shard * piece : (shard + 1) * piece]
                met = met_refs[shard // share][shard % share, :, span]
                write(shard // 2, shard % 2 == own, low(part + wide(met)))


def weight_sum(order, shards, left_side, right_side, met, join=False):
    rows, columns = left_side.shape[1], right_side.shape[1]
    piece = rows // shards

    def kernel(place, left_ref, right_ref, *refs):
        met_refs, outs = refs[: len(met)], refs[len(met) :]

        def write(line, mine, part):
            if join:
                start = piece if mine else 0
                outs[0][line, start : start + piece] = part
            else:
                outs[1 if mine else 0][line] = part

        total = dot(left_ref[...], right_ref[...], 0, 0)
        split_pairs(place, total, shards, met_refs, 0, write)

    if join:
        outs = (struct((shards // 2, 2 * piece, columns), jnp.bfloat16),)
    else:
        outs = (struct((shards // 2, piece, columns), jnp.bfloat16),) * 2
    return order.run(kernel, outs, left_side, right_side, *met)


def attention_sum(order, shards, attn_turned, qkv_grad, heads_out, grad_attn, met):
    rows = attn_turned.shape[0]
    columns, part = qkv_grad.shape[1], grad_attn.shape[1] // 4

    def kernel(place, turned_ref, qkv_ref, heads_ref, grad_ref, *refs):
        met_refs, (give, mine, held) = refs[: len(met)], refs[len(met) :]
        take_quarter(place, grad_ref, held, 0)
        for left, right, start in ((turned_ref, qkv_ref, 0), (heads_ref, held, columns)):
            total = dot(left[...], right[...], 1, 0)
            span = slice(start, start + total.shape[1])

            def write(line, own, block, span=span):
                target = mine if own else give
                target[line, :, span] = block

            split_pairs(place, total, shards, met_refs, start, write)

    outs = (struct((shards // 2, rows // shards, columns + part), jnp.bfloat16),) * 2
    return order.run(
        kernel,
        outs,
        attn_turned,
        qkv_grad,
        heads_out,
        grad_attn,
        *met,
        scratch=(pltpu.VMEM((grad_attn.shape[0], part), grad_attn.dtype),),
    )


def middle_back(order, part, far, normed, inverses, pieces, mod, branch):
    length, width = part.shape
    tokens = length // 4

    def kernel(place, part_ref, far_ref, normed_ref, inverse_ref, *refs):
        mod_ref, branch_ref, grad_attn, grad_middle, sums = refs[4:]
        gate, scale = mod_ref[2:3, :], 1.0 + mod_ref[4:5, :]
        totals = [jnp.zeros((1, width), jnp.float32)] * 4
        for index in range(4):
            span = slice(index * tokens, (index + 1) * tokens)
            other = slice((index ^ 2) * tokens, ((index ^ 2) + 1) * tokens)
            grad_in = wide(part_ref[span, :]) + wide(far_ref[other, :])
            values = normed_ref[span, :]
            grad = wide(refs[index][...]) + normalize_back(
                values, inverse_ref[span, :], grad_in * scale
            )
            result = low(gate * grad)
            grad_attn[span, :] = result
            if index < 2:
                grad_middle[span, :] = grad
                terms = (grad_in, grad_in * values, grad * branch_ref[span, :], wide(result))
                totals = [
                    total + jnp.sum(term, axis=0, keepdims=True)
                    for total, term in zip(totals, terms)
                ]
        for row, total in enumerate(totals):
            sums[row : row + 1, :] = total

    outs = (
        struct((length, width), jnp.bfloat16),
        struct((2 * tokens, width), jnp.float32),
        struct((4, width), jnp.float32),
    )
    return order.run(kernel, outs, part, far, normed, inverses, *pieces, mod, branch)


def attention_in_back(order, grad_mine, qkv_mine, grad_near, qkv_near, pieces, means, inverses):
    length, columns = grad_mine.shape
    width = qkv_mine.shape[0]
    tokens, half, step = length // 4, length // 2, width // 3

    def kernel(place, grad_mine_ref, qkv_mine_ref, grad_near_ref, qkv_near_ref, *refs):
        mean_ref, inverse_ref, own, give, sums = refs[4:]
        result = dot(grad_mine_ref[...], qkv_mine_ref[...], 1, 1) + dot(
            grad_near_ref[...], qkv_near_ref[...], 1, 1
        )
        own[...] = result[:half]
        give[...] = low(result[half:])
        scaled = jnp.zeros((1, step), jnp.float32)
        for index in range(4):
            span = slice(index * tokens, (index + 1) * tokens)
            normed = (wide(refs[index][...]) - mean_ref[span, :]) * inverse_ref[span, :]
            scaled = scaled + jnp.sum(result[span] * normed, axis=0, keepdims=True)
        sums[0:1, :] = jnp.sum(result, axis=0, keepdims=True)
        sums[1:2, :] = scaled

    outs = (
        struct((half, width), jnp.float32),
        struct((half, width), jnp.bfloat16),
        struct((2, width), jnp.float32),
    )
    weights = row_block((width, columns), step)
    grads = whole((length, columns))
    stats = whole((length, 1))
    return order.run(
        kernel,
        outs,
        grad_mine,
        qkv_mine,
        grad_near,
        qkv_near,
        *pieces,
        means,
        inverses,
        grid=(3,),
        in_specs=[grads, weights, grads, weights]
        + [column_block((tokens, width), step)] * 4
        + [stats, stats],
        out_specs=[
            column_block((half, width), step),
            column_block((half, width), step),
            column_block((2, width), step),
        ],
    )


def tokens_back(order, own, far, pieces, means, inverses, mod, grad_middle):
    half, width = own.shape
    tokens = half // 2

    def kernel(
        place, own_ref, far_ref, mine_ref, near_ref, mean_ref, inverse_ref, mod_ref, grad_ref,
        mine, give,
    ):
        for index, (source, target) in enumerate(((mine_ref, mine), (near_ref, give))):
            span = slice(index * tokens, (index + 1) * tokens)
            inverse = inverse_ref[span, :]
            normed = (wide(source[...]) - mean_ref[span, :]) * inverse
            grad = (own_ref[span, :] + wide(far_ref[span, :])) * (1.0 + mod_ref[1:2, :])
            target[...] = grad_ref[span, :] + normalize_back(normed, inverse, grad)

    outs = (struct((tokens, width), jnp.float32),) * 2
    return order.run(
        kernel, outs, own, far, pieces[0], pieces[1], means, inverses, mod, grad_middle
    )


def mix(order, own, far, down_bias, pieces, branch, grads, mod):
    half, width = own.shape
    tokens = half // 2

    def kernel(
        place, own_ref, far_ref, bias_ref, mine_ref, near_ref, branch_ref, grad_mine, grad_near,
        mod_ref, mine, give, sums,
    ):
        total = jnp.zeros((1, width), jnp.float32)
        sources = ((mine_ref, grad_mine, mine), (near_ref, grad_near, give))
        for index, (source, grad, target) in enumerate(sources):
            span = slice(index * tokens, (index + 1) * tokens)
            mlp_branch = own_ref[span, :] + wide(far_ref[span, :]) + bias_ref[...]
            middle = wide(source[...]) + mod_ref[2:3, :] * branch_ref[span, :]
            target[...] = low(middle + mod_ref[5:6, :] * mlp_branch)
            total = total + jnp.sum(wide(grad[...]) * mlp_branch, axis=0, keepdims=True)
        sums[...] = total

    outs = (struct((tokens, width), jnp.bfloat16),) * 2 + (struct((1, width), jnp.float32),)
    return order.run(
        kernel, outs, own, far, down_bias, pieces[0], pieces[1], branch, grads[0], grads[1], mod
    )


def per_device(
    latents,
    condition,
    mod_weight,
    mod_bias,
    qkv_weight,
    qv_bias,
    out_weight,
    out_bias,
    up_weight,
    up_bias,
    down_weight,
    down_bias,
    cotangent,
):
    here = Place()
    order = Order(here.place)
    shards, seat, core = here.shards, here.seat, here.core
    near_seat = seat ^ 1
    micros, tokens, width = latents.shape
    rows = width // shards
    hidden = up_weight.shape[1]
    heads = H // 4
    part = heads * HD
    block = hidden // shards // 4
    wait = order.wait

    hidden_part = shards * block
    attention_widths = (3 * part, width // 2)

    biases = jnp.concatenate([mod_bias, qv_bias, out_bias, up_bias, down_bias]).reshape(1, -1)
    ring = Gather(
        here, order, cut_attention(order, condition, biases, qkv_weight, out_weight), near=True
    )
    lat_mine, lat_give = cut_tokens(order, latents)
    lat_near, lat_far = here.to_core(lat_give), here.to_side(lat_mine)
    cot_mine, cot_give = cut_tokens(order, cotangent)
    cot_near, cot_far = here.to_core(cot_give), here.to_side(cot_mine)
    feed_piece = cut_feed(order, up_weight, down_weight, shards)
    ring.turn()
    lat_near, cot_near = wait(lat_near, cot_near)
    lat_far_near, cot_far_near = here.to_side(lat_near), here.to_side(cot_near)
    lat_far = wait(lat_far)
    ring.turn()
    cot_far, lat_far_near = wait(cot_far, lat_far_near)
    lats = (lat_mine, lat_near, lat_far, lat_far_near)
    ring.turn()
    feed_ring = Gather(here, order, wait(feed_piece), hold=True)
    qkv_mine, out_mine, heads_all = ring.finish(attention_widths, HEAD, True)
    feed_ring.release()
    (
        cond_rows,
        mod_bias,
        qkv_bias_mine,
        qkv_bias_near,
        out_bias,
        up_bias_mine,
        up_bias_near,
        down_bias,
        *mod_parts,
    ) = modulation_parts(order, heads_all, mod_weight, micros, width, hidden)
    mod_parts = here.exchange(mod_parts)
    qkv_near, out_near = ring.finish_near(attention_widths, HEAD)
    cots = (cot_mine, cot_near, cot_far, wait(cot_far_near))
    mod_parts = [mod_parts[0]] + list(wait(*mod_parts[1:]))
    feed_ring.turn()
    mod, attn_in, attn_turned, means_one, inverses_one = norm_tokens(
        order, lats, mod_parts, mod_bias
    )
    qkv_mine = qkv_mine.reshape(width, 3 * part)
    parts_mine, heads_mine = attend(order, attn_in, qkv_mine, qkv_bias_mine)
    heads_far = here.to_side(heads_mine)
    qkv_near = qkv_near.reshape(width, 3 * part)
    parts_near, heads_near = attend(order, attn_in, qkv_near, qkv_bias_near)
    heads_far_near = here.to_side(heads_near)
    heads_far = wait(heads_far)
    feed_ring.turn()
    quarters = (heads_mine, heads_near, heads_far, wait(heads_far_near))
    heads_out, out_full, branch, normed_two, inverses_two, mlp_in = attention_out(
        order,
        quarters,
        out_mine.reshape(width, width // 2),
        out_near.reshape(width, width // 2),
        out_bias,
        lats,
        mod,
    )
    grad_mlp, down_sums = gate_grad(order, cots, mod)
    feed_ring.turn()
    up_mine, down_mine = feed_ring.finish((hidden_part, width))
    up_near, down_near = here.to_core(up_mine), here.to_core(down_mine)
    up_mine = up_mine.reshape(width, hidden_part)
    down_mine = down_mine.reshape(hidden_part, width)
    act_mine, slope_mine = feed(order, mlp_in, up_mine, up_bias_mine)
    pre_mine, up_sums_mine = feed_back(order, grad_mlp, down_mine, slope_mine)
    up_near = wait(up_near).reshape(width, hidden_part)
    act_near, slope_near = feed(order, mlp_in, up_near, up_bias_near)
    down_near = wait(down_near).reshape(hidden_part, width)
    pre_near, up_sums_near = feed_back(order, grad_mlp, down_near, slope_near)

    mlp_part = feed_in_back(order, pre_mine, up_mine, pre_near, up_near)
    mlp_far = here.to_side(mlp_part)

    def to_core(chunks):
        return [here.to_core(chunk) for chunk in chunks]

    up_met = to_core(weight_grad(order, shards, mlp_in, pre_near, 8))
    down_met = to_core(weight_grad(order, shards, act_near, grad_mlp, 8))
    up_met = wait(*up_met)
    up_sum = ScatterLines(
        here, order, weight_sum(order, shards, mlp_in, pre_mine, up_met, join=True)
    )
    down_met = wait(*down_met)
    down_sum = Scatter(here, order, *weight_sum(order, shards, act_mine, grad_mlp, down_met))
    feed_own, feed_give = feed_out(order, act_mine, down_mine, act_near, down_near)
    feed_far = here.to_side(feed_give)

    mlp_far = wait(mlp_far)
    grad_attn, grad_middle, middle_sums = middle_back(
        order, mlp_part, mlp_far, normed_two, inverses_two, cots, mod, branch
    )
    qkv_grad_near, qv_sums_near = attend_back(order, 1, parts_near, out_full, grad_attn)
    met = to_core(
        attention_grad(order, shards, attn_turned, qkv_grad_near, heads_out, grad_attn, 4)
    )
    up_sum.turn()
    qkv_grad_mine, qv_sums_mine = attend_back(order, 0, parts_mine, out_full, grad_attn)
    down_sum.join()
    met = wait(*met)
    attention_total = Scatter(
        here,
        order,
        *attention_sum(order, shards, attn_turned, qkv_grad_mine, heads_out, grad_attn, met),
    )
    up_sum.turn()
    attn_own, attn_give, attn_sums = attention_in_back(
        order, qkv_grad_mine, qkv_mine, qkv_grad_near, qkv_near, lats, means_one, inverses_one
    )
    attn_far = here.to_side(attn_give)
    down_sum.turn()
    feed_far = wait(feed_far)
    mixed_mine, mixed_give, mix_sums = mix(
        order, feed_own, feed_far, down_bias, lats, branch, cots, mod
    )
    mixed_near = here.to_core(mixed_give)

    mods, biases = token_sums(
        order, shards, attn_sums, middle_sums, mix_sums, down_sums, qv_sums_mine, qv_sums_near,
        up_sums_mine, up_sums_near,
    )
    mods_far, biases_far = here.to_side(mods), here.to_side(biases)
    up_sum.join()
    mods_far, biases_far = wait(mods_far, biases_far)
    mods, biases = add_sums(order, mods, biases, mods_far, biases_far)
    mods_near, biases_near = here.to_core(mods), here.to_core(biases)
    down_sum.turn()
    attention_total.join()
    mods_near, biases_near = wait(mods_near, biases_near)
    received = here.exchange(sums_to_send(order, mods, biases, mods_near, biases_near))
    attention_total.turn()
    grad_down = down_sum.finish()
    down_far, down_near = here.to_side(grad_down), here.to_core(grad_down)
    received = [received[0]] + list(wait(*received[1:]))
    mod_all, grad_qv_bias, grad_out_bias, grad_up_bias, grad_down_bias, *grad_low = (
        modulation_back(order, received, mod_weight, hidden)
    )
    grad_low = here.exchange(grad_low)
    attention_total.turn()
    grad_up = up_sum.finish()
    up_far, up_near = here.to_side(grad_up), here.to_core(grad_up)
    grad_attention = attention_total.finish()
    attention_far = here.to_side(grad_attention)
    attention_near = here.to_core(grad_attention)
    down_far, down_near = wait(down_far, down_near)
    down_far_near = here.to_core(down_far)
    attn_far = wait(attn_far)
    tokens_mine, tokens_give = tokens_back(
        order, attn_own, attn_far, lats, means_one, inverses_one, mod, grad_middle
    )
    tokens_near = here.to_core(tokens_give)
    up_far, up_near = wait(up_far, up_near)
    up_far_near = here.to_core(up_far)
    down_far_near = wait(down_far_near)
    grad_down = lay_rows(order, (grad_down, down_near, down_far, down_far_near))
    attention_far, attention_near = wait(attention_far, attention_near)
    attention_far_near = here.to_core(attention_far)
    up_far_near = wait(up_far_near)
    grad_up = lay_columns(
        order, (grad_up, up_near, up_far, up_far_near), (hidden_part, shards)
    )
    attention_far_near = wait(attention_far_near)
    grad_qkv, grad_out = lay_columns(
        order,
        (grad_attention, attention_near, attention_far, attention_far_near),
        (3 * part, 3),
        (width // 4, 1),
    )
    grad_low = [grad_low[0]] + list(wait(*grad_low[1:]))
    grad_condition = condition_back(order, grad_low, condition)
    mixed_near, tokens_near = wait(mixed_near, tokens_near)
    mixed, grad_latents = lay_tokens(
        order, (mixed_mine, mixed_near), (tokens_mine, tokens_near)
    )
    mod_all = wait(mod_all)
    grad_mod_weight = wait(dot(cond_rows, mod_all, 0, 0))
    span = 6 * width // shards
    mod_span = lax.dynamic_slice_in_dim(mod_all, here.shard * span, span, 1)
    grad_mod_bias = jnp.sum(wide(mod_span), axis=0)
    grad_qv_bias, grad_out_bias, grad_up_bias, grad_down_bias = (
        vector.reshape(-1)
        for vector in (grad_qv_bias, grad_out_bias, grad_up_bias, grad_down_bias)
    )

    return (
        mixed,
        grad_latents,
        grad_condition,
        grad_mod_weight,
        grad_mod_bias,
        grad_qkv,
        grad_qv_bias,
        grad_out,
        grad_out_bias,
        grad_up,
        grad_up_bias,
        grad_down,
        grad_down_bias,
    )


def solution(mesh):
    tokens = P("fsdp", "seq", None)
    matrix = P("fsdp", None)
    vector = P("fsdp")
    parameters = (matrix, vector) * 5
    in_specs = (tokens, matrix) + parameters + (tokens,)
    out_specs = (tokens, tokens, matrix) + parameters
    return jax.shard_map(
        per_device, mesh=mesh, in_specs=in_specs, out_specs=out_specs, check_vma=False
    )
```

profile of v0, /device:TPU:0, one launch (start us, length us, event | category | flops | bytes accessed | tf_op | source)
XLA Modules:
  0.0 358.3 jit_solution(16856285755978529338)
XLA Ops:
  0.7 3.6 concatenate.3
  17.6 7.0 %collective-permute-done.refs_1_ = bf16[160,1440]{1,0:T(8,128)(2,1)S(1)} collective-permute-done((bf16[160,1440]{1,0:T(8,128)(2,1)S(1)}, bf16[160,1440]{1,0:T(8,128)(2,1)S(1)}, u32[]{:S(2)}, u32[]{:S(2)}) %collective-permute-start) | collective-permute-done | bytes 460832 | tf_op jit(solution)/shard_map/ppermute | solution.py:157
  29.1 7.5 %collective-permute-done.5.refs_11_.refs_9_.refs_6_ = bf16[128,1152]{1,0:T(8,128)(2,1)S(1)} collective-permute-done((bf16[128,1152]{1,0:T(8,128)(2,1)S(1)}, bf16[128,1152]{1,0:T(8,128)(2,1)S(1)}, u32[]{:S(2)}, u32[]{:S(2)}) %collective-permute-start.5) | collective-permute-done | bytes 294944 | tf_op jit(solution)/shard_map/ppermute | solution.py:151
  40.8 3.9 %collective-permute-done.10.refs_2_.refs_6_ = bf16[128,1152]{1,0:T(8,128)(2,1)S(1)} collective-permute-done((bf16[128,1152]{1,0:T(8,128)(2,1)S(1)}, bf16[128,1152]{1,0:T(8,128)(2,1)S(1)}, u32[]{:S(2)}, u32[]{:S(2)}) %collective-permute-start.10) | collective-permute-done | bytes 294944 | tf_op jit(solution)/shard_map/ppermute | solution.py:151
  46.3 5.7 %collective-permute-done.11.refs_12_.refs_10_.refs_7_ = bf16[128,1152]{1,0:T(8,128)(2,1)S(1)} collective-permute-done((bf16[128,1152]{1,0:T(8,128)(2,1)S(1)}, bf16[128,1152]{1,0:T(8,128)(2,1)S(1)}, u32[]{:S(2)}, u32[]{:S(2)}) %collective-permute-start.11) | collective-permute-done | bytes 294944 | tf_op jit(solution)/shard_map/ppermute | solution.py:151
  54.6 8.2 %collective-permute-done.16.refs_7_ = bf16[160,1440]{1,0:T(8,128)(2,1)S(1)} collective-permute-done((bf16[160,1440]{1,0:T(8,128)(2,1)S(1)}, bf16[160,1440]{1,0:T(8,128)(2,1)S(1)}, u32[]{:S(2)}, u32[]{:S(2)}) %collective-permute-start.16) | collective-permute-done | bytes 460832 | tf_op jit(solution)/shard_map/ppermute | solution.py:154
  68.9 5.6 %collective-permute-done.20.refs_3_.refs_7_ = bf16[128,1152]{1,0:T(8,128)(2,1)S(1)} collective-permute-done((bf16[128,1152]{1,0:T(8,128)(2,1)S(1)}, bf16[128,1152]{1,0:T(8,128)(2,1)S(1)}, u32[]{:S(2)}, u32[]{:S(2)}) %collective-permute-start.20) | collective-permute-done | bytes 294944 | tf_op jit(solution)/shard_map/ppermute | solution.py:151
  95.6 4.3 %shard_map.236 = (bf16[12,72,512]{2,1,0:T(8,128)(2,1)S(1)}, bf16[288,512]{1,0:T(8,128)(2,1)S(1)}, f32[8,128]{1,0:T(8,128)S(1)}) custom-call(s32[4]{0:T(128)S(1)} %pad_add_fusion.place, bf16[512,1152]{1,0:T(8,128)(2,1)S(1)} %get-tuple-element.429.refs_0_, bf16[1152,864]{1,0:T(8,128)(2,1)S(1)} %bitcast.26, ...), custom_call_target="tpu_custom_call", output_to_operand_aliasing={{2}: (4, {})} | custom-call | flops 1 | bytes 1 | tf_op jit(solution)/shard_map/pallas_call | solution.py:85
  101.4 4.3 %shard_map.237 = (bf16[12,72,512]{2,1,0:T(8,128)(2,1)S(1)}, bf16[288,512]{1,0:T(8,128)(2,1)S(1)}, f32[8,128]{1,0:T(8,128)S(1)}) custom-call(s32[4]{0:T(128)S(1)} %pad_add_fusion.place, bf16[512,1152]{1,0:T(8,128)(2,1)S(1)} %get-tuple-element.429.refs_0_, bf16[1152,864]{1,0:T(8,128)(2,1)S(1)} %bitcast.28, ...), custom_call_target="tpu_custom_call", output_to_operand_aliasing={{2}: (4, {})} | custom-call | flops 1 | bytes 1 | tf_op jit(solution)/shard_map/pallas_call | solution.py:85
  111.3 5.1 %collective-permute-done.33.refs_3_ = bf16[288,512]{1,0:T(8,128)(2,1)S(1)} collective-permute-done((bf16[288,512]{1,0:T(8,128)(2,1)S(1)}, bf16[288,512]{1,0:T(8,128)(2,1)S(1)}, u32[]{:S(2)}, u32[]{:S(2)}) %collective-permute-start.33) | collective-permute-done | bytes 294944 | tf_op jit(solution)/shard_map/ppermute | solution.py:151
  116.4 3.7 %shard_map.238 = (bf16[1152,512]{1,0:T(8,128)(2,1)S(1)}, bf16[1152,1152]{1,0:T(8,128)(2,1)S(1)}, f32[256,1152]{1,0:T(8,128)S(1)}, f32[512,1152]{1,0:T(8,128)S(1)...) custom-call(s32[4]{0:T(128)S(1)} %pad_add_fusion.place, ...), custom_call_target="tpu_custom_call", output_to_operand_aliasing={{6}: (13, {})} | custom-call | flops 1 | bytes 1 | tf_op jit(solution)/shard_map/pallas_call | solution.py:85
  123.1 11.4 %collective-permute-done.36.refs_7_ = bf16[144,2304]{1,0:T(8,128)(2,1)S(1)} collective-permute-done((bf16[144,2304]{1,0:T(8,128)(2,1)S(1)}, bf16[144,2304]{1,0:T(8,128)(2,1)S(1)}, u32[]{:S(2)}, u32[]{:S(2)}) %collective-permute-start.36) | collective-permute-done | bytes 663584 | tf_op jit(solution)/shard_map/ppermute | solution.py:154
  136.1 4.8 %shard_map.241 = (bf16[512,1152]{1,0:T(8,128)(2,1)S(1)}, f32[512,1152]{1,0:T(8,128)S(1)}, f32[8,128]{1,0:T(8,128)S(1)}) custom-call(s32[4]{0:T(128)S(1)} %pad_add_fusion.place, bf16[512,1152]{1,0:T(8,128)(2,1)S(1)} %get-tuple-element.449.refs_0_, bf16[1152,1152]{1,0:T(8,128)(2,1)S(1)} %bitcast.18, ...), custom_call_target="tpu_custom_call", output_to_operand_aliasing={{2}: (4, {})} | custom-call | flops 1 | bytes 1 | tf_op jit(solution)/shard_map/pallas_call | solution.py:85
  144.3 4.5 %shard_map.243 = (bf16[512,1152]{1,0:T(8,128)(2,1)S(1)}, f32[512,1152]{1,0:T(8,128)S(1)}, f32[8,128]{1,0:T(8,128)S(1)}) custom-call(s32[4]{0:T(128)S(1)} %pad_add_fusion.place, bf16[512,1152]{1,0:T(8,128)(2,1)S(1)} %get-tuple-element.449.refs_0_, bf16[1152,1152]{1,0:T(8,128)(2,1)S(1)} %bitcast.20, ...), custom_call_target="tpu_custom_call", output_to_operand_aliasing={{2}: (4, {})} | custom-call | flops 1 | bytes 1 | tf_op jit(solution)/shard_map/pallas_call | solution.py:85
  152.2 5.1 %shard_map.245 = (bf16[512,1152]{1,0:T(8,128)(2,1)S(1)}, f32[8,128]{1,0:T(8,128)S(1)}) custom-call(s32[4]{0:T(128)S(1)} %pad_add_fusion.place, bf16[512,1152]{1,0:T(8,128)(2,1)S(1)} %get-tuple-element.477.refs_0_.refs_1_, bf16[1152,1152]{1,0:T(8,128)(2,1)S(1)} %bitcast.19, ...), custom_call_target="tpu_custom_call", output_to_operand_aliasing={{1}: (5, {})} | custom-call | flops 1 | bytes 1 | tf_op jit(solution)/shard_map/pallas_call | solution.py:85
  172.2 3.9 %shard_map.250 = (bf16[4,144,1152]{2,1,0:T(8,128)(2,1)}, bf16[4,144,1152]{2,1,0:T(8,128)(2,1)S(1)}, f32[8,128]{1,0:T(8,128)S(1)}) custom-call(s32[4]{0:T(128)S(1)} %pad_add_fusion.place, bf16[512,1152]{1,0:T(8,128)(2,1)S(1)} %get-tuple-element.465.refs_0_, ...), custom_call_target="tpu_custom_call", output_to_operand_aliasing={{2}: (11, {})} | custom-call | flops 1 | bytes 1 | tf_op jit(solution)/shard_map/pallas_call | solution.py:85
  176.9 5.4 %shard_map.251 = (f32[256,1152]{1,0:T(8,128)S(1)}, bf16[256,1152]{1,0:T(8,128)(2,1)S(1)}, f32[8,128]{1,0:T(8,128)S(1)}) custom-call(s32[4]{0:T(128)S(1)} %pad_add_fusion.place, bf16[512,1152]{1,0:T(8,128)(2,1)S(1)} %get-tuple-element.465.refs_0_, bf16[1152,1152]{1,0:T(8,128)(2,1)S(1)} %bitcast.23, ...), custom_call_target="tpu_custom_call", output_to_operand_aliasing={{2}: (5, {})} | custom-call | flops 1 | bytes 1 | tf_op jit(solution)/shard_map/pallas_call | solution.py:85
  182.3 11.8 %collective-permute-done.55.refs_1_ = bf16[512,1152]{1,0:T(8,128)(2,1)S(1)} collective-permute-done((bf16[512,1152]{1,0:T(8,128)(2,1)S(1)}, bf16[512,1152]{1,0:T(8,128)(2,1)S(1)}, u32[]{:S(2)}, u32[]{:S(2)}) %collective-permute-start.55) | collective-permute-done | bytes 1179680 | tf_op jit(solution)/shard_map/ppermute | solution.py:151
  196.5 5.8 %shard_map.253 = (bf16[512,864]{1,0:T(8,128)(2,1)S(1)}, f32[1,864]{1,0:T(1,128)S(1)}, f32[8,128]{1,0:T(8,128)S(1)}) custom-call(s32[4]{0:T(128)S(1)} %pad_add_fusion.place, bf16[12,72,512]{2,1,0:T(8,128)(2,1)S(1)} %get-tuple-element.535.refs_0_, bf16[1152,1152]{1,0:T(8,128)(2,1)S(1)} %get-tuple-element.525.refs_1_, ...), custom_call_target="tpu_custom_call", output_to_operand_aliasing={{2}: (4, {})} | custom-call | flops 1 | bytes 1 | tf_op jit(solution)/shard_map/pallas_call | solution.py:85
  208.2 5.8 %shard_map.256 = (bf16[512,864]{1,0:T(8,128)(2,1)S(1)}, f32[1,864]{1,0:T(1,128)S(1)}, f32[8,128]{1,0:T(8,128)S(1)}) custom-call(s32[4]{0:T(128)S(1)} %pad_add_fusion.place, bf16[12,72,512]{2,1,0:T(8,128)(2,1)S(1)} %copy-done.7, bf16[1152,1152]{1,0:T(8,128)(2,1)S(1)} %get-tuple-element.525.refs_1_, ...), custom_call_target="tpu_custom_call", output_to_operand_aliasing={{2}: (4, {})} | custom-call | flops 1 | bytes 1 | tf_op jit(solution)/shard_map/pallas_call | solution.py:85
  215.5 4.1 %shard_map.259 = (bf16[4,144,1152]{2,1,0:T(8,128)(2,1)S(1)}, bf16[4,144,1152]{2,1,0:T(8,128)(2,1)S(1)}, f32[8,128]{1,0:T(8,128)S(1)}) custom-call(s32[4]{0:T(128)S(1)} %pad_add_fusion.place, bf16[1152,512]{1,0:T(8,128)(2,1)S(1)} %get-tuple-element.534.refs_0_, ...), custom_call_target="tpu_custom_call", output_to_operand_aliasing={{2}: (9, {})} | custom-call | flops 1 | bytes 1 | tf_op jit(solution)/shard_map/pallas_call | solution.py:85
  219.9 6.0 %collective-permute-done.62.refs_1_ = bf16[288,1152]{1,0:T(8,128)(2,1)S(1)} collective-permute-done((bf16[288,1152]{1,0:T(8,128)(2,1)S(1)}, bf16[288,1152]{1,0:T(8,128)(2,1)S(1)}, u32[]{:S(2)}, u32[]{:S(2)}) %collective-permute-start.62) | collective-permute-done | bytes 663584 | tf_op jit(solution)/shard_map/ppermute | solution.py:157
  228.7 4.5 %shard_map.261 = (f32[256,1152]{1,0:T(8,128)S(1)}, bf16[256,1152]{1,0:T(8,128)(2,1)S(1)}, f32[2,1152]{1,0:T(2,128)S(1)}, f32[8,128]{1,0:T(8,128)S(1)}) custom-call(s32[4]{0:T(128)S(1)} %pad_add_fusion.place, bf16[512,864]{1,0:T(8,128)(2,1)S(1)} %get-tuple-element.551.refs_1_.refs_0_, ...), custom_call_target="tpu_custom_call", output_to_operand_aliasing={{3}: (11, {})} | custom-call | flops 1 | bytes 1 | tf_op jit(solution)/shard_map/pallas_call | solution.py:85
  233.3 18.2 %collective-permute-done.63.refs_1_ = bf16[144,1152]{1,0:T(8,128)(2,1)S(1)} collective-permute-done((bf16[144,1152]{1,0:T(8,128)(2,1)S(1)}, bf16[144,1152]{1,0:T(8,128)(2,1)S(1)}, u32[]{:S(2)}, u32[]{:S(2)}) %collective-permute-start.63) | collective-permute-done | bytes 331808 | tf_op jit(solution)/shard_map/ppermute | solution.py:157
  267.3 7.7 %collective-permute-done.72.refs_1_ = bf16[144,1152]{1,0:T(8,128)(2,1)S(1)} collective-permute-done((bf16[144,1152]{1,0:T(8,128)(2,1)S(1)}, bf16[144,1152]{1,0:T(8,128)(2,1)S(1)}, u32[]{:S(2)}, u32[]{:S(2)}) %collective-permute-start.72) | collective-permute-done | bytes 331808 | tf_op jit(solution)/shard_map/ppermute | solution.py:157
  275.8 6.3 %collective-permute-done.73.refs_1_ = bf16[144,1152]{1,0:T(8,128)(2,1)S(1)} collective-permute-done((bf16[144,1152]{1,0:T(8,128)(2,1)S(1)}, bf16[144,1152]{1,0:T(8,128)(2,1)S(1)}, u32[]{:S(2)}, u32[]{:S(2)}) %collective-permute-start.73) | collective-permute-done | bytes 331808 | tf_op jit(solution)/shard_map/ppermute | solution.py:157
  283.1 6.5 %collective-permute-done.75.refs_3_ = f32[16,1152]{1,0:T(8,128)S(1)} collective-permute-done((f32[16,1152]{1,0:T(8,128)S(1)}, f32[16,1152]{1,0:T(8,128)S(1)}, u32[]{:S(2)}, u32[]{:S(2)}) %collective-permute-start.75) | collective-permute-done | bytes 73760 | tf_op jit(solution)/shard_map/ppermute | solution.py:165
  289.5 4.8 %collective-permute-done.76.refs_4_ = f32[16,1152]{1,0:T(8,128)S(1)} collective-permute-done((f32[16,1152]{1,0:T(8,128)S(1)}, f32[16,1152]{1,0:T(8,128)S(1)}, u32[]{:S(2)}, u32[]{:S(2)}) %collective-permute-start.76) | collective-permute-done | bytes 73760 | tf_op jit(solution)/shard_map/ppermute | solution.py:165
  296.6 3.5 collective-permute-done.78.refs_6_
  300.8 3.6 %collective-permute-done.80.refs_8_ = f32[16,1152]{1,0:T(8,128)S(1)} collective-permute-done((f32[16,1152]{1,0:T(8,128)S(1)}, f32[16,1152]{1,0:T(8,128)S(1)}, u32[]{:S(2)}, u32[]{:S(2)}) %collective-permute-start.80) | collective-permute-done | bytes 73760 | tf_op jit(solution)/shard_map/ppermute | solution.py:165
  309.8 6.1 %collective-permute-done.83.refs_1_ = bf16[144,1152]{1,0:T(8,128)(2,1)S(1)} collective-permute-done((bf16[144,1152]{1,0:T(8,128)(2,1)S(1)}, bf16[144,1152]{1,0:T(8,128)(2,1)S(1)}, u32[]{:S(2)}, u32[]{:S(2)}) %collective-permute-start.83) | collective-permute-done | bytes 331808 | tf_op jit(solution)/shard_map/ppermute | solution.py:157
  334.8 3.6 fusion.1
  (284 shorter events, 163.9 us)
Async XLA Ops:
  8.2 16.4 %collective-permute-start = (bf16[160,1440]{1,0:T(8,128)(2,1)S(1)}, bf16[160,1440]{1,0:T(8,128)(2,1)S(1)}, u32[]{:S(2)}, u32[]{:S(2)}) collective-permute-start(bf16[160,1440]{1,0:T(8,128)(2,1)S(1)} %get-tuple-element.365.refs_0_), channel_id=1, source_target_pairs={{0,8},{4,12},{8,16},{12,20},{16,24},{20,28},{24,0},{28,4},{1,9},{5... | collective-permute-start | bytes 1382408 | tf_op jit(solution)/shard_map/ppermute | solution.py:157
  11.3 13.3 %collective-permute-start.1 = (bf16[160,1440]{1,0:T(8,128)(2,1)S(1)}, bf16[160,1440]{1,0:T(8,128)(2,1)S(1)}, u32[]{:S(2)}, u32[]{:S(2)}) collective-permute-start(bf16[160,1440]{1,0:T(8,128)(2,1)S(1)} %get-tuple-element.365.refs_0_), channel_id=1, source_target_pairs={{0,4},{4,0},{8,12},{12,8},{16,20},{20,16},{24,28},{28,24},{1,5},{5... | collective-permute-start | bytes 1382408 | tf_op jit(solution)/shard_map/ppermute | solution.py:154
  14.5 12.6 %collective-permute-start.3 = (bf16[128,1152]{1,0:T(8,128)(2,1)S(1)}, bf16[128,1152]{1,0:T(8,128)(2,1)S(1)}, u32[]{:S(2)}, u32[]{:S(2)}) collective-permute-start(bf16[128,1152]{1,0:T(8,128)(2,1)S(1)} %get-tuple-element.373), channel_id=1, source_target_pairs={{0,1},{1,0},{2,3},{3,2},{4,5},{5,4},{6,7},{7,6},{8,9},{9,8},{10,11... | collective-permute-start | bytes 884744 | tf_op jit(solution)/shard_map/ppermute | solution.py:148
  24.6 14.2 %collective-permute-start.6 = (bf16[160,1440]{1,0:T(8,128)(2,1)S(1)}, bf16[160,1440]{1,0:T(8,128)(2,1)S(1)}, u32[]{:S(2)}, u32[]{:S(2)}) collective-permute-start(bf16[160,1440]{1,0:T(8,128)(2,1)S(1)} %collective-permute-done.refs_1_), channel_id=1, source_target_pairs={{0,8},{4,12},{8,16},{12,20},{16,24},{20,28},{24,0},{28,4},{1,9},{5... | collective-permute-start | bytes 1382408 | tf_op jit(solution)/shard_map/ppermute | solution.py:157
  25.6 13.2 %collective-permute-start.7 = (bf16[160,1440]{1,0:T(8,128)(2,1)S(1)}, bf16[160,1440]{1,0:T(8,128)(2,1)S(1)}, u32[]{:S(2)}, u32[]{:S(2)}) collective-permute-start(bf16[160,1440]{1,0:T(8,128)(2,1)S(1)} %collective-permute-done.refs_1_), channel_id=1, source_target_pairs={{0,4},{4,0},{8,12},{12,8},{16,20},{20,16},{24,28},{28,24},{1,5},{5... | collective-permute-start | bytes 1382408 | tf_op jit(solution)/shard_map/ppermute | solution.py:154
  38.8 13.4 %collective-permute-start.12 = (bf16[160,1440]{1,0:T(8,128)(2,1)S(1)}, bf16[160,1440]{1,0:T(8,128)(2,1)S(1)}, u32[]{:S(2)}, u32[]{:S(2)}) collective-permute-start(bf16[160,1440]{1,0:T(8,128)(2,1)S(1)} %collective-permute-done.6.refs_3_), channel_id=1, source_target_pairs={{0,8},{4,12},{8,16},{12,20},{16,24},{20,28},{24,0},{28,4},{1,9},{5... | collective-permute-start | bytes 1382408 | tf_op jit(solution)/shard_map/ppermute | solution.py:157
  53.8 37.7 %collective-permute-start.28 = (bf16[144,2304]{1,0:T(8,128)(2,1)S(1)}, bf16[144,2304]{1,0:T(8,128)(2,1)S(1)}, u32[]{:S(2)}, u32[]{:S(2)}) collective-permute-start(bf16[144,2304]{1,0:T(8,128)(2,1)S(1)} %get-tuple-element.427.refs_0_), channel_id=1, source_target_pairs={{0,8},{4,12},{8,16},{12,20},{16,24},{20,28},{24,0},{28,4},{1,9},{5... | collective-permute-start | bytes 1990664 | tf_op jit(solution)/shard_map/ppermute | solution.py:157
  64.2 27.3 %collective-permute-start.29 = (bf16[144,2304]{1,0:T(8,128)(2,1)S(1)}, bf16[144,2304]{1,0:T(8,128)(2,1)S(1)}, u32[]{:S(2)}, u32[]{:S(2)}) collective-permute-start(bf16[144,2304]{1,0:T(8,128)(2,1)S(1)} %get-tuple-element.427.refs_0_), channel_id=1, source_target_pairs={{0,4},{4,0},{8,12},{12,8},{16,20},{20,16},{24,28},{28,24},{1,5},{5... | collective-permute-start | bytes 1990664 | tf_op jit(solution)/shard_map/ppermute | solution.py:154
  65.1 22.3 %collective-permute-start.19 = (bf16[160,1440]{1,0:T(8,128)(2,1)S(1)}, bf16[160,1440]{1,0:T(8,128)(2,1)S(1)}, u32[]{:S(2)}, u32[]{:S(2)}) collective-permute-start(bf16[160,1440]{1,0:T(8,128)(2,1)S(1)} %collective-permute-done.16.refs_7_), channel_id=1, source_target_pairs={{0,1},{1,0},{2,3},{3,2},{4,5},{5,4},{6,7},{7,6},{8,9},{9,8},{10,11... | collective-permute-start | bytes 1382408 | tf_op jit(solution)/shard_map/ppermute | solution.py:148
  91.5 15.9 %collective-permute-start.31 = (bf16[144,2304]{1,0:T(8,128)(2,1)S(1)}, bf16[144,2304]{1,0:T(8,128)(2,1)S(1)}, u32[]{:S(2)}, u32[]{:S(2)}) collective-permute-start(bf16[144,2304]{1,0:T(8,128)(2,1)S(1)} %collective-permute-done.28.refs_1_), channel_id=1, source_target_pairs={{0,8},{4,12},{8,16},{12,20},{16,24},{20,28},{24,0},{28,4},{1,9},{5... | collective-permute-start | bytes 1990664 | tf_op jit(solution)/shard_map/ppermute | solution.py:157
  91.7 15.7 %collective-permute-start.32 = (bf16[144,2304]{1,0:T(8,128)(2,1)S(1)}, bf16[144,2304]{1,0:T(8,128)(2,1)S(1)}, u32[]{:S(2)}, u32[]{:S(2)}) collective-permute-start(bf16[144,2304]{1,0:T(8,128)(2,1)S(1)} %collective-permute-done.28.refs_1_), channel_id=1, source_target_pairs={{0,4},{4,0},{8,12},{12,8},{16,20},{20,16},{24,28},{28,24},{1,5},{5... | collective-permute-start | bytes 1990664 | tf_op jit(solution)/shard_map/ppermute | solution.py:154
  107.4 13.6 %collective-permute-start.34 = (bf16[144,2304]{1,0:T(8,128)(2,1)S(1)}, bf16[144,2304]{1,0:T(8,128)(2,1)S(1)}, u32[]{:S(2)}, u32[]{:S(2)}) collective-permute-start(bf16[144,2304]{1,0:T(8,128)(2,1)S(1)} %collective-permute-done.31.refs_3_), channel_id=1, source_target_pairs={{0,8},{4,12},{8,16},{12,20},{16,24},{20,28},{24,0},{28,4},{1,9},{5... | collective-permute-start | bytes 1990664 | tf_op jit(solution)/shard_map/ppermute | solution.py:157
  135.6 13.2 %collective-permute-start.38 = (bf16[8,144,1152]{2,1,0:T(8,128)(2,1)S(1)}, bf16[8,144,1152]{2,1,0:T(8,128)(2,1)S(1)}, u32[]{:S(2)}, u32[]{:S(2)}) collective-permute-start(bf16[8,144,1152]{2,1,0:T(8,128)(2,1)S(1)} %get-tuple-element.466), channel_id=1, source_target_pairs={{0,1},{1,0},{2,3},{3,2},{4,5},{5,4},{6,7},{7,6},{8,9},{9,8},{10,11... | collective-permute-start | bytes 7962632 | tf_op jit(solution)/shard_map/ppermute | solution.py:148
  165.8 28.2 %collective-permute-start.55 = (bf16[512,1152]{1,0:T(8,128)(2,1)S(1)}, bf16[512,1152]{1,0:T(8,128)(2,1)S(1)}, u32[]{:S(2)}, u32[]{:S(2)}) collective-permute-start(bf16[512,1152]{1,0:T(8,128)(2,1)S(1)} %get-tuple-element.526.refs_0_), channel_id=1, source_target_pairs={{0,2},{1,3},{2,0},{3,1},{4,6},{5,7},{6,4},{7,5},{8,10},{9,11},{10,... | collective-permute-start | bytes 3538952 | tf_op jit(solution)/shard_map/ppermute | solution.py:151
  176.1 31.3 %collective-permute-start.57 = (bf16[4,144,1152]{2,1,0:T(8,128)(2,1)}, bf16[4,144,1152]{2,1,0:T(8,128)(2,1)S(1)}, u32[]{:S(2)}, u32[]{:S(2)}) collective-permute-start(bf16[4,144,1152]{2,1,0:T(8,128)(2,1)} %get-tuple-element.546), channel_id=1, source_target_pairs={{0,4},{4,0},{8,12},{12,8},{16,20},{20,16},{24,28},{28,24},{1,5},{5... | collective-permute-start | bytes 3981320 | tf_op jit(solution)/shard_map/ppermute | solution.py:154
  176.1 30.0 %collective-permute-start.56 = (bf16[288,1152]{1,0:T(8,128)(2,1)S(1)}, bf16[288,1152]{1,0:T(8,128)(2,1)S(1)}, u32[]{:S(2)}, u32[]{:S(2)}) collective-permute-start(bf16[288,1152]{1,0:T(8,128)(2,1)S(1)} %get-tuple-element.541), channel_id=1, source_target_pairs={{0,8},{4,12},{8,16},{12,20},{16,24},{20,28},{24,0},{28,4},{1,9},{5... | collective-permute-start | bytes 1990664 | tf_op jit(solution)/shard_map/ppermute | solution.py:157
  207.4 18.6 %collective-permute-start.62 = (bf16[288,1152]{1,0:T(8,128)(2,1)S(1)}, bf16[288,1152]{1,0:T(8,128)(2,1)S(1)}, u32[]{:S(2)}, u32[]{:S(2)}) collective-permute-start(bf16[288,1152]{1,0:T(8,128)(2,1)S(1)} %get-tuple-element.566), channel_id=1, source_target_pairs={{0,8},{4,12},{8,16},{12,20},{16,24},{20,28},{24,0},{28,4},{1,9},{5... | collective-permute-start | bytes 1990664 | tf_op jit(solution)/shard_map/ppermute | solution.py:157
  219.6 42.9 %collective-permute-start.69 = (bf16[4,144,1152]{2,1,0:T(8,128)(2,1)S(1)}, bf16[4,144,1152]{2,1,0:T(8,128)(2,1)S(1)}, u32[]{:S(2)}, u32[]{:S(2)}) collective-permute-start(bf16[4,144,1152]{2,1,0:T(8,128)(2,1)S(1)} %get-tuple-element.606), channel_id=1, source_target_pairs={{0,4},{4,0},{8,12},{12,8},{16,20},{20,16},{24,28},{28,24},{1,5},{5... | collective-permute-start | bytes 3981320 | tf_op jit(solution)/shard_map/ppermute | solution.py:154
  226.6 29.4 %collective-permute-start.65 = (bf16[288,1152]{1,0:T(8,128)(2,1)S(1)}, bf16[288,1152]{1,0:T(8,128)(2,1)S(1)}, u32[]{:S(2)}, u32[]{:S(2)}) collective-permute-start(bf16[288,1152]{1,0:T(8,128)(2,1)S(1)} %get-tuple-element.592), channel_id=1, source_target_pairs={{0,8},{4,12},{8,16},{12,20},{16,24},{20,28},{24,0},{28,4},{1,9},{5... | collective-permute-start | bytes 1990664 | tf_op jit(solution)/shard_map/ppermute | solution.py:157
  226.7 24.8 %collective-permute-start.63 = (bf16[144,1152]{1,0:T(8,128)(2,1)S(1)}, bf16[144,1152]{1,0:T(8,128)(2,1)S(1)}, u32[]{:S(2)}, u32[]{:S(2)}) collective-permute-start(bf16[144,1152]{1,0:T(8,128)(2,1)S(1)} %get-tuple-element.571), channel_id=1, source_target_pairs={{0,8},{4,12},{8,16},{12,20},{16,24},{20,28},{24,0},{28,4},{1,9},{5... | collective-permute-start | bytes 995336 | tf_op jit(solution)/shard_map/ppermute | solution.py:157
  227.0 25.2 %collective-permute-start.64 = (bf16[256,1152]{1,0:T(8,128)(2,1)S(1)}, bf16[256,1152]{1,0:T(8,128)(2,1)S(1)}, u32[]{:S(2)}, u32[]{:S(2)}) collective-permute-start(bf16[256,1152]{1,0:T(8,128)(2,1)S(1)} %copy-done.21), channel_id=1, source_target_pairs={{0,2},{1,3},{2,0},{3,1},{4,6},{5,7},{6,4},{7,5},{8,10},{9,11},{10,... | collective-permute-start | bytes 1769480 | tf_op jit(solution)/shard_map/ppermute | solution.py:151
  264.6 54.1 %collective-permute-start.86 = (bf16[256,1152]{1,0:T(8,128)(2,1)S(1)}, bf16[256,1152]{1,0:T(8,128)(2,1)S(1)}, u32[]{:S(2)}, u32[]{:S(2)}) collective-permute-start(bf16[256,1152]{1,0:T(8,128)(2,1)S(1)} %get-tuple-element.661), channel_id=1, source_target_pairs={{0,2},{1,3},{2,0},{3,1},{4,6},{5,7},{6,4},{7,5},{8,10},{9,11},{10,... | collective-permute-start | bytes 1769480 | tf_op jit(solution)/shard_map/ppermute | solution.py:151
  266.5 15.5 %collective-permute-start.73 = (bf16[144,1152]{1,0:T(8,128)(2,1)S(1)}, bf16[144,1152]{1,0:T(8,128)(2,1)S(1)}, u32[]{:S(2)}, u32[]{:S(2)}) collective-permute-start(bf16[144,1152]{1,0:T(8,128)(2,1)S(1)} %get-tuple-element.622), channel_id=1, source_target_pairs={{0,8},{4,12},{8,16},{12,20},{16,24},{20,28},{24,0},{28,4},{1,9},{5... | collective-permute-start | bytes 995336 | tf_op jit(solution)/shard_map/ppermute | solution.py:157
  267.2 15.9 %collective-permute-start.74 = (f32[16,1152]{1,0:T(8,128)S(1)}, f32[16,1152]{1,0:T(8,128)S(1)}, u32[]{:S(2)}, u32[]{:S(2)}) collective-permute-start(f32[16,1152]{1,0:T(8,128)S(1)} %get-tuple-element.626), channel_id=1, source_target_pairs={{0,4},{4,8},{8,12},{12,16},{16,20},{20,24},{24,28},{28,0},{1,5},{5... | collective-permute-start | bytes 221192 | tf_op jit(solution)/shard_map/ppermute | solution.py:165
  275.6 30.7 %collective-permute-start.81 = (bf16[144,1152]{1,0:T(8,128)(2,1)S(1)}, bf16[144,1152]{1,0:T(8,128)(2,1)S(1)}, u32[]{:S(2)}, u32[]{:S(2)}) collective-permute-start(bf16[144,1152]{1,0:T(8,128)(2,1)S(1)} %get-tuple-element.643), channel_id=1, source_target_pairs={{0,8},{4,12},{8,16},{12,20},{16,24},{20,28},{24,0},{28,4},{1,9},{5... | collective-permute-start | bytes 995336 | tf_op jit(solution)/shard_map/ppermute | solution.py:157
  275.7 33.0 %collective-permute-start.82 = (bf16[144,1152]{1,0:T(8,128)(2,1)S(1)}, bf16[144,1152]{1,0:T(8,128)(2,1)S(1)}, u32[]{:S(2)}, u32[]{:S(2)}) collective-permute-start(bf16[144,1152]{1,0:T(8,128)(2,1)S(1)} %get-tuple-element.718), channel_id=1, source_target_pairs={{0,4},{4,0},{8,12},{12,8},{16,20},{20,16},{24,28},{28,24},{1,5},{5... | collective-permute-start | bytes 995336 | tf_op jit(solution)/shard_map/ppermute | solution.py:154
  309.3 13.2 %collective-permute-start.87 = (bf16[144,1152]{1,0:T(8,128)(2,1)S(1)}, bf16[144,1152]{1,0:T(8,128)(2,1)S(1)}, u32[]{:S(2)}, u32[]{:S(2)}) collective-permute-start(bf16[144,1152]{1,0:T(8,128)(2,1)S(1)} %get-tuple-element.666.refs_0_), channel_id=1, source_target_pairs={{0,2},{1,3},{2,0},{3,1},{4,6},{5,7},{6,4},{7,5},{8,10},{9,11},{10,... | collective-permute-start | bytes 995336 | tf_op jit(solution)/shard_map/ppermute | solution.py:151
  318.7 14.4 %collective-permute-start.91 = (bf16[144,1152]{1,0:T(8,128)(2,1)S(1)}, bf16[144,1152]{1,0:T(8,128)(2,1)S(1)}, u32[]{:S(2)}, u32[]{:S(2)}) collective-permute-start(bf16[144,1152]{1,0:T(8,128)(2,1)S(1)} %get-tuple-element.654.refs_0_), channel_id=1, source_target_pairs={{0,1},{1,0},{2,3},{3,2},{4,5},{5,4},{6,7},{7,6},{8,9},{9,8},{10,11... | collective-permute-start | bytes 995336 | tf_op jit(solution)/shard_map/ppermute | solution.py:148
  322.4 33.1 %collective-permute-start.102 = (f32[128,1152]{1,0:T(8,128)}, f32[128,1152]{1,0:T(8,128)S(1)}, u32[]{:S(2)}, u32[]{:S(2)}) collective-permute-start(f32[128,1152]{1,0:T(8,128)} %get-tuple-element.699), channel_id=1, source_target_pairs={{0,1},{1,0},{2,3},{3,2},{4,5},{5,4},{6,7},{7,6},{8,9},{9,8},{10,11... | collective-permute-start | bytes 1769480 | tf_op jit(solution)/shard_map/ppermute | solution.py:148
  333.6 21.9 %collective-permute-start.101 = (bf16[128,1152]{1,0:T(8,128)(2,1)}, bf16[128,1152]{1,0:T(8,128)(2,1)}, u32[]{:S(2)}, u32[]{:S(2)}) collective-permute-start(bf16[128,1152]{1,0:T(8,128)(2,1)} %copy-done.22), channel_id=1, source_target_pairs={{0,1},{1,0},{2,3},{3,2},{4,5},{5,4},{6,7},{7,6},{8,9},{9,8},{10,11... | collective-permute-start | bytes 884744 | tf_op jit(solution)/shard_map/ppermute | solution.py:148
  338.4 15.8 %collective-permute-start.98 = (f32[2,144]{1,0:T(2,128)S(1)}, f32[2,144]{1,0:T(2,128)S(1)}, u32[]{:S(2)}, u32[]{:S(2)}) collective-permute-start(f32[2,144]{1,0:T(2,128)S(1)} %get-tuple-element.686), channel_id=1, source_target_pairs={{0,20},{4,24},{8,28},{12,0},{16,4},{20,8},{24,12},{28,16},{1,21},{... | collective-permute-start | bytes 3464 | tf_op jit(solution)/shard_map/ppermute | solution.py:165
  341.5 12.7 %collective-permute-start.99 = (f32[2,144]{1,0:T(2,128)S(1)}, f32[2,144]{1,0:T(2,128)S(1)}, u32[]{:S(2)}, u32[]{:S(2)}) collective-permute-start(f32[2,144]{1,0:T(2,128)S(1)} %get-tuple-element.687), channel_id=1, source_target_pairs={{0,24},{4,28},{8,0},{12,4},{16,8},{20,12},{24,16},{28,20},{1,25},{... | collective-permute-start | bytes 3464 | tf_op jit(solution)/shard_map/ppermute | solution.py:165
  (94 other events, 670.8 us)
where the time goes:
time: 364 us; the launch traced here: 358 us
  waiting for transfers between devices  152 us (42%)
  Pallas kernels  115 us (32%)
  starting transfers between devices  73.8 us (20%)
  local copies, waits for them, and re-layouts  8.81 us (2%)
    pallas_call x43, Pallas kernels, run(): pl.pallas_call(body, out_shape=tuple(outs) + (struct(self.token.shape, se...  107 us
    ppermute x15, waiting for transfers between devices, to_line(): lax.ppermute(values, 'fsdp', [(i, (i + 2) % self.shards) for i in range(s...  53.6 us
    ppermute x14, waiting for transfers between devices, to_side(): return lax.ppermute(values, 'seq', [(i, i ^ 2) for i in range(self.seats)])  48.7 us
    ppermute x21, waiting for transfers between devices, exchange(): results.append(lax.ppermute(values[step], 'fsdp', shift))  27.6 us
    ppermute x21, starting transfers between devices, exchange(): results.append(lax.ppermute(values[step], 'fsdp', shift))  24.7 us
    ppermute x11, waiting for transfers between devices, to_pair(): lax.ppermute(values, 'fsdp', [(i, i ^ 1) for i in range(self.shards)])  21.1 us
    ppermute x14, starting transfers between devices, to_side(): return lax.ppermute(values, 'seq', [(i, i ^ 2) for i in range(self.seats)])  20.3 us
    ppermute x15, starting transfers between devices, to_line(): lax.ppermute(values, 'fsdp', [(i, (i + 2) % self.shards) for i in range(s...  10.5 us
  transfers between devices with their start and end apart: 103, of which 40 were waited for; matrix products, arithmetic and copies ran while one was open for 2% of the time, Pallas kernels for 28%

commit v1 on v0

--- a/solution.py
+++ b/solution.py
@@ -105,8 +105,8 @@
             for index in range(count):
                 result = refs[index][0]
                 if sums:
-                    result = low(wide(result) + wide(refs[count + index][...]))
-                outs[index][...] = result
+                    result = wide(result) + wide(refs[count + index][...])
+                outs[index][...] = result.astype(outs[index].dtype)
 
         def block_at(unused, place):
             return (lax.rem(place[LINE] + (lines - step), lines), 0, 0)
@@ -123,7 +123,7 @@
         results = pl.pallas_call(
             kernel,
             grid_spec=spec,
-            out_shape=(struct((rows, columns), jnp.bfloat16),) * count
+            out_shape=tuple(struct((rows, columns), block.dtype) for block in blocks)
             + (struct(self.token.shape, self.token.dtype),),
             input_output_aliases={1 + count + len(sums): count},
             compiler_params=ROOM,
@@ -153,17 +153,18 @@
     def to_pair(self, values):
         return lax.ppermute(values, "fsdp", [(i, i ^ 1) for i in range(self.shards)])
 
-    def to_line(self, values):
+    def to_line(self, values, step=1):
         return lax.ppermute(
-            values, "fsdp", [(i, (i + 2) % self.shards) for i in range(self.shards)]
+            values, "fsdp", [(i, (i + 2 * step) % self.shards) for i in range(self.shards)]
         )
 
-    def exchange(self, values):
-        results = [values[0]]
-        for step in range(1, self.shards):
-            shift = [(i, (i + step) % self.shards) for i in range(self.shards)]
-            results.append(lax.ppermute(values[step], "fsdp", shift))
-        return results
+
+def piece_shard(place, index, shards):
+    lines = shards // 2
+    near = index > 0 and (index % 2 == 0 or index == shards - 1)
+    back = (index - 1) // 2 if near else (index + 1) // 2
+    line = lax.rem(place[LINE] + (lines - back), lines)
+    return 2 * line + (1 - place[PAIR] if near else place[PAIR])
 
 
 class Gather:
@@ -206,18 +207,14 @@
         return self.place(self.copies + [self.order.wait(*self.copied)], widths, head, False)
 
     def place(self, pieces, widths, head, keep_head):
-        shards, lines = self.here.shards, self.here.line_size
+        shards = self.here.shards
         rows, total = pieces[0].shape
         rows -= head
 
         def kernel(place, *refs):
             targets = refs[shards:]
             for index in range(shards):
-                near = index > 0 and (index % 2 == 0 or index == shards - 1)
-                back = (index - 1) // 2 if near else (index + 1) // 2
-                line = lax.rem(place[LINE] + (lines - back), lines)
-                pair = 1 - place[PAIR] if near else place[PAIR]
-                shard = 2 * line + pair
+                shard = piece_shard(place, index, shards)
                 start = 0
                 for target, columns in zip(targets, widths):
                     target[shard] = refs[index][head:, start : start + columns]
@@ -231,20 +228,70 @@
         return self.order.run(kernel, outs, *pieces)
 
 
+class Lines:
+    def __init__(self, here, order, piece):
+        self.here, self.order = here, order
+        self.pieces = [piece] + [here.to_line(piece, step) for step in range(1, here.line_size)]
+
+    def join(self):
+        count = len(self.pieces)
+        self.pieces[1:] = self.order.wait(*self.pieces[1:])
+
+        def kernel(place, *refs):
+            for index in range(count):
+                refs[-1][index] = refs[index][...]
+
+        shape = struct((count,) + self.pieces[0].shape, self.pieces[0].dtype)
+        self.mine = self.order.run(kernel, [shape], *self.pieces)
+        self.got = self.here.to_pair(self.mine)
+
+    def finish(self):
+        return self.mine, self.order.wait(self.got)
+
+
+class LineSum:
+    def __init__(self, here, order, parts):
+        self.here, self.order = here, order
+        self.parts = [parts[0]]
+        self.parts += [here.to_line(parts[step], step) for step in range(1, here.line_size)]
+
+    def join(self):
+        count = len(self.parts)
+        self.parts[1:] = self.order.wait(*self.parts[1:])
+
+        def kernel(place, *refs):
+            give, mine = refs[count:]
+            total = refs[0][...]
+            for index in range(1, count):
+                total = total + refs[index][...]
+            give[...] = total[0:1]
+            mine[...] = total[1:2]
+
+        row = struct((1, self.parts[0].shape[1]), self.parts[0].dtype)
+        give, self.mine = self.order.run(kernel, [row, row], *self.parts)
+        self.got = self.here.to_pair(give)
+
+    def finish(self):
+        return self.order.wait(self.got), self.mine
+
+
 class Scatter:
-    def __init__(self, here, order, give, mine):
-        self.here, self.order, self.mine = here, order, mine
-        self.got = here.to_pair(give)
+    def __init__(self, here, order, *blocks):
+        self.here, self.order, self.mine = here, order, blocks[-1]
+        self.got = [here.to_pair(give) for give in blocks[:-1]]
         self.step = 0
 
     def join(self):
-        got = self.order.wait(self.got)
-
-        def kernel(place, got_ref, mine_ref, out):
-            out[...] = low(wide(mine_ref[...]) + wide(got_ref[...]))
+        got = [self.order.wait(part) for part in self.got]
+        share = self.mine.shape[0] // len(got)
+
+        def kernel(place, mine_ref, *refs):
+            for index in range(len(got)):
+                span = slice(index * share, (index + 1) * share)
+                refs[-1][span] = low(wide(mine_ref[span]) + wide(refs[index][...]))
 
         shape = struct(self.mine.shape, jnp.bfloat16)
-        self.kept = [self.order.run(kernel, [shape], got, self.mine)]
+        self.kept = [self.order.run(kernel, [shape], self.mine, *got)]
         self.sums = []
         self.send()
 
@@ -265,30 +312,6 @@
         while self.step < self.here.line_size:
             self.turn()
         return self.sums[0]
-
-
-class ScatterLines(Scatter):
-    def __init__(self, here, order, both):
-        self.here, self.order, self.step = here, order, 0
-        self.kept, self.sums = [both], []
-        self.send()
-
-    def join(self):
-        while self.step < self.here.line_size:
-            self.turn()
-        total = self.sums[0]
-        rows = total.shape[0] // 2
-        self.mine = total[rows:]
-        self.got = self.here.to_pair(total[:rows])
-
-    def finish(self):
-        got = self.order.wait(self.got)
-
-        def kernel(place, got_ref, mine_ref, out):
-            out[...] = low(wide(mine_ref[...]) + wide(got_ref[...]))
-
-        shape = struct(got.shape, jnp.bfloat16)
-        return self.order.run(kernel, [shape], got, self.mine)
 
 
 def cut_columns(place, source, target, offset, index, parts, groups):
@@ -342,7 +365,7 @@
 
     def kernel(place, heads_ref, weight_ref, *refs):
         cond_rows, mod_bias, qkv_mine, qkv_near, out_bias, up_mine, up_near, down_bias = refs[:8]
-        parts, (cond, mine, products) = refs[8 : 8 + shards], refs[8 + shards :]
+        parts, (cond, mine, products) = refs[8:-3], refs[-3:]
         shard = 2 * place[LINE] + place[PAIR]
         for index in range(shards):
             values = wide(heads_ref[index, :micros, :width])
@@ -356,9 +379,11 @@
 
         cond_rows[...] = mine[...]
         products[...] = dot(mine[...], weight_ref[...], 1, 0)
-        for step in range(shards):
-            row = lax.rem(shard + step, shards) * micros + place[CORE]
-            parts[step][...] = products[pl.ds(row, 1), :]
+        for step, target in enumerate(parts):
+            line = lax.rem(place[LINE] + step, shards // 2)
+            for row, pair in enumerate((1 - place[PAIR], place[PAIR])):
+                source = (2 * line + pair) * micros + place[CORE]
+                target[row : row + 1, :] = products[pl.ds(source, 1), :]
 
         def copy(target, row, column, name, start, count):
             base = 0
@@ -401,7 +426,7 @@
         row(shards * block),
         row(shards * block),
         row(width),
-    ] + [row(columns)] * shards
+    ] + [struct((2, columns), jnp.float32)] * (shards // 2)
     scratch = (
         pltpu.VMEM((shards * micros, width), jnp.float32),
         pltpu.VMEM((shards * micros, rows), jnp.bfloat16),
@@ -420,20 +445,20 @@
 
     def kernel(
         place, attn_ref, middle_ref, mixed_ref, down_ref, qv_mine_ref, qv_near_ref, up_mine_ref,
-        up_near_ref, mods, biases,
+        up_near_ref, out,
     ):
-        mods[0:2, :] = attn_ref[...]
-        mods[2:3, :] = middle_ref[2:3, :]
-        mods[3:5, :] = middle_ref[0:2, :]
-        mods[5:6, :] = mixed_ref[...]
-        biases[...] = jnp.zeros(biases.shape, jnp.float32)
+        out[0:2, :] = attn_ref[...]
+        out[2:3, :] = middle_ref[2:3, :]
+        out[3:5, :] = middle_ref[0:2, :]
+        out[5:6, :] = mixed_ref[...]
+        out[6:, :] = jnp.zeros((out.shape[0] - 6, width), jnp.float32)
 
         def copy(source, row, column, which, start, count):
             while count > 0:
                 index, offset = divmod(start, sizes[which])
-                length = min(count, sizes[which] - offset)
-                goal = starts[which] + offset
-                biases[index : index + 1, goal : goal + length] = source[
+                line, goal = divmod(index * sum(sizes) + starts[which] + offset, width)
+                length = min(count, sizes[which] - offset, width - goal)
+                out[6 + line : 7 + line, goal : goal + length] = source[
                     row : row + 1, column : column + length
                 ]
                 start, column, count = start + length, column + length, count - length
@@ -454,104 +479,109 @@
                         start = (index * 4 + seat) * block
                         copy(up, 0, index * block, 2, start, block)
 
-    outs = (struct((6, width), jnp.float32), struct((shards, sum(sizes)), jnp.float32))
+    outs = [struct((6 + sum(sizes) * shards // width, width), jnp.float32)]
     return order.run(
         kernel, outs, attn, middle, mixed, down, qv_mine, qv_near, up_mine, up_near
     )
 
 
-def add_sums(order, mods, biases, mods_far, biases_far):
-    def kernel(place, mods_ref, biases_ref, mods_far_ref, biases_far_ref, mods_out, biases_out):
-        mods_out[...] = mods_ref[...] + mods_far_ref[...]
-        biases_out[...] = biases_ref[...] + biases_far_ref[...]
-
-    outs = (struct(mods.shape, mods.dtype), struct(biases.shape, biases.dtype))
-    return order.run(kernel, outs, mods, biases, mods_far, biases_far)
-
-
-def sums_to_send(order, mods, biases, mods_near, biases_near):
-    rows, width = mods.shape
-    shards, columns = biases.shape
-
-    def kernel(place, mods_ref, biases_ref, mods_near_ref, biases_near_ref, *refs):
-        outs, (pair, total) = refs[:shards], refs[shards:]
-        pair[place[CORE]] = wide(low(mods_ref[...]))
-        pair[1 - place[CORE]] = wide(low(mods_near_ref[...]))
-        total[...] = biases_ref[...] + biases_near_ref[...]
-        shard = 2 * place[LINE] + place[PAIR]
-        for step in range(shards):
-            outs[step][:rows, :] = pair[0]
-            outs[step][rows : 2 * rows, :] = pair[1]
-            row = lax.rem(shard + step, shards)
-            outs[step][2 * rows :, :] = jnp.zeros((HEAD - 2 * rows, width), jnp.float32)
-            outs[step][2 * rows : 2 * rows + 1, :columns] = total[pl.ds(row, 1), :]
-
-    outs = [struct((HEAD, width), jnp.float32)] * shards
-    scratch = (
-        pltpu.VMEM((2, rows, width), jnp.float32),
-        pltpu.VMEM((shards, columns), jnp.float32),
-    )
-    return order.run(kernel, outs, mods, biases, mods_near, biases_near, scratch=scratch)
-
-
-def modulation_back(order, received, mod_weight, hidden):
-    shards, width = len(received), received[0].shape[1]
+def add_sums(order, sums, far):
+    def kernel(place, sums_ref, far_ref, out):
+        out[...] = sums_ref[...] + far_ref[...]
+
+    return order.run(kernel, [struct(sums.shape, sums.dtype)], sums, far)
+
+
+def join_sums(order, sums, near):
+    rows, width = sums.shape
+
+    def kernel(place, sums_ref, near_ref, out, held):
+        held[...] = jnp.zeros(held.shape, jnp.float32)
+        for own in range(2):
+
+            @pl.when(place[CORE] == own)
+            def _():
+                held[6 * own : 6 * own + 6, :] = sums_ref[:6, :]
+                held[6 - 6 * own : 12 - 6 * own, :] = near_ref[:6, :]
+
+        held[12 : 6 + rows, :] = sums_ref[6:, :] + near_ref[6:, :]
+        out[...] = low(held[...])
+
+    total = 2 * HEAD
+    return order.run(
+        kernel,
+        [struct((total, width), jnp.bfloat16)],
+        sums,
+        near,
+        scratch=(pltpu.VMEM((total, width), jnp.float32),),
+    )
+
+
+def modulation_back(order, mine, near, mod_weight, hidden):
+    lines, _, width = mine.shape
+    shards = 2 * lines
     rows, columns = mod_weight.shape
     sizes = (2 * width // shards, width // shards, hidden // shards, width // shards)
 
-    def kernel(place, weight_ref, *refs):
-        sources, refs = refs[:shards], refs[shards:]
-        mod_all, biases, parts, (held, products) = refs[0], refs[1:5], refs[5:-2], refs[-2:]
+    def kernel(place, weight_ref, mine_ref, near_ref, *refs):
+        mod_all, biases, (products, held, total) = refs[0], refs[1:5], refs[5:]
         shard = 2 * place[LINE] + place[PAIR]
-        total = jnp.zeros((1, sum(sizes)), jnp.float32)
-        for step in range(shards):
-            source = sources[step]
-            index = lax.rem(shard + (shards - step), shards)
+        total[...] = jnp.zeros(total.shape, jnp.float32)
+        for index in range(shards):
+            source = wide((near_ref if index % 2 else mine_ref)[index // 2])
+            line = lax.rem(place[LINE] + (lines - index // 2), lines)
+            owner = 2 * line + (1 - place[PAIR] if index % 2 else place[PAIR])
             for latent in range(2):
                 for row in range(6):
-                    held[pl.ds(2 * index + latent, 1), row * width : (row + 1) * width] = source[
+                    held[pl.ds(2 * owner + latent, 1), row * width : (row + 1) * width] = source[
                         6 * latent + row : 6 * latent + row + 1, :
                     ]
-            total = total + source[12:13, : sum(sizes)]
-        start = 0
-        for target, size in zip(biases, sizes):
-            target[...] = total[:, start : start + size]
-            start += size
+            total[...] += source[12 : 12 + total.shape[0], :]
+        for index in range(shards):
+
+            @pl.when(shard == index)
+            def _():
+                line, start = divmod(index * sum(sizes), width)
+                for target, size in zip(biases, sizes):
+                    target[...] = total[line : line + 1, start : start + size]
+                    start += size
+
         mod_all[...] = low(held[...])
         products[...] = dot(mod_all[...], weight_ref[...], 1, 1)
-        for step in range(shards):
-            row = 2 * lax.rem(shard + step, shards)
-            parts[step][0:1, :] = products[pl.ds(row, 1), :]
-            parts[step][1:2, :] = products[pl.ds(row + 1, 1), :]
 
     outs = [struct((2 * shards, columns), jnp.bfloat16)]
     outs += [struct((1, size), jnp.float32) for size in sizes]
-    outs += [struct((2, rows), jnp.float32)] * shards
+    outs.append(struct((2 * shards, rows), jnp.float32))
     scratch = (
         pltpu.VMEM((2 * shards, columns), jnp.float32),
-        pltpu.VMEM((2 * shards, rows), jnp.float32),
-    )
-    return order.run(kernel, outs, mod_weight, *received, scratch=scratch)
-
-
-def condition_back(order, received, condition):
-    shards, (micros, rows) = len(received), received[0].shape
-
-    def kernel(place, condition_ref, *refs):
-        out, held = refs[shards:]
+        pltpu.VMEM((sum(sizes) * shards // width, width), jnp.float32),
+    )
+    return order.run(kernel, outs, mod_weight, mine, near, scratch=scratch)
+
+
+def condition_back(order, mine, near, condition):
+    micros, width = condition.shape
+    lines, _, rows = mine.shape
+
+    def kernel(place, condition_ref, mine_ref, near_ref, out, held):
         shard = 2 * place[LINE] + place[PAIR]
-        for step in range(shards):
-            held[lax.rem(shard + (shards - step), shards)] = refs[step][...]
+        for index in range(2 * lines):
+            source = near_ref if index % 2 else mine_ref
+            line = lax.rem(place[LINE] + (lines - index // 2), lines)
+            owner = 2 * line + (1 - place[PAIR] if index % 2 else place[PAIR])
+            for latent in range(micros):
+                row = source[index // 2, pl.ds(micros * shard + latent, 1), :]
+                held[owner, latent : latent + 1, :] = row
         values = wide(condition_ref[...])
         sigma = 1.0 / (1.0 + jnp.exp(-values))
         slope = sigma * (1.0 + values * (1.0 - sigma))
-        for index in range(shards):
+        for index in range(2 * lines):
             span = slice(index * rows, (index + 1) * rows)
             out[:, span] = held[index] * slope[:, span]
 
     outs = [struct(condition.shape, jnp.float32)]
-    scratch = (pltpu.VMEM((shards, micros, rows), jnp.float32),)
-    return order.run(kernel, outs, condition, *received, scratch=scratch)
+    scratch = (pltpu.VMEM((2 * lines, micros, rows), jnp.float32),)
+    return order.run(kernel, outs, condition, mine, near, scratch=scratch)
 
 
 def cut_feed(order, up_weight, down_weight, shards):
@@ -955,27 +985,25 @@
                 write(shard // 2, shard % 2 == own, low(part + wide(met)))
 
 
-def weight_sum(order, shards, left_side, right_side, met, join=False):
+def weight_sum(order, shards, left_side, right_side, met, parts=1):
     rows, columns = left_side.shape[1], right_side.shape[1]
-    piece = rows // shards
+    lines = shards // 2
+    share = lines // parts
 
     def kernel(place, left_ref, right_ref, *refs):
         met_refs, outs = refs[: len(met)], refs[len(met) :]
 
-        def write(line, mine, part):
-            if join:
-                start = piece if mine else 0
-                outs[0][line, start : start + piece] = part
+        def write(line, own, part):
+            if own:
+                outs[parts][line] = part
             else:
-                outs[1 if mine else 0][line] = part
+                outs[line // share][line % share] = part
 
         total = dot(left_ref[...], right_ref[...], 0, 0)
         split_pairs(place, total, shards, met_refs, 0, write)
 
-    if join:
-        outs = (struct((shards // 2, 2 * piece, columns), jnp.bfloat16),)
-    else:
-        outs = (struct((shards // 2, piece, columns), jnp.bfloat16),) * 2
+    outs = [struct((share, rows // shards, columns), jnp.bfloat16)] * parts
+    outs.append(struct((lines, rows // shards, columns), jnp.bfloat16))
     return order.run(kernel, outs, left_side, right_side, *met)
 
 
@@ -1201,11 +1229,11 @@
         down_bias,
         *mod_parts,
     ) = modulation_parts(order, heads_all, mod_weight, micros, width, hidden)
-    mod_parts = here.exchange(mod_parts)
+    mod_sum = LineSum(here, order, mod_parts)
+    mod_sum.join()
+    mod_parts = mod_sum.finish()
+    feed_ring.turn()
     qkv_near, out_near = ring.finish_near(attention_widths, HEAD)
-    cots = (cot_mine, cot_near, cot_far, wait(cot_far_near))
-    mod_parts = [mod_parts[0]] + list(wait(*mod_parts[1:]))
-    feed_ring.turn()
     mod, attn_in, attn_turned, means_one, inverses_one = norm_tokens(
         order, lats, mod_parts, mod_bias
     )
@@ -1227,6 +1255,7 @@
         lats,
         mod,
     )
+    cots = (cot_mine, cot_near, cot_far, wait(cot_far_near))
     grad_mlp, down_sums = gate_grad(order, cots, mod)
     feed_ring.turn()
     up_mine, down_mine = feed_ring.finish((hidden_part, width))
@@ -1246,14 +1275,14 @@
     def to_core(chunks):
         return [here.to_core(chunk) for chunk in chunks]
 
+    down_met = to_core(weight_grad(order, shards, act_near, grad_mlp, 8))
     up_met = to_core(weight_grad(order, shards, mlp_in, pre_near, 8))
-    down_met = to_core(weight_grad(order, shards, act_near, grad_mlp, 8))
+    down_met = wait(*down_met)
+    down_sum = Scatter(
+        here, order, *weight_sum(order, shards, act_mine, grad_mlp, down_met, parts=2)
+    )
     up_met = wait(*up_met)
-    up_sum = ScatterLines(
-        here, order, weight_sum(order, shards, mlp_in, pre_mine, up_met, join=True)
-    )
-    down_met = wait(*down_met)
-    down_sum = Scatter(here, order, *weight_sum(order, shards, act_mine, grad_mlp, down_met))
+    up_sum = Scatter(here, order, *weight_sum(order, shards, mlp_in, pre_mine, up_met))
     feed_own, feed_give = feed_out(order, act_mine, down_mine, act_near, down_near)
     feed_far = here.to_side(feed_give)
 
@@ -1263,9 +1292,8 @@
     )
     qkv_grad_near, qv_sums_near = attend_back(order, 1, parts_near, out_full, grad_attn)
     met = to_core(
-        attention_grad(order, shards, attn_turned, qkv_grad_near, heads_out, grad_attn, 4)
-    )
-    up_sum.turn()
+        attention_grad(order, shards, attn_turned, qkv_grad_near, heads_out, grad_attn, 8)
+    )
     qkv_grad_mine, qv_sums_mine = attend_back(order, 0, parts_mine, out_full, grad_attn)
     down_sum.join()
     met = wait(*met)
@@ -1274,77 +1302,74 @@
         order,
         *attention_sum(order, shards, attn_turned, qkv_grad_mine, heads_out, grad_attn, met),
     )
-    up_sum.turn()
-    attn_own, attn_give, attn_sums = attention_in_back(
-        order, qkv_grad_mine, qkv_mine, qkv_grad_near, qkv_near, lats, means_one, inverses_one
-    )
-    attn_far = here.to_side(attn_give)
-    down_sum.turn()
     feed_far = wait(feed_far)
     mixed_mine, mixed_give, mix_sums = mix(
         order, feed_own, feed_far, down_bias, lats, branch, cots, mod
     )
-    mixed_near = here.to_core(mixed_give)
-
-    mods, biases = token_sums(
+    attn_own, attn_give, attn_sums = attention_in_back(
+        order, qkv_grad_mine, qkv_mine, qkv_grad_near, qkv_near, lats, means_one, inverses_one
+    )
+    down_sum.turn()
+
+    sums = token_sums(
         order, shards, attn_sums, middle_sums, mix_sums, down_sums, qv_sums_mine, qv_sums_near,
         up_sums_mine, up_sums_near,
     )
-    mods_far, biases_far = here.to_side(mods), here.to_side(biases)
+    sums_far = here.to_side(sums)
     up_sum.join()
-    mods_far, biases_far = wait(mods_far, biases_far)
-    mods, biases = add_sums(order, mods, biases, mods_far, biases_far)
-    mods_near, biases_near = here.to_core(mods), here.to_core(biases)
+    sums = add_sums(order, sums, wait(sums_far))
+    sums_near = here.to_core(sums)
     down_sum.turn()
+    sums = join_sums(order, sums, wait(sums_near))
+    up_sum.turn()
+    grad_down = down_sum.finish()
+    sums_ring = Lines(here, order, sums)
+    attn_far = here.to_side(wait(attn_give))
+    up_sum.turn()
+    sums_ring.join()
+    down_far, down_near = here.to_side(grad_down), here.to_core(grad_down)
+    grad_up = up_sum.finish()
     attention_total.join()
-    mods_near, biases_near = wait(mods_near, biases_near)
-    received = here.exchange(sums_to_send(order, mods, biases, mods_near, biases_near))
+    attn_far = wait(attn_far)
+    tokens_mine, tokens_give = tokens_back(
+        order, attn_own, attn_far, lats, means_one, inverses_one, mod, grad_middle
+    )
+    mod_all, grad_qv_bias, grad_out_bias, grad_up_bias, grad_down_bias, grad_low = (
+        modulation_back(order, *sums_ring.finish(), mod_weight, hidden)
+    )
+    low_ring = Lines(here, order, grad_low)
     attention_total.turn()
-    grad_down = down_sum.finish()
-    down_far, down_near = here.to_side(grad_down), here.to_core(grad_down)
-    received = [received[0]] + list(wait(*received[1:]))
-    mod_all, grad_qv_bias, grad_out_bias, grad_up_bias, grad_down_bias, *grad_low = (
-        modulation_back(order, received, mod_weight, hidden)
-    )
-    grad_low = here.exchange(grad_low)
+    low_ring.join()
+    down_far, down_near = wait(down_far, down_near)
+    down_far_near = here.to_core(down_far)
+    up_far, up_near = here.to_side(grad_up), here.to_core(grad_up)
     attention_total.turn()
-    grad_up = up_sum.finish()
-    up_far, up_near = here.to_side(grad_up), here.to_core(grad_up)
+    grad_condition = condition_back(order, *low_ring.finish(), condition)
+    down_far_near = wait(down_far_near)
+    grad_down = lay_rows(order, (grad_down, down_near, down_far, down_far_near))
+    up_far, up_near = wait(up_far, up_near)
+    up_far_near = here.to_core(up_far)
+    mod_all = wait(mod_all)
+    grad_mod_weight = wait(dot(cond_rows, mod_all, 0, 0))
     grad_attention = attention_total.finish()
     attention_far = here.to_side(grad_attention)
     attention_near = here.to_core(grad_attention)
-    down_far, down_near = wait(down_far, down_near)
-    down_far_near = here.to_core(down_far)
-    attn_far = wait(attn_far)
-    tokens_mine, tokens_give = tokens_back(
-        order, attn_own, attn_far, lats, means_one, inverses_one, mod, grad_middle
-    )
-    tokens_near = here.to_core(tokens_give)
-    up_far, up_near = wait(up_far, up_near)
-    up_far_near = here.to_core(up_far)
-    down_far_near = wait(down_far_near)
-    grad_down = lay_rows(order, (grad_down, down_near, down_far, down_far_near))
-    attention_far, attention_near = wait(attention_far, attention_near)
-    attention_far_near = here.to_core(attention_far)
     up_far_near = wait(up_far_near)
     grad_up = lay_columns(
         order, (grad_up, up_near, up_far, up_far_near), (hidden_part, shards)
     )
-    attention_far_near = wait(attention_far_near)
+    mixed_near, tokens_near = wait(here.to_core(mixed_give), here.to_core(tokens_give))
+    mixed, grad_latents = lay_tokens(
+        order, (mixed_mine, mixed_near), (tokens_mine, tokens_near)
+    )
+    attention_far, attention_near = wait(attention_far, attention_near)
+    attention_far_near = wait(here.to_core(attention_far))
     grad_qkv, grad_out = lay_columns(
         order,
         (grad_attention, attention_near, attention_far, attention_far_near),
         (3 * part, 3),
         (width // 4, 1),
     )
-    grad_low = [grad_low[0]] + list(wait(*grad_low[1:]))
-    grad_condition = condition_back(order, grad_low, condition)
-    mixed_near, tokens_near = wait(mixed_near, tokens_near)
-    mixed, grad_latents = lay_tokens(
-        order, (mixed_mine, mixed_near), (tokens_mine, tokens_near)
-    )
-    mod_all = wait(mod_all)
-    grad_mod_weight = wait(dot(cond_rows, mod_all, 0, 0))
     span = 6 * width // shards
     mod_span = lax.dynamic_slice_in_dim(mod_all, here.shard * span, span, 1)
     grad_mod_bias = jnp.sum(wide(mod_span), axis=0)

time: 364 us -> 336 us (0.923)
  waiting for transfers between devices: 152 us -> 133 us
  starting transfers between devices: 73.8 us -> 67.2 us
    ppermute x36 -> x24, waiting for transfers between devices: 81.2 us -> 57.4 us  [to_line(): lax.ppermute(values, 'fsdp', [(i, (i + 2 * step) % self.shards) for i in...]
    ppermute x11 -> x15, waiting for transfers between devices: 21.1 us -> 35.8 us  [to_pair(): lax.ppermute(values, 'fsdp', [(i, i ^ 1) for i in range(self.shards)])]
    ppermute x14 -> x13, waiting for transfers between devices: 48.7 us -> 35.5 us  [to_side(): return lax.ppermute(values, 'seq', [(i, i ^ 2) for i in range(self.seats)])]
    ppermute x36 -> x24, starting transfers between devices: 35.2 us -> 26.4 us  [to_line(): lax.ppermute(values, 'fsdp', [(i, (i + 2 * step) % self.shards) for i in...]
    ppermute x11 -> x15, starting transfers between devices: 8.89 us -> 15.6 us  [to_pair(): lax.ppermute(values, 'fsdp', [(i, i ^ 1) for i in range(self.shards)])]
    ppermute x14 -> x13, starting transfers between devices: 20.3 us -> 15.8 us  [to_side(): return lax.ppermute(values, 'seq', [(i, i ^ 2) for i in range(self.seats)])]
    pallas_call x43 -> x46, Pallas kernels: 107 us -> 109 us  [run(): pl.pallas_call(body, out_shape=tuple(outs) + (struct(self.token.shape, se...]
    ppermute x42 -> x45, starting transfers between devices: 9.45 us -> 9.35 us  [to_core(): return lax.ppermute(values, 'seq', [(i, i ^ 1) for i in range(self.seats)])]
  transfers between devices with their start and end apart: 103 -> 97, of which waited for: 40 -> 41; matrix products, arithmetic and copies ran while one was open for 2% -> 1% of each run, Pallas kernels for 28% -> 31%
where the time goes in v1:
time: 336 us; the launch traced here: 331 us
  waiting for transfers between devices  133 us (40%)
  Pallas kernels  116 us (35%)
  starting transfers between devices  67.2 us (20%)
  local copies, waits for them, and re-layouts  8.73 us (3%)
    pallas_call x46, Pallas kernels, run(): pl.pallas_call(body, out_shape=tuple(outs) + (struct(self.token.shape, se...  109 us
    ppermute x24, waiting for transfers between devices, to_line(): lax.ppermute(values, 'fsdp', [(i, (i + 2 * step) % self.shards) for i in...  57.4 us
    ppermute x15, waiting for transfers between devices, to_pair(): lax.ppermute(values, 'fsdp', [(i, i ^ 1) for i in range(self.shards)])  35.8 us
    ppermute x13, waiting for transfers between devices, to_side(): return lax.ppermute(values, 'seq', [(i, i ^ 2) for i in range(self.seats)])  35.5 us
    ppermute x24, starting transfers between devices, to_line(): lax.ppermute(values, 'fsdp', [(i, (i + 2 * step) % self.shards) for i in...  26.4 us
    ppermute x13, starting transfers between devices, to_side(): return lax.ppermute(values, 'seq', [(i, i ^ 2) for i in range(self.seats)])  15.8 us
    ppermute x15, starting transfers between devices, to_pair(): lax.ppermute(values, 'fsdp', [(i, i ^ 1) for i in range(self.shards)])  15.6 us
    ppermute x45, starting transfers between devices, to_core(): return lax.ppermute(values, 'seq', [(i, i ^ 1) for i in range(self.seats)])  9.35 us
  transfers between devices with their start and end apart: 97, of which 41 were waited for; matrix products, arithmetic and copies ran while one was open for 1% of the time, Pallas kernels for 31%

profile of v1, /device:TPU:0, one launch (start us, length us, event | category | flops | bytes accessed | tf_op | source)
XLA Modules:
  0.0 331.3 jit_solution(2227016962518997466)
XLA Ops:
  0.7 3.6 %concatenate.3 = bf16[2016]{0:T(1024)(128)(2,1)S(1)} concatenate(bf16[864]{0:T(1024)(128)(2,1)} %param.16, bf16[288]{0:T(512)(128)(2,1)} %param.18, bf16[144]{0:T(256)(128)(2,1)} %param.20, bf16[576]{0:T(1024)(128)(2,1)} %param.22, bf16[144]{0:T(256)(128)(2,1)} %param.24), dimensions={0} | concatenate | bytes 8064 | tf_op jit(solution)/shard_map/concatenate | solution.py:1201
  17.6 7.0 %collective-permute-done.refs_1_ = bf16[160,1440]{1,0:T(8,128)(2,1)S(1)} collective-permute-done((bf16[160,1440]{1,0:T(8,128)(2,1)S(1)}, bf16[160,1440]{1,0:T(8,128)(2,1)S(1)}, u32[]{:S(2)}, u32[]{:S(2)}) %collective-permute-start) | collective-permute-done | bytes 460832 | tf_op jit(solution)/shard_map/ppermute | solution.py:157
  29.1 7.5 %collective-permute-done.5.refs_5_.refs_9_.refs_6_ = bf16[128,1152]{1,0:T(8,128)(2,1)S(1)} collective-permute-done((bf16[128,1152]{1,0:T(8,128)(2,1)S(1)}, bf16[128,1152]{1,0:T(8,128)(2,1)S(1)}, u32[]{:S(2)}, u32[]{:S(2)}) %collective-permute-start.5) | collective-permute-done | bytes 294944 | tf_op jit(solution)/shard_map/ppermute | solution.py:151
  40.8 3.9 %collective-permute-done.10.refs_2_.refs_6_ = bf16[128,1152]{1,0:T(8,128)(2,1)S(1)} collective-permute-done((bf16[128,1152]{1,0:T(8,128)(2,1)S(1)}, bf16[128,1152]{1,0:T(8,128)(2,1)S(1)}, u32[]{:S(2)}, u32[]{:S(2)}) %collective-permute-start.10) | collective-permute-done | bytes 294944 | tf_op jit(solution)/shard_map/ppermute | solution.py:151
  46.3 5.7 %collective-permute-done.11.refs_6_.refs_10_.refs_7_ = bf16[128,1152]{1,0:T(8,128)(2,1)S(1)} collective-permute-done((bf16[128,1152]{1,0:T(8,128)(2,1)S(1)}, bf16[128,1152]{1,0:T(8,128)(2,1)S(1)}, u32[]{:S(2)}, u32[]{:S(2)}) %collective-permute-start.11) | collective-permute-done | bytes 294944 | tf_op jit(solution)/shard_map/ppermute | solution.py:151
  54.6 8.2 %collective-permute-done.16.refs_7_ = bf16[160,1440]{1,0:T(8,128)(2,1)S(1)} collective-permute-done((bf16[160,1440]{1,0:T(8,128)(2,1)S(1)}, bf16[160,1440]{1,0:T(8,128)(2,1)S(1)}, u32[]{:S(2)}, u32[]{:S(2)}) %collective-permute-start.16) | collective-permute-done | bytes 460832 | tf_op jit(solution)/shard_map/ppermute | solution.py:154
  69.3 5.3 %collective-permute-done.19.refs_1_ = f32[2,6912]{1,0:T(2,128)S(1)} collective-permute-done((f32[2,6912]{1,0:T(2,128)S(1)}, f32[2,6912]{1,0:T(2,128)S(1)}, u32[]{:S(2)}, u32[]{:S(2)}) %collective-permute-start.19) | collective-permute-done | bytes 55328 | tf_op jit(solution)/shard_map/ppermute | solution.py:157
  87.3 4.3 %shard_map.237 = (bf16[12,72,512]{2,1,0:T(8,128)(2,1)S(1)}, bf16[288,512]{1,0:T(8,128)(2,1)S(1)}, f32[8,128]{1,0:T(8,128)S(1)}) custom-call(s32[4]{0:T(128)S(1)} %pad_add_fusion.place, bf16[512,1152]{1,0:T(8,128)(2,1)S(1)} %get-tuple-element.421.refs_0_, bf16[1152,864]{1,0:T(8,128)(2,1)S(1)} %bitcast.26, ...), custom_call_target="tpu_custom_call", output_to_operand_aliasing={{2}: (4, {})} | custom-call | flops 1 | bytes 1 | tf_op jit(solution)/shard_map/pallas_call | solution.py:85
  93.1 4.3 %shard_map.238 = (bf16[12,72,512]{2,1,0:T(8,128)(2,1)S(1)}, bf16[288,512]{1,0:T(8,128)(2,1)S(1)}, f32[8,128]{1,0:T(8,128)S(1)}) custom-call(s32[4]{0:T(128)S(1)} %pad_add_fusion.place, bf16[512,1152]{1,0:T(8,128)(2,1)S(1)} %get-tuple-element.421.refs_0_, bf16[1152,864]{1,0:T(8,128)(2,1)S(1)} %bitcast.28, ...), custom_call_target="tpu_custom_call", output_to_operand_aliasing={{2}: (4, {})} | custom-call | flops 1 | bytes 1 | tf_op jit(solution)/shard_map/pallas_call | solution.py:85
  101.9 6.3 %collective-permute-done.29.refs_3_ = bf16[288,512]{1,0:T(8,128)(2,1)S(1)} collective-permute-done((bf16[288,512]{1,0:T(8,128)(2,1)S(1)}, bf16[288,512]{1,0:T(8,128)(2,1)S(1)}, u32[]{:S(2)}, u32[]{:S(2)}) %collective-permute-start.29) | collective-permute-done | bytes 294944 | tf_op jit(solution)/shard_map/ppermute | solution.py:151
  108.2 3.8 %shard_map.239 = (bf16[1152,512]{1,0:T(8,128)(2,1)S(1)}, bf16[1152,1152]{1,0:T(8,128)(2,1)S(1)}, f32[256,1152]{1,0:T(8,128)S(1)}, f32[512,1152]{1,0:T(8,128)S(1)...) custom-call(s32[4]{0:T(128)S(1)} %pad_add_fusion.place, ...), custom_call_target="tpu_custom_call", output_to_operand_aliasing={{6}: (13, {})} | custom-call | flops 1 | bytes 1 | tf_op jit(solution)/shard_map/pallas_call | solution.py:85
  114.8 11.5 %collective-permute-done.33.refs_7_ = bf16[144,2304]{1,0:T(8,128)(2,1)S(1)} collective-permute-done((bf16[144,2304]{1,0:T(8,128)(2,1)S(1)}, bf16[144,2304]{1,0:T(8,128)(2,1)S(1)}, u32[]{:S(2)}, u32[]{:S(2)}) %collective-permute-start.33) | collective-permute-done | bytes 663584 | tf_op jit(solution)/shard_map/ppermute | solution.py:154
  127.9 4.8 %shard_map.242 = (bf16[512,1152]{1,0:T(8,128)(2,1)S(1)}, f32[512,1152]{1,0:T(8,128)S(1)}, f32[8,128]{1,0:T(8,128)S(1)}) custom-call(s32[4]{0:T(128)S(1)} %pad_add_fusion.place, bf16[512,1152]{1,0:T(8,128)(2,1)S(1)} %get-tuple-element.441.refs_0_, bf16[1152,1152]{1,0:T(8,128)(2,1)S(1)} %bitcast.18, ...), custom_call_target="tpu_custom_call", output_to_operand_aliasing={{2}: (4, {})} | custom-call | flops 1 | bytes 1 | tf_op jit(solution)/shard_map/pallas_call | solution.py:85
  136.1 4.5 %shard_map.244 = (bf16[512,1152]{1,0:T(8,128)(2,1)S(1)}, f32[512,1152]{1,0:T(8,128)S(1)}, f32[8,128]{1,0:T(8,128)S(1)}) custom-call(s32[4]{0:T(128)S(1)} %pad_add_fusion.place, bf16[512,1152]{1,0:T(8,128)(2,1)S(1)} %get-tuple-element.441.refs_0_, bf16[1152,1152]{1,0:T(8,128)(2,1)S(1)} %bitcast.20, ...), custom_call_target="tpu_custom_call", output_to_operand_aliasing={{2}: (4, {})} | custom-call | flops 1 | bytes 1 | tf_op jit(solution)/shard_map/pallas_call | solution.py:85
  144.0 5.1 %shard_map.246 = (bf16[512,1152]{1,0:T(8,128)(2,1)S(1)}, f32[8,128]{1,0:T(8,128)S(1)}) custom-call(s32[4]{0:T(128)S(1)} %pad_add_fusion.place, bf16[512,1152]{1,0:T(8,128)(2,1)S(1)} %get-tuple-element.471.refs_0_.refs_1_, bf16[1152,1152]{1,0:T(8,128)(2,1)S(1)} %bitcast.19, ...), custom_call_target="tpu_custom_call", output_to_operand_aliasing={{1}: (5, {})} | custom-call | flops 1 | bytes 1 | tf_op jit(solution)/shard_map/pallas_call | solution.py:85
  161.2 4.1 %shard_map.249 = (bf16[2,144,1152]{2,1,0:T(8,128)(2,1)}, bf16[2,144,1152]{2,1,0:T(8,128)(2,1)}, bf16[4,144,1152]{2,1,0:T(8,128)(2,1)S(1)}, f32[8,128]{1,0:T(8,128)S(1)}) custom-call(s32[4]{0:T(128)S(1)} %pad_add_fusion.place, bf16[512,1152]{1,0:T(8,128)(2,1)S(1)} %get-tuple-element.459.refs_0_, ...), custom_call_target="tpu_custom_call", output_to_operand_aliasing={{3}: (11, {})} | custom-call | flops 1 | bytes 1 | tf_op jit(solution)/shard_map/pallas_call | solution.py:85
  167.3 3.9 %shard_map.250 = (bf16[4,144,1152]{2,1,0:T(8,128)(2,1)}, bf16[4,144,1152]{2,1,0:T(8,128)(2,1)S(1)}, f32[8,128]{1,0:T(8,128)S(1)}) custom-call(s32[4]{0:T(128)S(1)} %pad_add_fusion.place, bf16[512,1152]{1,0:T(8,128)(2,1)S(1)} %get-tuple-element.441.refs_0_, ...), custom_call_target="tpu_custom_call", output_to_operand_aliasing={{2}: (11, {})} | custom-call | flops 1 | bytes 1 | tf_op jit(solution)/shard_map/pallas_call | solution.py:85
  172.3 5.5 %shard_map.251 = (f32[256,1152]{1,0:T(8,128)S(1)}, bf16[256,1152]{1,0:T(8,128)(2,1)S(1)}, f32[8,128]{1,0:T(8,128)S(1)}) custom-call(s32[4]{0:T(128)S(1)} %pad_add_fusion.place, bf16[512,1152]{1,0:T(8,128)(2,1)S(1)} %get-tuple-element.459.refs_0_, bf16[1152,1152]{1,0:T(8,128)(2,1)S(1)} %bitcast.23, ...), custom_call_target="tpu_custom_call", output_to_operand_aliasing={{2}: (5, {})} | custom-call | flops 1 | bytes 1 | tf_op jit(solution)/shard_map/pallas_call | solution.py:85
  177.8 3.8 %collective-permute-done.52.refs_1_ = bf16[512,1152]{1,0:T(8,128)(2,1)S(1)} collective-permute-done((bf16[512,1152]{1,0:T(8,128)(2,1)S(1)}, bf16[512,1152]{1,0:T(8,128)(2,1)S(1)}, u32[]{:S(2)}, u32[]{:S(2)}) %collective-permute-start.52) | collective-permute-done | bytes 1179680 | tf_op jit(solution)/shard_map/ppermute | solution.py:151
  184.1 5.8 %shard_map.253 = (bf16[512,864]{1,0:T(8,128)(2,1)S(1)}, f32[1,864]{1,0:T(1,128)S(1)}, f32[8,128]{1,0:T(8,128)S(1)}) custom-call(s32[4]{0:T(128)S(1)} %pad_add_fusion.place, bf16[12,72,512]{2,1,0:T(8,128)(2,1)S(1)} %get-tuple-element.527.refs_0_, bf16[1152,1152]{1,0:T(8,128)(2,1)S(1)} %get-tuple-element.518.refs_1_, ...), custom_call_target="tpu_custom_call", output_to_operand_aliasing={{2}: (4, {})} | custom-call | flops 1 | bytes 1 | tf_op jit(solution)/shard_map/pallas_call | solution.py:85
  193.6 3.8 %collective-permute-done.54.refs_2_ = bf16[2,144,1152]{2,1,0:T(8,128)(2,1)S(1)} collective-permute-done((bf16[2,144,1152]{2,1,0:T(8,128)(2,1)}, bf16[2,144,1152]{2,1,0:T(8,128)(2,1)S(1)}, u32[]{:S(2)}, u32[]{:S(2)}) %collective-permute-start.54) | collective-permute-done | bytes 663584 | tf_op jit(solution)/shard_map/ppermute | solution.py:154
  200.3 5.8 %shard_map.255 = (bf16[512,864]{1,0:T(8,128)(2,1)S(1)}, f32[1,864]{1,0:T(1,128)S(1)}, f32[8,128]{1,0:T(8,128)S(1)}) custom-call(s32[4]{0:T(128)S(1)} %pad_add_fusion.place, bf16[12,72,512]{2,1,0:T(8,128)(2,1)S(1)} %copy-done.5, bf16[1152,1152]{1,0:T(8,128)(2,1)S(1)} %get-tuple-element.518.refs_1_, ...), custom_call_target="tpu_custom_call", output_to_operand_aliasing={{2}: (4, {})} | custom-call | flops 1 | bytes 1 | tf_op jit(solution)/shard_map/pallas_call | solution.py:85
  209.0 4.4 %shard_map.258 = (bf16[4,144,1152]{2,1,0:T(8,128)(2,1)S(1)}, bf16[4,144,1152]{2,1,0:T(8,128)(2,1)S(1)}, f32[8,128]{1,0:T(8,128)S(1)}) custom-call(s32[4]{0:T(128)S(1)} %pad_add_fusion.place, bf16[1152,512]{1,0:T(8,128)(2,1)S(1)} %get-tuple-element.516.refs_0_, ...), custom_call_target="tpu_custom_call", output_to_operand_aliasing={{2}: (13, {})} | custom-call | flops 1 | bytes 1 | tf_op jit(solution)/shard_map/pallas_call | solution.py:85
  215.9 4.6 %shard_map.260 = (f32[256,1152]{1,0:T(8,128)S(1)}, bf16[256,1152]{1,0:T(8,128)(2,1)S(1)}, f32[2,1152]{1,0:T(2,128)S(1)}, f32[8,128]{1,0:T(8,128)S(1)}) custom-call(s32[4]{0:T(128)S(1)} %pad_add_fusion.place, bf16[512,864]{1,0:T(8,128)(2,1)S(1)} %get-tuple-element.533.refs_1_.refs_0_, ...), custom_call_target="tpu_custom_call", output_to_operand_aliasing={{3}: (11, {})} | custom-call | flops 1 | bytes 1 | tf_op jit(solution)/shard_map/pallas_call | solution.py:85
  229.5 3.5 %collective-permute-done.66.refs_1_ = f32[14,1152]{1,0:T(8,128)S(1)} collective-permute-done((f32[14,1152]{1,0:T(8,128)S(1)}, f32[14,1152]{1,0:T(8,128)S(1)}, u32[]{:S(2)}, u32[]{:S(2)}) %collective-permute-start.66) | collective-permute-done | bytes 64544 | tf_op jit(solution)/shard_map/ppermute | solution.py:151
  239.9 7.5 %collective-permute-done.70.refs_1_ = bf16[144,1152]{1,0:T(8,128)(2,1)S(1)} collective-permute-done((bf16[144,1152]{1,0:T(8,128)(2,1)S(1)}, bf16[144,1152]{1,0:T(8,128)(2,1)S(1)}, u32[]{:S(2)}, u32[]{:S(2)}) %collective-permute-start.70) | collective-permute-done | bytes 331808 | tf_op jit(solution)/shard_map/ppermute | solution.py:157
  247.9 5.7 %collective-permute-done.71.refs_1_ = bf16[144,1152]{1,0:T(8,128)(2,1)S(1)} collective-permute-done((bf16[144,1152]{1,0:T(8,128)(2,1)S(1)}, bf16[144,1152]{1,0:T(8,128)(2,1)S(1)}, u32[]{:S(2)}, u32[]{:S(2)}) %collective-permute-start.71) | collective-permute-done | bytes 331808 | tf_op jit(solution)/shard_map/ppermute | solution.py:157
  259.6 8.9 %collective-permute-done.72.refs_1_ = bf16[32,1152]{1,0:T(8,128)(2,1)S(1)} collective-permute-done((bf16[32,1152]{1,0:T(8,128)(2,1)S(1)}, bf16[32,1152]{1,0:T(8,128)(2,1)S(1)}, u32[]{:S(2)}, u32[]{:S(2)}) %collective-permute-start.72) | collective-permute-done | bytes 73760 | tf_op jit(solution)/shard_map/ppermute | solution.py:157
  278.6 6.8 %collective-permute-done.78.refs_2_ = bf16[4,32,1152]{2,1,0:T(8,128)(2,1)S(1)} collective-permute-done((bf16[4,32,1152]{2,1,0:T(8,128)(2,1)S(1)}, bf16[4,32,1152]{2,1,0:T(8,128)(2,1)S(1)}, u32[]{:S(2)}, u32[]{:S(2)}) %collective-permute-start.78) | collective-permute-done | bytes 294944 | tf_op jit(solution)/shard_map/ppermute | solution.py:154
  288.2 3.4 %collective-permute-start.81 = (f32[16,144]{1,0:T(8,128)S(1)}, f32[16,144]{1,0:T(8,128)S(1)}, u32[]{:S(2)}, u32[]{:S(2)}) collective-permute-start(f32[16,144]{1,0:T(8,128)S(1)} %get-tuple-element.646.refs_0_), channel_id=1, source_target_pairs={{0,16},{4,20},{8,24},{12,28},{16,0},{20,4},{24,8},{28,12},{1,17},{... | collective-permute-start | bytes 27656 | tf_op jit(solution)/shard_map/ppermute | solution.py:157
  298.7 4.9 %collective-permute-done.85.refs_1_ = bf16[144,1152]{1,0:T(8,128)(2,1)S(1)} collective-permute-done((bf16[144,1152]{1,0:T(8,128)(2,1)S(1)}, bf16[144,1152]{1,0:T(8,128)(2,1)S(1)}, u32[]{:S(2)}, u32[]{:S(2)}) %collective-permute-start.85) | collective-permute-done | bytes 331808 | tf_op jit(solution)/shard_map/ppermute | solution.py:157
  311.0 5.3 %collective-permute-done.90.refs_1_ = bf16[144,1152]{1,0:T(8,128)(2,1)S(1)} collective-permute-done((bf16[144,1152]{1,0:T(8,128)(2,1)S(1)}, bf16[144,1152]{1,0:T(8,128)(2,1)S(1)}, u32[]{:S(2)}, u32[]{:S(2)}) %collective-permute-start.90) | collective-permute-done | bytes 331808 | tf_op jit(solution)/shard_map/ppermute | solution.py:157
  (262 shorter events, 156.0 us)
Async XLA Ops:
  8.2 16.4 %collective-permute-start = (bf16[160,1440]{1,0:T(8,128)(2,1)S(1)}, bf16[160,1440]{1,0:T(8,128)(2,1)S(1)}, u32[]{:S(2)}, u32[]{:S(2)}) collective-permute-start(bf16[160,1440]{1,0:T(8,128)(2,1)S(1)} %get-tuple-element.362.refs_0_), channel_id=1, source_target_pairs={{0,8},{4,12},{8,16},{12,20},{16,24},{20,28},{24,0},{28,4},{1,9},{5... | collective-permute-start | bytes 1382408 | tf_op jit(solution)/shard_map/ppermute | solution.py:157
  11.3 13.3 %collective-permute-start.1 = (bf16[160,1440]{1,0:T(8,128)(2,1)S(1)}, bf16[160,1440]{1,0:T(8,128)(2,1)S(1)}, u32[]{:S(2)}, u32[]{:S(2)}) collective-permute-start(bf16[160,1440]{1,0:T(8,128)(2,1)S(1)} %get-tuple-element.362.refs_0_), channel_id=1, source_target_pairs={{0,4},{4,0},{8,12},{12,8},{16,20},{20,16},{24,28},{28,24},{1,5},{5... | collective-permute-start | bytes 1382408 | tf_op jit(solution)/shard_map/ppermute | solution.py:154
  24.6 14.2 %collective-permute-start.6 = (bf16[160,1440]{1,0:T(8,128)(2,1)S(1)}, bf16[160,1440]{1,0:T(8,128)(2,1)S(1)}, u32[]{:S(2)}, u32[]{:S(2)}) collective-permute-start(bf16[160,1440]{1,0:T(8,128)(2,1)S(1)} %collective-permute-done.refs_1_), channel_id=1, source_target_pairs={{0,8},{4,12},{8,16},{12,20},{16,24},{20,28},{24,0},{28,4},{1,9},{5... | collective-permute-start | bytes 1382408 | tf_op jit(solution)/shard_map/ppermute | solution.py:157
  25.6 13.2 %collective-permute-start.7 = (bf16[160,1440]{1,0:T(8,128)(2,1)S(1)}, bf16[160,1440]{1,0:T(8,128)(2,1)S(1)}, u32[]{:S(2)}, u32[]{:S(2)}) collective-permute-start(bf16[160,1440]{1,0:T(8,128)(2,1)S(1)} %collective-permute-done.refs_1_), channel_id=1, source_target_pairs={{0,4},{4,0},{8,12},{12,8},{16,20},{20,16},{24,28},{28,24},{1,5},{5... | collective-permute-start | bytes 1382408 | tf_op jit(solution)/shard_map/ppermute | solution.py:154
  38.8 13.4 %collective-permute-start.12 = (bf16[160,1440]{1,0:T(8,128)(2,1)S(1)}, bf16[160,1440]{1,0:T(8,128)(2,1)S(1)}, u32[]{:S(2)}, u32[]{:S(2)}) collective-permute-start(bf16[160,1440]{1,0:T(8,128)(2,1)S(1)} %collective-permute-done.6.refs_3_), channel_id=1, source_target_pairs={{0,8},{4,12},{8,16},{12,20},{16,24},{20,28},{24,0},{28,4},{1,9},{5... | collective-permute-start | bytes 1382408 | tf_op jit(solution)/shard_map/ppermute | solution.py:157
  53.8 29.4 %collective-permute-start.23 = (bf16[144,2304]{1,0:T(8,128)(2,1)S(1)}, bf16[144,2304]{1,0:T(8,128)(2,1)S(1)}, u32[]{:S(2)}, u32[]{:S(2)}) collective-permute-start(bf16[144,2304]{1,0:T(8,128)(2,1)S(1)} %get-tuple-element.416.refs_0_), channel_id=1, source_target_pairs={{0,8},{4,12},{8,16},{12,20},{16,24},{20,28},{24,0},{28,4},{1,9},{5... | collective-permute-start | bytes 1990664 | tf_op jit(solution)/shard_map/ppermute | solution.py:157
  64.2 19.0 %collective-permute-start.24 = (bf16[144,2304]{1,0:T(8,128)(2,1)S(1)}, bf16[144,2304]{1,0:T(8,128)(2,1)S(1)}, u32[]{:S(2)}, u32[]{:S(2)}) collective-permute-start(bf16[144,2304]{1,0:T(8,128)(2,1)S(1)} %get-tuple-element.416.refs_0_), channel_id=1, source_target_pairs={{0,4},{4,0},{8,12},{12,8},{16,20},{20,16},{24,28},{28,24},{1,5},{5... | collective-permute-start | bytes 1990664 | tf_op jit(solution)/shard_map/ppermute | solution.py:154
  67.4 16.8 %collective-permute-start.25 = (bf16[160,1440]{1,0:T(8,128)(2,1)S(1)}, bf16[160,1440]{1,0:T(8,128)(2,1)S(1)}, u32[]{:S(2)}, u32[]{:S(2)}) collective-permute-start(bf16[160,1440]{1,0:T(8,128)(2,1)S(1)} %collective-permute-done.16.refs_7_), channel_id=1, source_target_pairs={{0,1},{1,0},{2,3},{3,2},{4,5},{5,4},{6,7},{7,6},{8,9},{9,8},{10,11... | collective-permute-start | bytes 1382408 | tf_op jit(solution)/shard_map/ppermute | solution.py:148
  83.2 15.6 %collective-permute-start.27 = (bf16[144,2304]{1,0:T(8,128)(2,1)S(1)}, bf16[144,2304]{1,0:T(8,128)(2,1)S(1)}, u32[]{:S(2)}, u32[]{:S(2)}) collective-permute-start(bf16[144,2304]{1,0:T(8,128)(2,1)S(1)} %collective-permute-done.23.refs_1_), channel_id=1, source_target_pairs={{0,8},{4,12},{8,16},{12,20},{16,24},{20,28},{24,0},{28,4},{1,9},{5... | collective-permute-start | bytes 1990664 | tf_op jit(solution)/shard_map/ppermute | solution.py:157
  83.4 15.4 %collective-permute-start.28 = (bf16[144,2304]{1,0:T(8,128)(2,1)S(1)}, bf16[144,2304]{1,0:T(8,128)(2,1)S(1)}, u32[]{:S(2)}, u32[]{:S(2)}) collective-permute-start(bf16[144,2304]{1,0:T(8,128)(2,1)S(1)} %collective-permute-done.23.refs_1_), channel_id=1, source_target_pairs={{0,4},{4,0},{8,12},{12,8},{16,20},{20,16},{24,28},{28,24},{1,5},{5... | collective-permute-start | bytes 1990664 | tf_op jit(solution)/shard_map/ppermute | solution.py:154
  98.8 14.6 %collective-permute-start.31 = (bf16[144,2304]{1,0:T(8,128)(2,1)S(1)}, bf16[144,2304]{1,0:T(8,128)(2,1)S(1)}, u32[]{:S(2)}, u32[]{:S(2)}) collective-permute-start(bf16[144,2304]{1,0:T(8,128)(2,1)S(1)} %collective-permute-done.27.refs_3_), channel_id=1, source_target_pairs={{0,8},{4,12},{8,16},{12,20},{16,24},{20,28},{24,0},{28,4},{1,9},{5... | collective-permute-start | bytes 1990664 | tf_op jit(solution)/shard_map/ppermute | solution.py:157
  98.8 14.6 %collective-permute-start.32 = (bf16[144,2304]{1,0:T(8,128)(2,1)S(1)}, bf16[144,2304]{1,0:T(8,128)(2,1)S(1)}, u32[]{:S(2)}, u32[]{:S(2)}) collective-permute-start(bf16[144,2304]{1,0:T(8,128)(2,1)S(1)} %collective-permute-done.27.refs_3_), channel_id=1, source_target_pairs={{0,4},{4,0},{8,12},{12,8},{16,20},{20,16},{24,28},{28,24},{1,5},{5... | collective-permute-start | bytes 1990664 | tf_op jit(solution)/shard_map/ppermute | solution.py:154
  113.4 13.0 %collective-permute-start.33 = (bf16[144,2304]{1,0:T(8,128)(2,1)S(1)}, bf16[144,2304]{1,0:T(8,128)(2,1)S(1)}, u32[]{:S(2)}, u32[]{:S(2)}) collective-permute-start(bf16[144,2304]{1,0:T(8,128)(2,1)S(1)} %collective-permute-done.31.refs_5_), channel_id=1, source_target_pairs={{0,4},{4,0},{8,12},{12,8},{16,20},{20,16},{24,28},{28,24},{1,5},{5... | collective-permute-start | bytes 1990664 | tf_op jit(solution)/shard_map/ppermute | solution.py:154
  127.4 13.2 %collective-permute-start.35 = (bf16[8,144,1152]{2,1,0:T(8,128)(2,1)S(1)}, bf16[8,144,1152]{2,1,0:T(8,128)(2,1)S(1)}, u32[]{:S(2)}, u32[]{:S(2)}) collective-permute-start(bf16[8,144,1152]{2,1,0:T(8,128)(2,1)S(1)} %get-tuple-element.460), channel_id=1, source_target_pairs={{0,1},{1,0},{2,3},{3,2},{4,5},{5,4},{6,7},{7,6},{8,9},{9,8},{10,11... | collective-permute-start | bytes 7962632 | tf_op jit(solution)/shard_map/ppermute | solution.py:148
  153.6 28.0 %collective-permute-start.52 = (bf16[512,1152]{1,0:T(8,128)(2,1)S(1)}, bf16[512,1152]{1,0:T(8,128)(2,1)S(1)}, u32[]{:S(2)}, u32[]{:S(2)}) collective-permute-start(bf16[512,1152]{1,0:T(8,128)(2,1)S(1)} %get-tuple-element.519.refs_0_), channel_id=1, source_target_pairs={{0,2},{1,3},{2,0},{3,1},{4,6},{5,7},{6,4},{7,5},{8,10},{9,11},{10,... | collective-permute-start | bytes 3538952 | tf_op jit(solution)/shard_map/ppermute | solution.py:151
  165.2 28.3 %collective-permute-start.53 = (bf16[2,144,1152]{2,1,0:T(8,128)(2,1)}, bf16[2,144,1152]{2,1,0:T(8,128)(2,1)S(1)}, u32[]{:S(2)}, u32[]{:S(2)}) collective-permute-start(bf16[2,144,1152]{2,1,0:T(8,128)(2,1)} %get-tuple-element.536), channel_id=1, source_target_pairs={{0,4},{4,0},{8,12},{12,8},{16,20},{20,16},{24,28},{28,24},{1,5},{5... | collective-permute-start | bytes 1990664 | tf_op jit(solution)/shard_map/ppermute | solution.py:154
  166.3 31.1 %collective-permute-start.54 = (bf16[2,144,1152]{2,1,0:T(8,128)(2,1)}, bf16[2,144,1152]{2,1,0:T(8,128)(2,1)S(1)}, u32[]{:S(2)}, u32[]{:S(2)}) collective-permute-start(bf16[2,144,1152]{2,1,0:T(8,128)(2,1)} %get-tuple-element.539), channel_id=1, source_target_pairs={{0,4},{4,0},{8,12},{12,8},{16,20},{20,16},{24,28},{28,24},{1,5},{5... | collective-permute-start | bytes 1990664 | tf_op jit(solution)/shard_map/ppermute | solution.py:154
  171.2 54.6 %collective-permute-start.65 = (bf16[4,144,1152]{2,1,0:T(8,128)(2,1)}, bf16[4,144,1152]{2,1,0:T(8,128)(2,1)S(1)}, u32[]{:S(2)}, u32[]{:S(2)}) collective-permute-start(bf16[4,144,1152]{2,1,0:T(8,128)(2,1)} %get-tuple-element.586), channel_id=1, source_target_pairs={{0,4},{4,0},{8,12},{12,8},{16,20},{20,16},{24,28},{28,24},{1,5},{5... | collective-permute-start | bytes 3981320 | tf_op jit(solution)/shard_map/ppermute | solution.py:154
  199.5 15.4 %collective-permute-start.63 = (bf16[256,1152]{1,0:T(8,128)(2,1)S(1)}, bf16[256,1152]{1,0:T(8,128)(2,1)S(1)}, u32[]{:S(2)}, u32[]{:S(2)}) collective-permute-start(bf16[256,1152]{1,0:T(8,128)(2,1)S(1)} %get-tuple-element.563), channel_id=1, source_target_pairs={{0,2},{1,3},{2,0},{3,1},{4,6},{5,7},{6,4},{7,5},{8,10},{9,11},{10,... | collective-permute-start | bytes 1769480 | tf_op jit(solution)/shard_map/ppermute | solution.py:151
  207.6 12.9 %collective-permute-start.64 = (bf16[144,1152]{1,0:T(8,128)(2,1)S(1)}, bf16[144,1152]{1,0:T(8,128)(2,1)S(1)}, u32[]{:S(2)}, u32[]{:S(2)}) collective-permute-start(bf16[144,1152]{1,0:T(8,128)(2,1)S(1)} %get-tuple-element.581), channel_id=1, source_target_pairs={{0,8},{4,12},{8,16},{12,20},{16,24},{20,28},{24,0},{28,4},{1,9},{5... | collective-permute-start | bytes 995336 | tf_op jit(solution)/shard_map/ppermute | solution.py:157
  213.4 60.6 %collective-permute-start.76 = (bf16[4,144,1152]{2,1,0:T(8,128)(2,1)S(1)}, bf16[4,144,1152]{2,1,0:T(8,128)(2,1)S(1)}, u32[]{:S(2)}, u32[]{:S(2)}) collective-permute-start(bf16[4,144,1152]{2,1,0:T(8,128)(2,1)S(1)} %get-tuple-element.633), channel_id=1, source_target_pairs={{0,4},{4,0},{8,12},{12,8},{16,20},{20,16},{24,28},{28,24},{1,5},{5... | collective-permute-start | bytes 3981320 | tf_op jit(solution)/shard_map/ppermute | solution.py:154
  221.2 12.4 %collective-permute-start.67 = (bf16[144,1152]{1,0:T(8,128)(2,1)S(1)}, bf16[144,1152]{1,0:T(8,128)(2,1)S(1)}, u32[]{:S(2)}, u32[]{:S(2)}) collective-permute-start(bf16[144,1152]{1,0:T(8,128)(2,1)S(1)} %get-tuple-element.597), channel_id=1, source_target_pairs={{0,8},{4,12},{8,16},{12,20},{16,24},{20,28},{24,0},{28,4},{1,9},{5... | collective-permute-start | bytes 995336 | tf_op jit(solution)/shard_map/ppermute | solution.py:157
  234.9 12.4 %collective-permute-start.70 = (bf16[144,1152]{1,0:T(8,128)(2,1)S(1)}, bf16[144,1152]{1,0:T(8,128)(2,1)S(1)}, u32[]{:S(2)}, u32[]{:S(2)}) collective-permute-start(bf16[144,1152]{1,0:T(8,128)(2,1)S(1)} %get-tuple-element.609), channel_id=1, source_target_pairs={{0,8},{4,12},{8,16},{12,20},{16,24},{20,28},{24,0},{28,4},{1,9},{5... | collective-permute-start | bytes 995336 | tf_op jit(solution)/shard_map/ppermute | solution.py:157
  239.8 13.8 %collective-permute-start.71 = (bf16[144,1152]{1,0:T(8,128)(2,1)S(1)}, bf16[144,1152]{1,0:T(8,128)(2,1)S(1)}, u32[]{:S(2)}, u32[]{:S(2)}) collective-permute-start(bf16[144,1152]{1,0:T(8,128)(2,1)S(1)} %get-tuple-element.615), channel_id=1, source_target_pairs={{0,8},{4,12},{8,16},{12,20},{16,24},{20,28},{24,0},{28,4},{1,9},{5... | collective-permute-start | bytes 995336 | tf_op jit(solution)/shard_map/ppermute | solution.py:157
  254.3 19.1 %collective-permute-start.75 = (bf16[144,1152]{1,0:T(8,128)(2,1)S(1)}, bf16[144,1152]{1,0:T(8,128)(2,1)S(1)}, u32[]{:S(2)}, u32[]{:S(2)}) collective-permute-start(bf16[144,1152]{1,0:T(8,128)(2,1)S(1)} %get-tuple-element.624), channel_id=1, source_target_pairs={{0,8},{4,12},{8,16},{12,20},{16,24},{20,28},{24,0},{28,4},{1,9},{5... | collective-permute-start | bytes 995336 | tf_op jit(solution)/shard_map/ppermute | solution.py:157
  254.5 22.9 %collective-permute-start.77 = (bf16[256,1152]{1,0:T(8,128)(2,1)S(1)}, bf16[256,1152]{1,0:T(8,128)(2,1)S(1)}, u32[]{:S(2)}, u32[]{:S(2)}) collective-permute-start(bf16[256,1152]{1,0:T(8,128)(2,1)S(1)} %get-tuple-element.639), channel_id=1, source_target_pairs={{0,2},{1,3},{2,0},{3,1},{4,6},{5,7},{6,4},{7,5},{8,10},{9,11},{10,... | collective-permute-start | bytes 1769480 | tf_op jit(solution)/shard_map/ppermute | solution.py:151
  255.3 13.1 %collective-permute-start.72 = (bf16[32,1152]{1,0:T(8,128)(2,1)S(1)}, bf16[32,1152]{1,0:T(8,128)(2,1)S(1)}, u32[]{:S(2)}, u32[]{:S(2)}) collective-permute-start(bf16[32,1152]{1,0:T(8,128)(2,1)S(1)} %get-tuple-element.603.refs_0_), channel_id=1, source_target_pairs={{0,8},{4,12},{8,16},{12,20},{16,24},{20,28},{24,0},{28,4},{1,9},{5... | collective-permute-start | bytes 221192 | tf_op jit(solution)/shard_map/ppermute | solution.py:157
  256.4 13.5 %collective-permute-start.73 = (bf16[32,1152]{1,0:T(8,128)(2,1)S(1)}, bf16[32,1152]{1,0:T(8,128)(2,1)S(1)}, u32[]{:S(2)}, u32[]{:S(2)}) collective-permute-start(bf16[32,1152]{1,0:T(8,128)(2,1)S(1)} %get-tuple-element.603.refs_0_), channel_id=1, source_target_pairs={{0,16},{4,20},{8,24},{12,28},{16,0},{20,4},{24,8},{28,12},{1,17},{... | collective-permute-start | bytes 221192 | tf_op jit(solution)/shard_map/ppermute | solution.py:157
  275.5 16.2 %collective-permute-start.79 = (bf16[144,1152]{1,0:T(8,128)(2,1)S(1)}, bf16[144,1152]{1,0:T(8,128)(2,1)S(1)}, u32[]{:S(2)}, u32[]{:S(2)}) collective-permute-start(bf16[144,1152]{1,0:T(8,128)(2,1)S(1)} %get-tuple-element.648), channel_id=1, source_target_pairs={{0,8},{4,12},{8,16},{12,20},{16,24},{20,28},{24,0},{28,4},{1,9},{5... | collective-permute-start | bytes 995336 | tf_op jit(solution)/shard_map/ppermute | solution.py:157
  275.5 20.4 %collective-permute-start.83 = (bf16[144,1152]{1,0:T(8,128)(2,1)S(1)}, bf16[144,1152]{1,0:T(8,128)(2,1)S(1)}, u32[]{:S(2)}, u32[]{:S(2)}) collective-permute-start(bf16[144,1152]{1,0:T(8,128)(2,1)S(1)} %get-tuple-element.628.refs_0_), channel_id=1, source_target_pairs={{0,2},{1,3},{2,0},{3,1},{4,6},{5,7},{6,4},{7,5},{8,10},{9,11},{10,... | collective-permute-start | bytes 995336 | tf_op jit(solution)/shard_map/ppermute | solution.py:151
  276.0 19.9 %collective-permute-start.84 = (bf16[144,1152]{1,0:T(8,128)(2,1)S(1)}, bf16[144,1152]{1,0:T(8,128)(2,1)S(1)}, u32[]{:S(2)}, u32[]{:S(2)}) collective-permute-start(bf16[144,1152]{1,0:T(8,128)(2,1)S(1)} %get-tuple-element.628.refs_0_), channel_id=1, source_target_pairs={{0,1},{1,0},{2,3},{3,2},{4,5},{5,4},{6,7},{7,6},{8,9},{9,8},{10,11... | collective-permute-start | bytes 995336 | tf_op jit(solution)/shard_map/ppermute | solution.py:148
  303.6 18.2 %collective-permute-start.93 = (f32[128,1152]{1,0:T(8,128)S(1)}, f32[128,1152]{1,0:T(8,128)S(1)}, u32[]{:S(2)}, u32[]{:S(2)}) collective-permute-start(f32[128,1152]{1,0:T(8,128)S(1)} %get-tuple-element.687), channel_id=1, source_target_pairs={{0,1},{1,0},{2,3},{3,2},{4,5},{5,4},{6,7},{7,6},{8,9},{9,8},{10,11... | collective-permute-start | bytes 1769480 | tf_op jit(solution)/shard_map/ppermute | solution.py:148
  (82 other events, 603.4 us)

commit v2 on v1

--- a/solution.py
+++ b/solution.py
@@ -96,42 +96,6 @@
         self.token = results[-1]
         return results[:-1] if count > 1 else results[0]
 
-    def pass_on(self, blocks, step, sums):
-        lines, rows, columns = blocks[0].shape
-        count = len(blocks)
-
-        def kernel(place, *refs):
-            outs = refs[-1 - count : -1]
-            for index in range(count):
-                result = refs[index][0]
-                if sums:
-                    result = wide(result) + wide(refs[count + index][...])
-                outs[index][...] = result.astype(outs[index].dtype)
-
-        def block_at(unused, place):
-            return (lax.rem(place[LINE] + (lines - step), lines), 0, 0)
-
-        piece = pl.BlockSpec((rows, columns), lambda unused, place: (0, 0))
-        spec = pltpu.PrefetchScalarGridSpec(
-            num_scalar_prefetch=1,
-            grid=(1,),
-            in_specs=[pl.BlockSpec((1, rows, columns), block_at)] * count
-            + [piece] * len(sums)
-            + [ANY],
-            out_specs=(piece,) * count + (ANY,),
-        )
-        results = pl.pallas_call(
-            kernel,
-            grid_spec=spec,
-            out_shape=tuple(struct((rows, columns), block.dtype) for block in blocks)
-            + (struct(self.token.shape, self.token.dtype),),
-            input_output_aliases={1 + count + len(sums): count},
-            compiler_params=ROOM,
-            cost_estimate=SHORT,
-        )(self.place, *blocks, *sums, self.token)
-        self.token = results[-1]
-        return results[:-1]
-
 
 class Place:
     def __init__(self):
@@ -276,42 +240,35 @@
 
 
 class Scatter:
-    def __init__(self, here, order, *blocks):
-        self.here, self.order, self.mine = here, order, blocks[-1]
-        self.got = [here.to_pair(give) for give in blocks[:-1]]
-        self.step = 0
-
-    def join(self):
-        got = [self.order.wait(part) for part in self.got]
-        share = self.mine.shape[0] // len(got)
-
-        def kernel(place, mine_ref, *refs):
-            for index in range(len(got)):
-                span = slice(index * share, (index + 1) * share)
-                refs[-1][span] = low(wide(mine_ref[span]) + wide(refs[index][...]))
-
-        shape = struct(self.mine.shape, jnp.bfloat16)
-        self.kept = [self.order.run(kernel, [shape], self.mine, *got)]
-        self.sums = []
-        self.send()
-
-    def send(self):
+    def __init__(self, here, order, blocks):
+        count = here.line_size
+        self.here, self.order, self.step = here, order, 0
+        self.give, self.mine = blocks[:count], blocks[count:]
+        self.under_way = [here.to_pair(self.give[1 % count])]
+
+    def turn(self):
+        here, count = self.here, self.here.line_size
+        arrived = self.order.wait(*self.under_way)
+        arrived = list(arrived) if len(self.under_way) > 1 else [arrived]
         self.step += 1
-        sums = self.order.pass_on(self.kept, self.step, self.sums)
-        if self.step < self.here.line_size:
-            sums = [self.here.to_line(total) for total in sums]
-        self.sums = sums
-
-    def turn(self):
-        if self.step < self.here.line_size:
-            sums = self.order.wait(*self.sums)
-            self.sums = list(sums) if len(self.kept) > 1 else [sums]
-            self.send()
+        own = self.mine[self.step % count]
+
+        def kernel(place, *refs):
+            total = wide(refs[0][...])
+            for ref in refs[1:-1]:
+                total = total + wide(ref[...])
+            refs[-1][...] = low(total)
+
+        total = self.order.run(kernel, [struct(own.shape, jnp.bfloat16)], own, *arrived)
+        if self.step < count:
+            back = (self.step + 1) % count
+            self.under_way = [here.to_line(total), here.to_pair(self.give[back])]
+        return total
 
     def finish(self):
         while self.step < self.here.line_size:
-            self.turn()
-        return self.sums[0]
+            total = self.turn()
+        return total
 
 
 def cut_columns(place, source, target, offset, index, parts, groups):
@@ -486,57 +443,52 @@
 
 
 def add_sums(order, sums, far):
-    def kernel(place, sums_ref, far_ref, out):
-        out[...] = sums_ref[...] + far_ref[...]
-
-    return order.run(kernel, [struct(sums.shape, sums.dtype)], sums, far)
-
-
-def join_sums(order, sums, near):
     rows, width = sums.shape
 
-    def kernel(place, sums_ref, near_ref, out, held):
+    def kernel(place, sums_ref, far_ref, out, held):
         held[...] = jnp.zeros(held.shape, jnp.float32)
-        for own in range(2):
-
-            @pl.when(place[CORE] == own)
-            def _():
-                held[6 * own : 6 * own + 6, :] = sums_ref[:6, :]
-                held[6 - 6 * own : 12 - 6 * own, :] = near_ref[:6, :]
-
-        held[12 : 6 + rows, :] = sums_ref[6:, :] + near_ref[6:, :]
+        held[:rows, :] = sums_ref[...] + far_ref[...]
         out[...] = low(held[...])
 
-    total = 2 * HEAD
     return order.run(
         kernel,
-        [struct((total, width), jnp.bfloat16)],
+        [struct((HEAD, width), jnp.bfloat16)],
         sums,
-        near,
-        scratch=(pltpu.VMEM((total, width), jnp.float32),),
-    )
-
-
-def modulation_back(order, mine, near, mod_weight, hidden):
+        far,
+        scratch=(pltpu.VMEM((HEAD, width), jnp.float32),),
+    )
+
+
+def modulation_back(order, mine, near, mine_far, near_far, mod_weight, hidden):
     lines, _, width = mine.shape
     shards = 2 * lines
     rows, columns = mod_weight.shape
     sizes = (2 * width // shards, width // shards, hidden // shards, width // shards)
 
-    def kernel(place, weight_ref, mine_ref, near_ref, *refs):
+    def kernel(place, weight_ref, mine_ref, near_ref, mine_far_ref, near_far_ref, *refs):
         mod_all, biases, (products, held, total) = refs[0], refs[1:5], refs[5:]
         shard = 2 * place[LINE] + place[PAIR]
         total[...] = jnp.zeros(total.shape, jnp.float32)
-        for index in range(shards):
-            source = wide((near_ref if index % 2 else mine_ref)[index // 2])
-            line = lax.rem(place[LINE] + (lines - index // 2), lines)
-            owner = 2 * line + (1 - place[PAIR] if index % 2 else place[PAIR])
-            for latent in range(2):
+        sources = (
+            (mine_ref, place[PAIR], place[CORE]),
+            (near_ref, 1 - place[PAIR], place[CORE]),
+            (mine_far_ref, place[PAIR], 1 - place[CORE]),
+            (near_far_ref, 1 - place[PAIR], 1 - place[CORE]),
+        )
+        for back in range(lines):
+            line = lax.rem(place[LINE] + (lines - back), lines)
+            for source_ref, pair, core in sources:
+                source = wide(source_ref[back])
+                goal = 2 * (2 * line + pair) + core
                 for row in range(6):
-                    held[pl.ds(2 * owner + latent, 1), row * width : (row + 1) * width] = source[
-                        6 * latent + row : 6 * latent + row + 1, :
-                    ]
-            total[...] += source[12 : 12 + total.shape[0], :]
+                    span = slice(row * width, (row + 1) * width)
+                    held[pl.ds(goal, 1), span] = source[row : row + 1, :]
+        for core in range(2):
+            for back in range(lines):
+                for source_ref in (mine_ref, near_ref, mine_far_ref, near_far_ref)[
+                    2 * core : 2 * core + 2
+                ]:
+                    total[...] += wide(source_ref[back])[6 : 6 + total.shape[0], :]
         for index in range(shards):
 
             @pl.when(shard == index)
@@ -556,7 +508,9 @@
         pltpu.VMEM((2 * shards, columns), jnp.float32),
         pltpu.VMEM((sum(sizes) * shards // width, width), jnp.float32),
     )
-    return order.run(kernel, outs, mod_weight, mine, near, scratch=scratch)
+    return order.run(
+        kernel, outs, mod_weight, mine, near, mine_far, near_far, scratch=scratch
+    )
 
 
 def condition_back(order, mine, near, condition):
@@ -971,69 +925,58 @@
             target[...] = source[:, index * columns : (index + 1) * columns]
 
 
-def split_pairs(place, total, shards, met_refs, start, write):
+def add_met(total, shards, met_refs, held, start):
     piece = total.shape[0] // shards
     share = shards // len(met_refs)
     span = slice(start, start + total.shape[1])
-    for own in range(2):
-
-        @pl.when(place[PAIR] == own)
-        def _():
-            for shard in range(shards):
-                part = total[shard * piece : (shard + 1) * piece]
-                met = met_refs[shard // share][shard % share, :, span]
-                write(shard // 2, shard % 2 == own, low(part + wide(met)))
-
-
-def weight_sum(order, shards, left_side, right_side, met, parts=1):
+    for shard in range(shards):
+        part = total[shard * piece : (shard + 1) * piece]
+        met = met_refs[shard // share][shard % share, :, span]
+        held[shard, :, span] = low(part + wide(met))
+
+
+def give_blocks(place, shards, held, outs):
+    lines = shards // 2
+    for back in range(lines):
+        line = lax.rem(place[LINE] + (lines - back), lines)
+        outs[back][...] = held[2 * line + 1 - place[PAIR]]
+        outs[lines + back][...] = held[2 * line + place[PAIR]]
+
+
+def weight_sum(order, shards, left_side, right_side, met):
     rows, columns = left_side.shape[1], right_side.shape[1]
-    lines = shards // 2
-    share = lines // parts
+    piece = rows // shards
 
     def kernel(place, left_ref, right_ref, *refs):
-        met_refs, outs = refs[: len(met)], refs[len(met) :]
-
-        def write(line, own, part):
-            if own:
-                outs[parts][line] = part
-            else:
-                outs[line // share][line % share] = part
-
+        met_refs, outs, held = refs[: len(met)], refs[len(met) : -1], refs[-1]
         total = dot(left_ref[...], right_ref[...], 0, 0)
-        split_pairs(place, total, shards, met_refs, 0, write)
-
-    outs = [struct((share, rows // shards, columns), jnp.bfloat16)] * parts
-    outs.append(struct((lines, rows // shards, columns), jnp.bfloat16))
-    return order.run(kernel, outs, left_side, right_side, *met)
+        add_met(total, shards, met_refs, held, 0)
+        give_blocks(place, shards, held, outs)
+
+    outs = [struct((piece, columns), jnp.bfloat16)] * shards
+    scratch = (pltpu.VMEM((shards, piece, columns), jnp.bfloat16),)
+    return order.run(kernel, outs, left_side, right_side, *met, scratch=scratch)
 
 
 def attention_sum(order, shards, attn_turned, qkv_grad, heads_out, grad_attn, met):
     rows = attn_turned.shape[0]
+    piece = rows // shards
     columns, part = qkv_grad.shape[1], grad_attn.shape[1] // 4
 
     def kernel(place, turned_ref, qkv_ref, heads_ref, grad_ref, *refs):
-        met_refs, (give, mine, held) = refs[: len(met)], refs[len(met) :]
-        take_quarter(place, grad_ref, held, 0)
-        for left, right, start in ((turned_ref, qkv_ref, 0), (heads_ref, held, columns)):
-            total = dot(left[...], right[...], 1, 0)
-            span = slice(start, start + total.shape[1])
-
-            def write(line, own, block, span=span):
-                target = mine if own else give
-                target[line, :, span] = block
-
-            split_pairs(place, total, shards, met_refs, start, write)
-
-    outs = (struct((shards // 2, rows // shards, columns + part), jnp.bfloat16),) * 2
+        met_refs, outs, (quarter, held) = refs[: len(met)], refs[len(met) : -2], refs[-2:]
+        take_quarter(place, grad_ref, quarter, 0)
+        for left, right, start in ((turned_ref, qkv_ref, 0), (heads_ref, quarter, columns)):
+            add_met(dot(left[...], right[...], 1, 0), shards, met_refs, held, start)
+        give_blocks(place, shards, held, outs)
+
+    outs = [struct((piece, columns + part), jnp.bfloat16)] * shards
+    scratch = (
+        pltpu.VMEM((grad_attn.shape[0], part), grad_attn.dtype),
+        pltpu.VMEM((shards, piece, columns + part), jnp.bfloat16),
+    )
     return order.run(
-        kernel,
-        outs,
-        attn_turned,
-        qkv_grad,
-        heads_out,
-        grad_attn,
-        *met,
-        scratch=(pltpu.VMEM((grad_attn.shape[0], part), grad_attn.dtype),),
+        kernel, outs, attn_turned, qkv_grad, heads_out, grad_attn, *met, scratch=scratch
     )
 
 
@@ -1278,98 +1221,99 @@
     down_met = to_core(weight_grad(order, shards, act_near, grad_mlp, 8))
     up_met = to_core(weight_grad(order, shards, mlp_in, pre_near, 8))
     down_met = wait(*down_met)
-    down_sum = Scatter(
-        here, order, *weight_sum(order, shards, act_mine, grad_mlp, down_met, parts=2)
-    )
+    down_sum = Scatter(here, order, weight_sum(order, shards, act_mine, grad_mlp, down_met))
     up_met = wait(*up_met)
-    up_sum = Scatter(here, order, *weight_sum(order, shards, mlp_in, pre_mine, up_met))
+    up_sum = Scatter(here, order, weight_sum(order, shards, mlp_in, pre_mine, up_met))
+    down_sum.turn()
     feed_own, feed_give = feed_out(order, act_mine, down_mine, act_near, down_near)
     feed_far = here.to_side(feed_give)
 
+    up_sum.turn()
     mlp_far = wait(mlp_far)
     grad_attn, grad_middle, middle_sums = middle_back(
         order, mlp_part, mlp_far, normed_two, inverses_two, cots, mod, branch
     )
+    down_sum.turn()
     qkv_grad_near, qv_sums_near = attend_back(order, 1, parts_near, out_full, grad_attn)
+    up_sum.turn()
     met = to_core(
         attention_grad(order, shards, attn_turned, qkv_grad_near, heads_out, grad_attn, 8)
     )
+    met = wait(*met)
+    down_sum.turn()
     qkv_grad_mine, qv_sums_mine = attend_back(order, 0, parts_mine, out_full, grad_attn)
-    down_sum.join()
-    met = wait(*met)
+    up_sum.turn()
     attention_total = Scatter(
         here,
         order,
-        *attention_sum(order, shards, attn_turned, qkv_grad_mine, heads_out, grad_attn, met),
-    )
+        attention_sum(order, shards, attn_turned, qkv_grad_mine, heads_out, grad_attn, met),
+    )
+    grad_down = down_sum.finish()
+    down_far, down_near = here.to_side(grad_down), here.to_core(grad_down)
     feed_far = wait(feed_far)
     mixed_mine, mixed_give, mix_sums = mix(
         order, feed_own, feed_far, down_bias, lats, branch, cots, mod
     )
+    grad_up = up_sum.finish()
+    attention_total.turn()
+    down_far, down_near = wait(down_far, down_near)
+    down_far_near = here.to_core(down_far)
+    up_far, up_near = here.to_side(grad_up), here.to_core(grad_up)
     attn_own, attn_give, attn_sums = attention_in_back(
         order, qkv_grad_mine, qkv_mine, qkv_grad_near, qkv_near, lats, means_one, inverses_one
     )
-    down_sum.turn()
-
     sums = token_sums(
         order, shards, attn_sums, middle_sums, mix_sums, down_sums, qv_sums_mine, qv_sums_near,
         up_sums_mine, up_sums_near,
     )
     sums_far = here.to_side(sums)
-    up_sum.join()
+    attention_total.turn()
     sums = add_sums(order, sums, wait(sums_far))
-    sums_near = here.to_core(sums)
-    down_sum.turn()
-    sums = join_sums(order, sums, wait(sums_near))
-    up_sum.turn()
-    grad_down = down_sum.finish()
+    up_far, up_near, down_far_near = wait(up_far, up_near, down_far_near)
     sums_ring = Lines(here, order, sums)
+    grad_down = lay_rows(order, (grad_down, down_near, down_far, down_far_near))
+    attention_total.turn()
+    sums_ring.join()
+    up_far_near = here.to_core(up_far)
     attn_far = here.to_side(wait(attn_give))
-    up_sum.turn()
-    sums_ring.join()
-    down_far, down_near = here.to_side(grad_down), here.to_core(grad_down)
-    grad_up = up_sum.finish()
-    attention_total.join()
+    up_far_near = wait(up_far_near)
+    grad_up = lay_columns(
+        order, (grad_up, up_near, up_far, up_far_near), (hidden_part, shards)
+    )
+    sums_mine, sums_near = sums_ring.finish()
+    sums_mine_far, sums_near_far = here.to_core(sums_mine), here.to_core(sums_near)
+    grad_attention = attention_total.finish()
+    attention_far = here.to_side(grad_attention)
+    attention_near = here.to_core(grad_attention)
+    sums_mine_far, sums_near_far = wait(sums_mine_far, sums_near_far)
+    mod_all, grad_qv_bias, grad_out_bias, grad_up_bias, grad_down_bias, grad_low = (
+        modulation_back(
+            order, sums_mine, sums_near, sums_mine_far, sums_near_far, mod_weight, hidden
+        )
+    )
+    low_ring = Lines(here, order, grad_low)
     attn_far = wait(attn_far)
     tokens_mine, tokens_give = tokens_back(
         order, attn_own, attn_far, lats, means_one, inverses_one, mod, grad_middle
     )
-    mod_all, grad_qv_bias, grad_out_bias, grad_up_bias, grad_down_bias, grad_low = (
-        modulation_back(order, *sums_ring.finish(), mod_weight, hidden)
-    )
-    low_ring = Lines(here, order, grad_low)
-    attention_total.turn()
+    attention_far, attention_near = wait(attention_far, attention_near)
+    attention_far_near = here.to_core(attention_far)
+    mixed_near, tokens_near = here.to_core(mixed_give), here.to_core(tokens_give)
     low_ring.join()
-    down_far, down_near = wait(down_far, down_near)
-    down_far_near = here.to_core(down_far)
-    up_far, up_near = here.to_side(grad_up), here.to_core(grad_up)
-    attention_total.turn()
-    grad_condition = condition_back(order, *low_ring.finish(), condition)
-    down_far_near = wait(down_far_near)
-    grad_down = lay_rows(order, (grad_down, down_near, down_far, down_far_near))
-    up_far, up_near = wait(up_far, up_near)
-    up_far_near = here.to_core(up_far)
-    mod_all = wait(mod_all)
-    grad_mod_weight = wait(dot(cond_rows, mod_all, 0, 0))
-    grad_attention = attention_total.finish()
-    attention_far = here.to_side(grad_attention)
-    attention_near = here.to_core(grad_attention)
-    up_far_near = wait(up_far_near)
-    grad_up = lay_columns(
-        order, (grad_up, up_near, up_far, up_far_near), (hidden_part, shards)
-    )
-    mixed_near, tokens_near = wait(here.to_core(mixed_give), here.to_core(tokens_give))
-    mixed, grad_latents = lay_tokens(
-        order, (mixed_mine, mixed_near), (tokens_mine, tokens_near)
-    )
-    attention_far, attention_near = wait(attention_far, attention_near)
-    attention_far_near = wait(here.to_core(attention_far))
+    attention_far_near = wait(attention_far_near)
     grad_qkv, grad_out = lay_columns(
         order,
         (grad_attention, attention_near, attention_far, attention_far_near),
         (3 * part, 3),
         (width // 4, 1),
     )
+    mixed_near, tokens_near = wait(mixed_near, tokens_near)
+    mixed, grad_latents = lay_tokens(
+        order, (mixed_mine, mixed_near), (tokens_mine, tokens_near)
+    )
+    grad_condition = condition_back(order, *low_ring.finish(), condition)
+    mod_all = wait(mod_all)
+    grad_mod_weight = dot(cond_rows, mod_all, 0, 0)
     span = 6 * width // shards
     mod_span = lax.dynamic_slice_in_dim(mod_all, here.shard * span, span, 1)
     grad_mod_bias = jnp.sum(wide(mod_span), axis=0)

time: 336 us -> 314 us (0.935)
  waiting for transfers between devices: 133 us -> 99.1 us
  starting transfers between devices: 67.2 us -> 82.9 us
  Pallas kernels: 116 us -> 110 us
    ppermute x24, waiting for transfers between devices: 57.4 us -> 31.6 us  [to_line(): lax.ppermute(values, 'fsdp', [(i, (i + 2 * step) % self.shards) for i in...]
    ppermute x15 -> x23, starting transfers between devices: 15.6 us -> 23.5 us  [to_pair(): lax.ppermute(values, 'fsdp', [(i, i ^ 1) for i in range(self.shards)])]
    pallas_call x12 -> x0, Pallas kernels: 7.39 us -> none  [pass_on(): pl.pallas_call(kernel, grid_spec=spec, out_shape=tuple((struct((rows, col...]
    ppermute x13, waiting for transfers between devices: 35.5 us -> 29.3 us  [to_side(): return lax.ppermute(values, 'seq', [(i, i ^ 2) for i in range(self.seats)])]
    ppermute x24, starting transfers between devices: 26.4 us -> 32 us  [to_line(): lax.ppermute(values, 'fsdp', [(i, (i + 2 * step) % self.shards) for i in...]
    pallas_call x46 -> x54, Pallas kernels: 109 us -> 110 us  [run(): pl.pallas_call(body, out_shape=tuple(outs) + (struct(self.token.shape, se...]
    ppermute x15 -> x23, waiting for transfers between devices: 35.8 us -> 35.4 us  [to_pair(): lax.ppermute(values, 'fsdp', [(i, i ^ 1) for i in range(self.shards)])]
    ppermute x45 -> x46, starting transfers between devices: 9.35 us -> 9.68 us  [to_core(): return lax.ppermute(values, 'seq', [(i, i ^ 1) for i in range(self.seats)])]
  transfers between devices with their start and end apart: 97 -> 106, of which waited for: 41 -> 37; matrix products, arithmetic and copies ran while one was open for 1% -> 2% of each run, Pallas kernels for 31% -> 31%
where the time goes in v2:
time: 314 us; the launch traced here: 309 us
  Pallas kernels  110 us (35%)
  waiting for transfers between devices  99.1 us (32%)
  starting transfers between devices  82.9 us (26%)
  local copies, waits for them, and re-layouts  9.17 us (3%)
  matrix products  3.58 us (1%)
    pallas_call x54, Pallas kernels, run(): pl.pallas_call(body, out_shape=tuple(outs) + (struct(self.token.shape, se...  110 us
    ppermute x23, waiting for transfers between devices, to_pair(): lax.ppermute(values, 'fsdp', [(i, i ^ 1) for i in range(self.shards)])  35.4 us
    ppermute x24, starting transfers between devices, to_line(): lax.ppermute(values, 'fsdp', [(i, (i + 2 * step) % self.shards) for i in...  32 us
    ppermute x24, waiting for transfers between devices, to_line(): lax.ppermute(values, 'fsdp', [(i, (i + 2 * step) % self.shards) for i in...  31.6 us
    ppermute x13, waiting for transfers between devices, to_side(): return lax.ppermute(values, 'seq', [(i, i ^ 2) for i in range(self.seats)])  29.3 us
    ppermute x23, starting transfers between devices, to_pair(): lax.ppermute(values, 'fsdp', [(i, i ^ 1) for i in range(self.shards)])  23.5 us
    ppermute x13, starting transfers between devices, to_side(): return lax.ppermute(values, 'seq', [(i, i ^ 2) for i in range(self.seats)])  17.7 us
    ppermute x46, starting transfers between devices, to_core(): return lax.ppermute(values, 'seq', [(i, i ^ 1) for i in range(self.seats)])  9.68 us
  transfers between devices with their start and end apart: 106, of which 37 were waited for; matrix products, arithmetic and copies ran while one was open for 2% of the time, Pallas kernels for 31%

profile of v2, /device:TPU:0, one launch (start us, length us, event | category | flops | bytes accessed | tf_op | source)
XLA Modules:
  0.0 309.3 jit_solution(6521993088156356132)
XLA Ops:
  0.7 3.6 %concatenate.3 = bf16[2016]{0:T(1024)(128)(2,1)S(1)} concatenate(bf16[864]{0:T(1024)(128)(2,1)} %param.16, bf16[288]{0:T(512)(128)(2,1)} %param.18, bf16[144]{0:T(256)(128)(2,1)} %param.20, bf16[576]{0:T(1024)(128)(2,1)} %param.22, bf16[144]{0:T(256)(128)(2,1)} %param.24), dimensions={0} | concatenate | bytes 8064 | tf_op jit(solution)/shard_map/concatenate | solution.py:1144
  8.2 3.1 collective-permute-start
  17.6 7.0 %collective-permute-done.refs_1_ = bf16[160,1440]{1,0:T(8,128)(2,1)S(1)} collective-permute-done((bf16[160,1440]{1,0:T(8,128)(2,1)S(1)}, bf16[160,1440]{1,0:T(8,128)(2,1)S(1)}, u32[]{:S(2)}, u32[]{:S(2)}) %collective-permute-start) | collective-permute-done | bytes 460832 | tf_op jit(solution)/shard_map/ppermute | solution.py:121
  29.1 7.5 %collective-permute-done.5.refs_5_.refs_9_.refs_6_ = bf16[128,1152]{1,0:T(8,128)(2,1)S(1)} collective-permute-done((bf16[128,1152]{1,0:T(8,128)(2,1)S(1)}, bf16[128,1152]{1,0:T(8,128)(2,1)S(1)}, u32[]{:S(2)}, u32[]{:S(2)}) %collective-permute-start.5) | collective-permute-done | bytes 294944 | tf_op jit(solution)/shard_map/ppermute | solution.py:115
  40.8 3.9 %collective-permute-done.10.refs_2_.refs_6_ = bf16[128,1152]{1,0:T(8,128)(2,1)S(1)} collective-permute-done((bf16[128,1152]{1,0:T(8,128)(2,1)S(1)}, bf16[128,1152]{1,0:T(8,128)(2,1)S(1)}, u32[]{:S(2)}, u32[]{:S(2)}) %collective-permute-start.10) | collective-permute-done | bytes 294944 | tf_op jit(solution)/shard_map/ppermute | solution.py:115
  46.3 5.7 %collective-permute-done.11.refs_6_.refs_10_.refs_7_ = bf16[128,1152]{1,0:T(8,128)(2,1)S(1)} collective-permute-done((bf16[128,1152]{1,0:T(8,128)(2,1)S(1)}, bf16[128,1152]{1,0:T(8,128)(2,1)S(1)}, u32[]{:S(2)}, u32[]{:S(2)}) %collective-permute-start.11) | collective-permute-done | bytes 294944 | tf_op jit(solution)/shard_map/ppermute | solution.py:115
  54.6 8.2 %collective-permute-done.16.refs_7_ = bf16[160,1440]{1,0:T(8,128)(2,1)S(1)} collective-permute-done((bf16[160,1440]{1,0:T(8,128)(2,1)S(1)}, bf16[160,1440]{1,0:T(8,128)(2,1)S(1)}, u32[]{:S(2)}, u32[]{:S(2)}) %collective-permute-start.16) | collective-permute-done | bytes 460832 | tf_op jit(solution)/shard_map/ppermute | solution.py:118
  69.2 5.3 %collective-permute-done.19.refs_1_ = f32[2,6912]{1,0:T(2,128)S(1)} collective-permute-done((f32[2,6912]{1,0:T(2,128)S(1)}, f32[2,6912]{1,0:T(2,128)S(1)}, u32[]{:S(2)}, u32[]{:S(2)}) %collective-permute-start.19) | collective-permute-done | bytes 55328 | tf_op jit(solution)/shard_map/ppermute | solution.py:121
  80.1 3.1 %collective-permute-done.22.refs_0_ = f32[1,6912]{1,0:T(1,128)S(1)} collective-permute-done((f32[1,6912]{1,0:T(1,128)S(1)}, f32[1,6912]{1,0:T(1,128)S(1)}, u32[]{:S(2)}, u32[]{:S(2)}) %collective-permute-start.22) | collective-permute-done | bytes 27680 | tf_op jit(solution)/shard_map/ppermute | solution.py:118
  87.3 4.3 %shard_map.237 = (bf16[12,72,512]{2,1,0:T(8,128)(2,1)S(1)}, bf16[288,512]{1,0:T(8,128)(2,1)S(1)}, f32[8,128]{1,0:T(8,128)S(1)}) custom-call(s32[4]{0:T(128)S(1)} %pad_add_fusion.place, bf16[512,1152]{1,0:T(8,128)(2,1)S(1)} %get-tuple-element.433.refs_0_, bf16[1152,864]{1,0:T(8,128)(2,1)S(1)} %bitcast.26, ...), custom_call_target="tpu_custom_call", output_to_operand_aliasing={{2}: (4, {})} | custom-call | flops 1 | bytes 1 | tf_op jit(solution)/shard_map/pallas_call | solution.py:85
  93.0 4.3 %shard_map.238 = (bf16[12,72,512]{2,1,0:T(8,128)(2,1)S(1)}, bf16[288,512]{1,0:T(8,128)(2,1)S(1)}, f32[8,128]{1,0:T(8,128)S(1)}) custom-call(s32[4]{0:T(128)S(1)} %pad_add_fusion.place, bf16[512,1152]{1,0:T(8,128)(2,1)S(1)} %get-tuple-element.433.refs_0_, bf16[1152,864]{1,0:T(8,128)(2,1)S(1)} %bitcast.28, ...), custom_call_target="tpu_custom_call", output_to_operand_aliasing={{2}: (4, {})} | custom-call | flops 1 | bytes 1 | tf_op jit(solution)/shard_map/pallas_call | solution.py:85
  101.8 6.3 %collective-permute-done.29.refs_3_ = bf16[288,512]{1,0:T(8,128)(2,1)S(1)} collective-permute-done((bf16[288,512]{1,0:T(8,128)(2,1)S(1)}, bf16[288,512]{1,0:T(8,128)(2,1)S(1)}, u32[]{:S(2)}, u32[]{:S(2)}) %collective-permute-start.29) | collective-permute-done | bytes 294944 | tf_op jit(solution)/shard_map/ppermute | solution.py:115
  108.1 4.0 %shard_map.239 = (bf16[1152,512]{1,0:T(8,128)(2,1)S(1)}, bf16[1152,1152]{1,0:T(8,128)(2,1)S(1)}, f32[256,1152]{1,0:T(8,128)S(1)}, f32[512,1152]{1,0:T(8,128)S(1)...) custom-call(s32[4]{0:T(128)S(1)} %pad_add_fusion.place, ...), custom_call_target="tpu_custom_call", output_to_operand_aliasing={{6}: (13, {})} | custom-call | flops 1 | bytes 1 | tf_op jit(solution)/shard_map/pallas_call | solution.py:85
  114.8 11.5 %collective-permute-done.33.refs_7_ = bf16[144,2304]{1,0:T(8,128)(2,1)S(1)} collective-permute-done((bf16[144,2304]{1,0:T(8,128)(2,1)S(1)}, bf16[144,2304]{1,0:T(8,128)(2,1)S(1)}, u32[]{:S(2)}, u32[]{:S(2)}) %collective-permute-start.33) | collective-permute-done | bytes 663584 | tf_op jit(solution)/shard_map/ppermute | solution.py:118
  127.8 4.5 %shard_map.242 = (bf16[512,1152]{1,0:T(8,128)(2,1)S(1)}, f32[512,1152]{1,0:T(8,128)S(1)}, f32[8,128]{1,0:T(8,128)S(1)}) custom-call(s32[4]{0:T(128)S(1)} %pad_add_fusion.place, bf16[512,1152]{1,0:T(8,128)(2,1)S(1)} %get-tuple-element.453.refs_0_, bf16[1152,1152]{1,0:T(8,128)(2,1)S(1)} %bitcast.18, ...), custom_call_target="tpu_custom_call", output_to_operand_aliasing={{2}: (4, {})} | custom-call | flops 1 | bytes 1 | tf_op jit(solution)/shard_map/pallas_call | solution.py:85
  132.3 3.4 %shard_map.243 = (bf16[512,1152]{1,0:T(8,128)(2,1)S(1)}, f32[1,1152]{1,0:T(1,128)S(1)}, f32[8,128]{1,0:T(8,128)S(1)}) custom-call(s32[4]{0:T(128)S(1)} %pad_add_fusion.place, bf16[512,1152]{1,0:T(8,128)(2,1)S(1)} %get-tuple-element.473.refs_0_.refs_1_, bf16[1152,1152]{1,0:T(8,128)(2,1)S(1)} %bitcast.22, ...), custom_call_target="tpu_custom_call", output_to_operand_aliasing={{2}: (4, {})} | custom-call | flops 1 | bytes 1 | tf_op jit(solution)/shard_map/pallas_call | solution.py:85
  135.7 4.5 %shard_map.244 = (bf16[512,1152]{1,0:T(8,128)(2,1)S(1)}, f32[512,1152]{1,0:T(8,128)S(1)}, f32[8,128]{1,0:T(8,128)S(1)}) custom-call(s32[4]{0:T(128)S(1)} %pad_add_fusion.place, bf16[512,1152]{1,0:T(8,128)(2,1)S(1)} %get-tuple-element.453.refs_0_, bf16[1152,1152]{1,0:T(8,128)(2,1)S(1)} %bitcast.20, ...), custom_call_target="tpu_custom_call", output_to_operand_aliasing={{2}: (4, {})} | custom-call | flops 1 | bytes 1 | tf_op jit(solution)/shard_map/pallas_call | solution.py:85
  140.1 3.4 %shard_map.245 = (bf16[512,1152]{1,0:T(8,128)(2,1)S(1)}, f32[1,1152]{1,0:T(1,128)S(1)}, f32[8,128]{1,0:T(8,128)S(1)}) custom-call(s32[4]{0:T(128)S(1)} %pad_add_fusion.place, bf16[512,1152]{1,0:T(8,128)(2,1)S(1)} %get-tuple-element.473.refs_0_.refs_1_, bf16[1152,1152]{1,0:T(8,128)(2,1)S(1)} %bitcast.24, ...), custom_call_target="tpu_custom_call", output_to_operand_aliasing={{2}: (4, {})} | custom-call | flops 1 | bytes 1 | tf_op jit(solution)/shard_map/pallas_call | solution.py:85
  143.5 5.5 %shard_map.246 = (bf16[512,1152]{1,0:T(8,128)(2,1)S(1)}, f32[8,128]{1,0:T(8,128)S(1)}) custom-call(s32[4]{0:T(128)S(1)} %pad_add_fusion.place, bf16[512,1152]{1,0:T(8,128)(2,1)S(1)} %get-tuple-element.486.refs_0_.refs_1_, bf16[1152,1152]{1,0:T(8,128)(2,1)S(1)} %bitcast.19, ...), custom_call_target="tpu_custom_call", output_to_operand_aliasing={{1}: (5, {})} | custom-call | flops 1 | bytes 1 | tf_op jit(solution)/shard_map/pallas_call | solution.py:85
  168.3 5.0 %collective-permute-done.52.refs_1_ = bf16[144,1152]{1,0:T(8,128)(2,1)S(1)} collective-permute-done((bf16[144,1152]{1,0:T(8,128)(2,1)S(1)}, bf16[144,1152]{1,0:T(8,128)(2,1)S(1)}, u32[]{:S(2)}, u32[]{:S(2)}) %collective-permute-start.52) | collective-permute-done | bytes 331808 | tf_op jit(solution)/shard_map/ppermute | solution.py:118
  175.8 5.5 %shard_map.252 = (f32[256,1152]{1,0:T(8,128)S(1)}, bf16[256,1152]{1,0:T(8,128)(2,1)S(1)}, f32[8,128]{1,0:T(8,128)S(1)}) custom-call(s32[4]{0:T(128)S(1)} %pad_add_fusion.place, bf16[512,1152]{1,0:T(8,128)(2,1)S(1)} %get-tuple-element.471.refs_0_, bf16[1152,1152]{1,0:T(8,128)(2,1)S(1)} %bitcast.23, ...), custom_call_target="tpu_custom_call", output_to_operand_aliasing={{2}: (5, {})} | custom-call | flops 1 | bytes 1 | tf_op jit(solution)/shard_map/pallas_call | solution.py:85
  190.5 5.8 %shard_map.256 = (bf16[512,864]{1,0:T(8,128)(2,1)S(1)}, f32[1,864]{1,0:T(1,128)S(1)}, f32[8,128]{1,0:T(8,128)S(1)}) custom-call(s32[4]{0:T(128)S(1)} %pad_add_fusion.place, bf16[12,72,512]{2,1,0:T(8,128)(2,1)S(1)} %copy-done.7, bf16[1152,1152]{1,0:T(8,128)(2,1)S(1)} %get-tuple-element.536.refs_1_, ...), custom_call_target="tpu_custom_call", output_to_operand_aliasing={{2}: (4, {})} | custom-call | flops 1 | bytes 1 | tf_op jit(solution)/shard_map/pallas_call | solution.py:85
  197.0 2.8 shard_map.258
  209.9 5.6 %collective-permute-done.67.refs_1_ = bf16[144,1152]{1,0:T(8,128)(2,1)S(1)} collective-permute-done((bf16[144,1152]{1,0:T(8,128)(2,1)S(1)}, bf16[144,1152]{1,0:T(8,128)(2,1)S(1)}, u32[]{:S(2)}, u32[]{:S(2)}) %collective-permute-start.67) | collective-permute-done | bytes 331808 | tf_op jit(solution)/shard_map/ppermute | solution.py:121
  217.4 5.8 %shard_map.260 = (bf16[512,864]{1,0:T(8,128)(2,1)S(1)}, f32[1,864]{1,0:T(1,128)S(1)}, f32[8,128]{1,0:T(8,128)S(1)}) custom-call(s32[4]{0:T(128)S(1)} %pad_add_fusion.place, bf16[12,72,512]{2,1,0:T(8,128)(2,1)S(1)} %copy-done.5, bf16[1152,1152]{1,0:T(8,128)(2,1)S(1)} %get-tuple-element.536.refs_1_, ...), custom_call_target="tpu_custom_call", output_to_operand_aliasing={{2}: (4, {})} | custom-call | flops 1 | bytes 1 | tf_op jit(solution)/shard_map/pallas_call | solution.py:85
  225.5 2.9 shard_map.262
  238.8 4.6 %shard_map.267 = (f32[256,1152]{1,0:T(8,128)S(1)}, bf16[256,1152]{1,0:T(8,128)(2,1)S(1)}, f32[2,1152]{1,0:T(2,128)S(1)}, f32[8,128]{1,0:T(8,128)S(1)}) custom-call(s32[4]{0:T(128)S(1)} %pad_add_fusion.place, bf16[512,864]{1,0:T(8,128)(2,1)S(1)} %get-tuple-element.586.refs_1_.refs_0_, ...), custom_call_target="tpu_custom_call", output_to_operand_aliasing={{3}: (11, {})} | custom-call | flops 1 | bytes 1 | tf_op jit(solution)/shard_map/pallas_call | solution.py:85
  269.4 2.9 shard_map.274
  272.4 7.1 %collective-permute-done.91.refs_2_ = bf16[4,16,1152]{2,1,0:T(8,128)(2,1)S(1)} collective-permute-done((bf16[4,16,1152]{2,1,0:T(8,128)(2,1)S(1)}, bf16[4,16,1152]{2,1,0:T(8,128)(2,1)S(1)}, u32[]{:S(2)}, u32[]{:S(2)}) %collective-permute-start.91) | collective-permute-done | bytes 147488 | tf_op jit(solution)/shard_map/ppermute | solution.py:118
  285.5 3.1 %collective-permute-start.101 = (f32[16,144]{1,0:T(8,128)S(1)}, f32[16,144]{1,0:T(8,128)S(1)}, u32[]{:S(2)}, u32[]{:S(2)}) collective-permute-start(f32[16,144]{1,0:T(8,128)S(1)} %get-tuple-element.702.refs_0_), channel_id=1, source_target_pairs={{0,24},{4,28},{8,0},{12,4},{16,8},{20,12},{24,16},{28,20},{1,25},{... | collective-permute-start | bytes 27656 | tf_op jit(solution)/shard_map/ppermute | solution.py:121
  292.3 3.8 %collective-permute-done.99.refs_1_ = f32[16,144]{1,0:T(8,128)S(1)} collective-permute-done((f32[16,144]{1,0:T(8,128)S(1)}, f32[16,144]{1,0:T(8,128)S(1)}, u32[]{:S(2)}, u32[]{:S(2)}) %collective-permute-start.99) | collective-permute-done | bytes 9248 | tf_op jit(solution)/shard_map/ppermute | solution.py:121
  297.1 3.6 %fusion = f32[144,6912]{1,0:T(8,128)} fusion(bf16[16,144]{1,0:T(8,128)(2,1)S(1)} %get-tuple-element.725, bf16[16,6912]{1,0:T(8,128)(2,1)} %copy-done.11), kind=kOutput, calls=%fused_computation.2 | convolution fusion | flops 31850496 | bytes 4207104 | tf_op jit(solution)/shard_map/dot_general | solution.py:47
  (272 shorter events, 150.1 us)
Async XLA Ops:
  8.2 16.4 %collective-permute-start = (bf16[160,1440]{1,0:T(8,128)(2,1)S(1)}, bf16[160,1440]{1,0:T(8,128)(2,1)S(1)}, u32[]{:S(2)}, u32[]{:S(2)}) collective-permute-start(bf16[160,1440]{1,0:T(8,128)(2,1)S(1)} %get-tuple-element.374.refs_0_), channel_id=1, source_target_pairs={{0,8},{4,12},{8,16},{12,20},{16,24},{20,28},{24,0},{28,4},{1,9},{5... | collective-permute-start | bytes 1382408 | tf_op jit(solution)/shard_map/ppermute | solution.py:121
  11.3 13.3 %collective-permute-start.1 = (bf16[160,1440]{1,0:T(8,128)(2,1)S(1)}, bf16[160,1440]{1,0:T(8,128)(2,1)S(1)}, u32[]{:S(2)}, u32[]{:S(2)}) collective-permute-start(bf16[160,1440]{1,0:T(8,128)(2,1)S(1)} %get-tuple-element.374.refs_0_), channel_id=1, source_target_pairs={{0,4},{4,0},{8,12},{12,8},{16,20},{20,16},{24,28},{28,24},{1,5},{5... | collective-permute-start | bytes 1382408 | tf_op jit(solution)/shard_map/ppermute | solution.py:118
  24.6 14.2 %collective-permute-start.6 = (bf16[160,1440]{1,0:T(8,128)(2,1)S(1)}, bf16[160,1440]{1,0:T(8,128)(2,1)S(1)}, u32[]{:S(2)}, u32[]{:S(2)}) collective-permute-start(bf16[160,1440]{1,0:T(8,128)(2,1)S(1)} %collective-permute-done.refs_1_), channel_id=1, source_target_pairs={{0,8},{4,12},{8,16},{12,20},{16,24},{20,28},{24,0},{28,4},{1,9},{5... | collective-permute-start | bytes 1382408 | tf_op jit(solution)/shard_map/ppermute | solution.py:121
  25.6 13.2 %collective-permute-start.7 = (bf16[160,1440]{1,0:T(8,128)(2,1)S(1)}, bf16[160,1440]{1,0:T(8,128)(2,1)S(1)}, u32[]{:S(2)}, u32[]{:S(2)}) collective-permute-start(bf16[160,1440]{1,0:T(8,128)(2,1)S(1)} %collective-permute-done.refs_1_), channel_id=1, source_target_pairs={{0,4},{4,0},{8,12},{12,8},{16,20},{20,16},{24,28},{28,24},{1,5},{5... | collective-permute-start | bytes 1382408 | tf_op jit(solution)/shard_map/ppermute | solution.py:118
  38.8 13.4 %collective-permute-start.12 = (bf16[160,1440]{1,0:T(8,128)(2,1)S(1)}, bf16[160,1440]{1,0:T(8,128)(2,1)S(1)}, u32[]{:S(2)}, u32[]{:S(2)}) collective-permute-start(bf16[160,1440]{1,0:T(8,128)(2,1)S(1)} %collective-permute-done.6.refs_3_), channel_id=1, source_target_pairs={{0,8},{4,12},{8,16},{12,20},{16,24},{20,28},{24,0},{28,4},{1,9},{5... | collective-permute-start | bytes 1382408 | tf_op jit(solution)/shard_map/ppermute | solution.py:121
  53.8 29.4 %collective-permute-start.23 = (bf16[144,2304]{1,0:T(8,128)(2,1)S(1)}, bf16[144,2304]{1,0:T(8,128)(2,1)S(1)}, u32[]{:S(2)}, u32[]{:S(2)}) collective-permute-start(bf16[144,2304]{1,0:T(8,128)(2,1)S(1)} %get-tuple-element.428.refs_0_), channel_id=1, source_target_pairs={{0,8},{4,12},{8,16},{12,20},{16,24},{20,28},{24,0},{28,4},{1,9},{5... | collective-permute-start | bytes 1990664 | tf_op jit(solution)/shard_map/ppermute | solution.py:121
  64.2 19.0 %collective-permute-start.24 = (bf16[144,2304]{1,0:T(8,128)(2,1)S(1)}, bf16[144,2304]{1,0:T(8,128)(2,1)S(1)}, u32[]{:S(2)}, u32[]{:S(2)}) collective-permute-start(bf16[144,2304]{1,0:T(8,128)(2,1)S(1)} %get-tuple-element.428.refs_0_), channel_id=1, source_target_pairs={{0,4},{4,0},{8,12},{12,8},{16,20},{20,16},{24,28},{28,24},{1,5},{5... | collective-permute-start | bytes 1990664 | tf_op jit(solution)/shard_map/ppermute | solution.py:118
  67.4 16.8 %collective-permute-start.25 = (bf16[160,1440]{1,0:T(8,128)(2,1)S(1)}, bf16[160,1440]{1,0:T(8,128)(2,1)S(1)}, u32[]{:S(2)}, u32[]{:S(2)}) collective-permute-start(bf16[160,1440]{1,0:T(8,128)(2,1)S(1)} %collective-permute-done.16.refs_7_), channel_id=1, source_target_pairs={{0,1},{1,0},{2,3},{3,2},{4,5},{5,4},{6,7},{7,6},{8,9},{9,8},{10,11... | collective-permute-start | bytes 1382408 | tf_op jit(solution)/shard_map/ppermute | solution.py:112
  83.2 15.5 %collective-permute-start.27 = (bf16[144,2304]{1,0:T(8,128)(2,1)S(1)}, bf16[144,2304]{1,0:T(8,128)(2,1)S(1)}, u32[]{:S(2)}, u32[]{:S(2)}) collective-permute-start(bf16[144,2304]{1,0:T(8,128)(2,1)S(1)} %collective-permute-done.23.refs_1_), channel_id=1, source_target_pairs={{0,8},{4,12},{8,16},{12,20},{16,24},{20,28},{24,0},{28,4},{1,9},{5... | collective-permute-start | bytes 1990664 | tf_op jit(solution)/shard_map/ppermute | solution.py:121
  83.4 15.4 %collective-permute-start.28 = (bf16[144,2304]{1,0:T(8,128)(2,1)S(1)}, bf16[144,2304]{1,0:T(8,128)(2,1)S(1)}, u32[]{:S(2)}, u32[]{:S(2)}) collective-permute-start(bf16[144,2304]{1,0:T(8,128)(2,1)S(1)} %collective-permute-done.23.refs_1_), channel_id=1, source_target_pairs={{0,4},{4,0},{8,12},{12,8},{16,20},{20,16},{24,28},{28,24},{1,5},{5... | collective-permute-start | bytes 1990664 | tf_op jit(solution)/shard_map/ppermute | solution.py:118
  98.7 14.6 %collective-permute-start.31 = (bf16[144,2304]{1,0:T(8,128)(2,1)S(1)}, bf16[144,2304]{1,0:T(8,128)(2,1)S(1)}, u32[]{:S(2)}, u32[]{:S(2)}) collective-permute-start(bf16[144,2304]{1,0:T(8,128)(2,1)S(1)} %collective-permute-done.27.refs_3_), channel_id=1, source_target_pairs={{0,8},{4,12},{8,16},{12,20},{16,24},{20,28},{24,0},{28,4},{1,9},{5... | collective-permute-start | bytes 1990664 | tf_op jit(solution)/shard_map/ppermute | solution.py:121
  98.7 14.6 %collective-permute-start.32 = (bf16[144,2304]{1,0:T(8,128)(2,1)S(1)}, bf16[144,2304]{1,0:T(8,128)(2,1)S(1)}, u32[]{:S(2)}, u32[]{:S(2)}) collective-permute-start(bf16[144,2304]{1,0:T(8,128)(2,1)S(1)} %collective-permute-done.27.refs_3_), channel_id=1, source_target_pairs={{0,4},{4,0},{8,12},{12,8},{16,20},{20,16},{24,28},{28,24},{1,5},{5... | collective-permute-start | bytes 1990664 | tf_op jit(solution)/shard_map/ppermute | solution.py:118
  113.3 13.0 %collective-permute-start.33 = (bf16[144,2304]{1,0:T(8,128)(2,1)S(1)}, bf16[144,2304]{1,0:T(8,128)(2,1)S(1)}, u32[]{:S(2)}, u32[]{:S(2)}) collective-permute-start(bf16[144,2304]{1,0:T(8,128)(2,1)S(1)} %collective-permute-done.31.refs_5_), channel_id=1, source_target_pairs={{0,4},{4,0},{8,12},{12,8},{16,20},{20,16},{24,28},{28,24},{1,5},{5... | collective-permute-start | bytes 1990664 | tf_op jit(solution)/shard_map/ppermute | solution.py:118
  157.5 28.2 %collective-permute-start.54 = (bf16[512,1152]{1,0:T(8,128)(2,1)S(1)}, bf16[512,1152]{1,0:T(8,128)(2,1)S(1)}, u32[]{:S(2)}, u32[]{:S(2)}) collective-permute-start(bf16[512,1152]{1,0:T(8,128)(2,1)S(1)} %get-tuple-element.537.refs_0_), channel_id=1, source_target_pairs={{0,2},{1,3},{2,0},{3,1},{4,6},{5,7},{6,4},{7,5},{8,10},{9,11},{10,... | collective-permute-start | bytes 3538952 | tf_op jit(solution)/shard_map/ppermute | solution.py:115
  166.3 15.0 %collective-permute-start.53 = (bf16[144,1152]{1,0:T(8,128)(2,1)S(1)}, bf16[144,1152]{1,0:T(8,128)(2,1)S(1)}, u32[]{:S(2)}, u32[]{:S(2)}) collective-permute-start(bf16[144,1152]{1,0:T(8,128)(2,1)S(1)} %get-tuple-element.540), channel_id=1, source_target_pairs={{0,4},{4,0},{8,12},{12,8},{16,20},{20,16},{24,28},{28,24},{1,5},{5... | collective-permute-start | bytes 995336 | tf_op jit(solution)/shard_map/ppermute | solution.py:118
  167.3 22.1 %collective-permute-start.56 = (bf16[144,1152]{1,0:T(8,128)(2,1)S(1)}, bf16[144,1152]{1,0:T(8,128)(2,1)S(1)}, u32[]{:S(2)}, u32[]{:S(2)}) collective-permute-start(bf16[144,1152]{1,0:T(8,128)(2,1)S(1)} %get-tuple-element.555), channel_id=1, source_target_pairs={{0,4},{4,0},{8,12},{12,8},{16,20},{20,16},{24,28},{28,24},{1,5},{5... | collective-permute-start | bytes 995336 | tf_op jit(solution)/shard_map/ppermute | solution.py:118
  173.9 15.4 %collective-permute-start.55 = (bf16[144,1152]{1,0:T(8,128)(2,1)S(1)}, bf16[144,1152]{1,0:T(8,128)(2,1)S(1)}, u32[]{:S(2)}, u32[]{:S(2)}) collective-permute-start(bf16[144,1152]{1,0:T(8,128)(2,1)S(1)} %get-tuple-element.554), channel_id=1, source_target_pairs={{0,8},{4,12},{8,16},{12,20},{16,24},{20,28},{24,0},{28,4},{1,9},{5... | collective-permute-start | bytes 995336 | tf_op jit(solution)/shard_map/ppermute | solution.py:121
  175.3 21.1 %collective-permute-start.58 = (bf16[144,1152]{1,0:T(8,128)(2,1)S(1)}, bf16[144,1152]{1,0:T(8,128)(2,1)S(1)}, u32[]{:S(2)}, u32[]{:S(2)}) collective-permute-start(bf16[144,1152]{1,0:T(8,128)(2,1)S(1)} %get-tuple-element.565), channel_id=1, source_target_pairs={{0,4},{4,0},{8,12},{12,8},{16,20},{20,16},{24,28},{28,24},{1,5},{5... | collective-permute-start | bytes 995336 | tf_op jit(solution)/shard_map/ppermute | solution.py:118
  181.9 14.5 %collective-permute-start.57 = (bf16[144,1152]{1,0:T(8,128)(2,1)S(1)}, bf16[144,1152]{1,0:T(8,128)(2,1)S(1)}, u32[]{:S(2)}, u32[]{:S(2)}) collective-permute-start(bf16[144,1152]{1,0:T(8,128)(2,1)S(1)} %get-tuple-element.564), channel_id=1, source_target_pairs={{0,8},{4,12},{8,16},{12,20},{16,24},{20,28},{24,0},{28,4},{1,9},{5... | collective-permute-start | bytes 995336 | tf_op jit(solution)/shard_map/ppermute | solution.py:121
  185.8 15.2 %collective-permute-start.68 = (bf16[144,1152]{1,0:T(8,128)(2,1)S(1)}, bf16[144,1152]{1,0:T(8,128)(2,1)S(1)}, u32[]{:S(2)}, u32[]{:S(2)}) collective-permute-start(bf16[144,1152]{1,0:T(8,128)(2,1)S(1)} %get-tuple-element.581), channel_id=1, source_target_pairs={{0,4},{4,0},{8,12},{12,8},{16,20},{20,16},{24,28},{28,24},{1,5},{5... | collective-permute-start | bytes 995336 | tf_op jit(solution)/shard_map/ppermute | solution.py:118
  205.3 18.0 %collective-permute-start.69 = (bf16[144,1152]{1,0:T(8,128)(2,1)S(1)}, bf16[144,1152]{1,0:T(8,128)(2,1)S(1)}, u32[]{:S(2)}, u32[]{:S(2)}) collective-permute-start(bf16[144,1152]{1,0:T(8,128)(2,1)S(1)} %get-tuple-element.597), channel_id=1, source_target_pairs={{0,8},{4,12},{8,16},{12,20},{16,24},{20,28},{24,0},{28,4},{1,9},{5... | collective-permute-start | bytes 995336 | tf_op jit(solution)/shard_map/ppermute | solution.py:121
  207.4 21.1 %collective-permute-start.72 = (bf16[144,1152]{1,0:T(8,128)(2,1)S(1)}, bf16[144,1152]{1,0:T(8,128)(2,1)S(1)}, u32[]{:S(2)}, u32[]{:S(2)}) collective-permute-start(bf16[144,1152]{1,0:T(8,128)(2,1)S(1)} %get-tuple-element.605), channel_id=1, source_target_pairs={{0,4},{4,0},{8,12},{12,8},{16,20},{20,16},{24,28},{28,24},{1,5},{5... | collective-permute-start | bytes 995336 | tf_op jit(solution)/shard_map/ppermute | solution.py:118
  208.4 23.6 %collective-permute-start.73 = (bf16[256,1152]{1,0:T(8,128)(2,1)S(1)}, bf16[256,1152]{1,0:T(8,128)(2,1)S(1)}, u32[]{:S(2)}, u32[]{:S(2)}) collective-permute-start(bf16[256,1152]{1,0:T(8,128)(2,1)S(1)} %get-tuple-element.610), channel_id=1, source_target_pairs={{0,2},{1,3},{2,0},{3,1},{4,6},{5,7},{6,4},{7,5},{8,10},{9,11},{10,... | collective-permute-start | bytes 1769480 | tf_op jit(solution)/shard_map/ppermute | solution.py:115
  216.1 13.6 %collective-permute-start.71 = (bf16[144,1152]{1,0:T(8,128)(2,1)S(1)}, bf16[144,1152]{1,0:T(8,128)(2,1)S(1)}, u32[]{:S(2)}, u32[]{:S(2)}) collective-permute-start(bf16[144,1152]{1,0:T(8,128)(2,1)S(1)} %get-tuple-element.604), channel_id=1, source_target_pairs={{0,8},{4,12},{8,16},{12,20},{16,24},{20,28},{24,0},{28,4},{1,9},{5... | collective-permute-start | bytes 995336 | tf_op jit(solution)/shard_map/ppermute | solution.py:121
  216.4 15.5 %collective-permute-start.75 = (bf16[144,1152]{1,0:T(8,128)(2,1)S(1)}, bf16[144,1152]{1,0:T(8,128)(2,1)S(1)}, u32[]{:S(2)}, u32[]{:S(2)}) collective-permute-start(bf16[144,1152]{1,0:T(8,128)(2,1)S(1)} %get-tuple-element.619), channel_id=1, source_target_pairs={{0,4},{4,0},{8,12},{12,8},{16,20},{20,16},{24,28},{28,24},{1,5},{5... | collective-permute-start | bytes 995336 | tf_op jit(solution)/shard_map/ppermute | solution.py:118
  232.0 15.0 %collective-permute-start.80 = (bf16[144,1152]{1,0:T(8,128)(2,1)S(1)}, bf16[144,1152]{1,0:T(8,128)(2,1)S(1)}, u32[]{:S(2)}, u32[]{:S(2)}) collective-permute-start(bf16[144,1152]{1,0:T(8,128)(2,1)S(1)} %get-tuple-element.647), channel_id=1, source_target_pairs={{0,4},{4,0},{8,12},{12,8},{16,20},{20,16},{24,28},{28,24},{1,5},{5... | collective-permute-start | bytes 995336 | tf_op jit(solution)/shard_map/ppermute | solution.py:118
  248.2 13.2 %collective-permute-start.86 = (bf16[144,1152]{1,0:T(8,128)(2,1)S(1)}, bf16[144,1152]{1,0:T(8,128)(2,1)S(1)}, u32[]{:S(2)}, u32[]{:S(2)}) collective-permute-start(bf16[144,1152]{1,0:T(8,128)(2,1)S(1)} %get-tuple-element.665), channel_id=1, source_target_pairs={{0,4},{4,0},{8,12},{12,8},{16,20},{20,16},{24,28},{28,24},{1,5},{5... | collective-permute-start | bytes 995336 | tf_op jit(solution)/shard_map/ppermute | solution.py:118
  264.1 18.7 %collective-permute-start.96 = (bf16[256,1152]{1,0:T(8,128)(2,1)S(1)}, bf16[256,1152]{1,0:T(8,128)(2,1)S(1)}, u32[]{:S(2)}, u32[]{:S(2)}) collective-permute-start(bf16[256,1152]{1,0:T(8,128)(2,1)S(1)} %get-tuple-element.695), channel_id=1, source_target_pairs={{0,2},{1,3},{2,0},{3,1},{4,6},{5,7},{6,4},{7,5},{8,10},{9,11},{10,... | collective-permute-start | bytes 1769480 | tf_op jit(solution)/shard_map/ppermute | solution.py:115
  266.1 13.4 %collective-permute-start.93 = (bf16[144,1152]{1,0:T(8,128)(2,1)S(1)}, bf16[144,1152]{1,0:T(8,128)(2,1)S(1)}, u32[]{:S(2)}, u32[]{:S(2)}) collective-permute-start(bf16[144,1152]{1,0:T(8,128)(2,1)S(1)} %get-tuple-element.683), channel_id=1, source_target_pairs={{0,4},{4,0},{8,12},{12,8},{16,20},{20,16},{24,28},{28,24},{1,5},{5... | collective-permute-start | bytes 995336 | tf_op jit(solution)/shard_map/ppermute | solution.py:118
  266.6 12.9 %collective-permute-start.92 = (bf16[144,1152]{1,0:T(8,128)(2,1)S(1)}, bf16[144,1152]{1,0:T(8,128)(2,1)S(1)}, u32[]{:S(2)}, u32[]{:S(2)}) collective-permute-start(bf16[144,1152]{1,0:T(8,128)(2,1)S(1)} %get-tuple-element.682), channel_id=1, source_target_pairs={{0,8},{4,12},{8,16},{12,20},{16,24},{20,28},{24,0},{28,4},{1,9},{5... | collective-permute-start | bytes 995336 | tf_op jit(solution)/shard_map/ppermute | solution.py:121
  284.8 21.0 %collective-permute-start.104 = (f32[128,1152]{1,0:T(8,128)}, f32[128,1152]{1,0:T(8,128)S(1)}, u32[]{:S(2)}, u32[]{:S(2)}) collective-permute-start(f32[128,1152]{1,0:T(8,128)} %get-tuple-element.713), channel_id=1, source_target_pairs={{0,1},{1,0},{2,3},{3,2},{4,5},{5,4},{6,7},{7,6},{8,9},{9,8},{10,11... | collective-permute-start | bytes 1769480 | tf_op jit(solution)/shard_map/ppermute | solution.py:112
  291.7 14.1 %collective-permute-start.103 = (bf16[128,1152]{1,0:T(8,128)(2,1)}, bf16[128,1152]{1,0:T(8,128)(2,1)S(1)}, u32[]{:S(2)}, u32[]{:S(2)}) collective-permute-start(bf16[128,1152]{1,0:T(8,128)(2,1)} %copy-done.14), channel_id=1, source_target_pairs={{0,1},{1,0},{2,3},{3,2},{4,5},{5,4},{6,7},{7,6},{8,9},{9,8},{10,11... | collective-permute-start | bytes 884744 | tf_op jit(solution)/shard_map/ppermute | solution.py:112
  (89 other events, 644.3 us)

commit v3 on v2

--- a/solution.py
+++ b/solution.py
@@ -15,7 +15,7 @@
 SCALARS = pl.BlockSpec(memory_space=pltpu.SMEM)
 WHOLE = pl.BlockSpec(memory_space=pltpu.VMEM)
 ANY = pl.BlockSpec(memory_space=pl.ANY)
-ROOM = pltpu.CompilerParams(vmem_limit_bytes=20 << 20)
+ROOM = pltpu.CompilerParams(vmem_limit_bytes=14 << 20)
 SHORT = pl.CostEstimate(flops=1, transcendentals=0, bytes_accessed=1)
 
 
@@ -1218,8 +1218,8 @@
     def to_core(chunks):
         return [here.to_core(chunk) for chunk in chunks]
 
-    down_met = to_core(weight_grad(order, shards, act_near, grad_mlp, 8))
-    up_met = to_core(weight_grad(order, shards, mlp_in, pre_near, 8))
+    down_met = to_core(weight_grad(order, shards, act_near, grad_mlp, 2))
+    up_met = to_core(weight_grad(order, shards, mlp_in, pre_near, 2))
     down_met = wait(*down_met)
     down_sum = Scatter(here, order, weight_sum(order, shards, act_mine, grad_mlp, down_met))
     up_met = wait(*up_met)
@@ -1240,14 +1240,14 @@
         attention_grad(order, shards, attn_turned, qkv_grad_near, heads_out, grad_attn, 8)
     )
     met = wait(*met)
+    qkv_grad_mine, qv_sums_mine = attend_back(order, 0, parts_mine, out_full, grad_attn)
     down_sum.turn()
-    qkv_grad_mine, qv_sums_mine = attend_back(order, 0, parts_mine, out_full, grad_attn)
-    up_sum.turn()
     attention_total = Scatter(
         here,
         order,
         attention_sum(order, shards, attn_turned, qkv_grad_mine, heads_out, grad_attn, met),
     )
+    up_sum.turn()
     grad_down = down_sum.finish()
     down_far, down_near = here.to_side(grad_down), here.to_core(grad_down)
     feed_far = wait(feed_far)

time: 314 us -> 306 us (0.975)
  starting transfers between devices: 82.9 us -> 77.4 us
    ppermute x46 -> x34, starting transfers between devices: 9.68 us -> 7.01 us  [to_core(): return lax.ppermute(values, 'seq', [(i, i ^ 1) for i in range(self.seats)])]
  transfers between devices with their start and end apart: 106 -> 94, of which waited for: 37 -> 34; matrix products, arithmetic and copies ran while one was open for 2% -> 2% of each run, Pallas kernels for 31% -> 32%
where the time goes in v3:
time: 306 us; the launch traced here: 301 us
  Pallas kernels  110 us (36%)
  waiting for transfers between devices  98.8 us (32%)
  starting transfers between devices  77.4 us (25%)
  local copies, waits for them, and re-layouts  8.65 us (3%)
    pallas_call x54, Pallas kernels, run(): pl.pallas_call(body, out_shape=tuple(outs) + (struct(self.token.shape, se...  110 us
    ppermute x23, waiting for transfers between devices, to_pair(): lax.ppermute(values, 'fsdp', [(i, i ^ 1) for i in range(self.shards)])  34.9 us
    ppermute x13, waiting for transfers between devices, to_side(): return lax.ppermute(values, 'seq', [(i, i ^ 2) for i in range(self.seats)])  31.5 us
    ppermute x24, waiting for transfers between devices, to_line(): lax.ppermute(values, 'fsdp', [(i, (i + 2 * step) % self.shards) for i in...  30.4 us
    ppermute x24, starting transfers between devices, to_line(): lax.ppermute(values, 'fsdp', [(i, (i + 2 * step) % self.shards) for i in...  29.9 us
    ppermute x23, starting transfers between devices, to_pair(): lax.ppermute(values, 'fsdp', [(i, i ^ 1) for i in range(self.shards)])  23.6 us
    ppermute x13, starting transfers between devices, to_side(): return lax.ppermute(values, 'seq', [(i, i ^ 2) for i in range(self.seats)])  16.9 us
    ppermute x34, starting transfers between devices, to_core(): return lax.ppermute(values, 'seq', [(i, i ^ 1) for i in range(self.seats)])  7.01 us
  transfers between devices with their start and end apart: 94, of which 34 were waited for; matrix products, arithmetic and copies ran while one was open for 2% of the time, Pallas kernels for 32%

profile of v3, /device:TPU:0, one launch (start us, length us, event | category | flops | bytes accessed | tf_op | source)
XLA Modules:
  0.0 301.4 jit_solution(8672908027064342513)
XLA Ops:
  0.7 3.6 %concatenate.3 = bf16[2016]{0:T(1024)(128)(2,1)S(1)} concatenate(bf16[864]{0:T(1024)(128)(2,1)} %param.16, bf16[288]{0:T(512)(128)(2,1)} %param.18, bf16[144]{0:T(256)(128)(2,1)} %param.20, bf16[576]{0:T(1024)(128)(2,1)} %param.22, bf16[144]{0:T(256)(128)(2,1)} %param.24), dimensions={0} | concatenate | bytes 8064 | tf_op jit(solution)/shard_map/concatenate | solution.py:1144
  8.2 3.1 %collective-permute-start = (bf16[160,1440]{1,0:T(8,128)(2,1)S(1)}, bf16[160,1440]{1,0:T(8,128)(2,1)S(1)}, u32[]{:S(2)}, u32[]{:S(2)}) collective-permute-start(bf16[160,1440]{1,0:T(8,128)(2,1)S(1)} %get-tuple-element.350.refs_0_), channel_id=1, source_target_pairs={{0,8},{4,12},{8,16},{12,20},{16,24},{20,28},{24,0},{28,4},{1,9},{5... | collective-permute-start | bytes 1382408 | tf_op jit(solution)/shard_map/ppermute | solution.py:121
  17.5 7.0 %collective-permute-done.refs_1_ = bf16[160,1440]{1,0:T(8,128)(2,1)S(1)} collective-permute-done((bf16[160,1440]{1,0:T(8,128)(2,1)S(1)}, bf16[160,1440]{1,0:T(8,128)(2,1)S(1)}, u32[]{:S(2)}, u32[]{:S(2)}) %collective-permute-start) | collective-permute-done | bytes 460832 | tf_op jit(solution)/shard_map/ppermute | solution.py:121
  29.1 7.5 %collective-permute-done.5.refs_5_.refs_9_.refs_6_ = bf16[128,1152]{1,0:T(8,128)(2,1)S(1)} collective-permute-done((bf16[128,1152]{1,0:T(8,128)(2,1)S(1)}, bf16[128,1152]{1,0:T(8,128)(2,1)S(1)}, u32[]{:S(2)}, u32[]{:S(2)}) %collective-permute-start.5) | collective-permute-done | bytes 294944 | tf_op jit(solution)/shard_map/ppermute | solution.py:115
  40.8 3.9 %collective-permute-done.10.refs_2_.refs_6_ = bf16[128,1152]{1,0:T(8,128)(2,1)S(1)} collective-permute-done((bf16[128,1152]{1,0:T(8,128)(2,1)S(1)}, bf16[128,1152]{1,0:T(8,128)(2,1)S(1)}, u32[]{:S(2)}, u32[]{:S(2)}) %collective-permute-start.10) | collective-permute-done | bytes 294944 | tf_op jit(solution)/shard_map/ppermute | solution.py:115
  46.2 5.7 %collective-permute-done.11.refs_6_.refs_10_.refs_7_ = bf16[128,1152]{1,0:T(8,128)(2,1)S(1)} collective-permute-done((bf16[128,1152]{1,0:T(8,128)(2,1)S(1)}, bf16[128,1152]{1,0:T(8,128)(2,1)S(1)}, u32[]{:S(2)}, u32[]{:S(2)}) %collective-permute-start.11) | collective-permute-done | bytes 294944 | tf_op jit(solution)/shard_map/ppermute | solution.py:115
  54.6 8.2 %collective-permute-done.16.refs_7_ = bf16[160,1440]{1,0:T(8,128)(2,1)S(1)} collective-permute-done((bf16[160,1440]{1,0:T(8,128)(2,1)S(1)}, bf16[160,1440]{1,0:T(8,128)(2,1)S(1)}, u32[]{:S(2)}, u32[]{:S(2)}) %collective-permute-start.16) | collective-permute-done | bytes 460832 | tf_op jit(solution)/shard_map/ppermute | solution.py:118
  69.2 5.3 %collective-permute-done.19.refs_1_ = f32[2,6912]{1,0:T(2,128)S(1)} collective-permute-done((f32[2,6912]{1,0:T(2,128)S(1)}, f32[2,6912]{1,0:T(2,128)S(1)}, u32[]{:S(2)}, u32[]{:S(2)}) %collective-permute-start.19) | collective-permute-done | bytes 55328 | tf_op jit(solution)/shard_map/ppermute | solution.py:121
  80.1 3.1 %collective-permute-done.22.refs_0_ = f32[1,6912]{1,0:T(1,128)S(1)} collective-permute-done((f32[1,6912]{1,0:T(1,128)S(1)}, f32[1,6912]{1,0:T(1,128)S(1)}, u32[]{:S(2)}, u32[]{:S(2)}) %collective-permute-start.22) | collective-permute-done | bytes 27680 | tf_op jit(solution)/shard_map/ppermute | solution.py:118
  87.3 4.3 %shard_map.237 = (bf16[12,72,512]{2,1,0:T(8,128)(2,1)S(1)}, bf16[288,512]{1,0:T(8,128)(2,1)S(1)}, f32[8,128]{1,0:T(8,128)S(1)}) custom-call(s32[4]{0:T(128)S(1)} %pad_add_fusion.place, bf16[512,1152]{1,0:T(8,128)(2,1)S(1)} %get-tuple-element.409.refs_0_, bf16[1152,864]{1,0:T(8,128)(2,1)S(1)} %bitcast.26, ...), custom_call_target="tpu_custom_call", output_to_operand_aliasing={{2}: (4, {})} | custom-call | flops 1 | bytes 1 | tf_op jit(solution)/shard_map/pallas_call | solution.py:85
  93.0 4.3 %shard_map.238 = (bf16[12,72,512]{2,1,0:T(8,128)(2,1)S(1)}, bf16[288,512]{1,0:T(8,128)(2,1)S(1)}, f32[8,128]{1,0:T(8,128)S(1)}) custom-call(s32[4]{0:T(128)S(1)} %pad_add_fusion.place, bf16[512,1152]{1,0:T(8,128)(2,1)S(1)} %get-tuple-element.409.refs_0_, bf16[1152,864]{1,0:T(8,128)(2,1)S(1)} %bitcast.28, ...), custom_call_target="tpu_custom_call", output_to_operand_aliasing={{2}: (4, {})} | custom-call | flops 1 | bytes 1 | tf_op jit(solution)/shard_map/pallas_call | solution.py:85
  101.8 6.3 %collective-permute-done.29.refs_3_ = bf16[288,512]{1,0:T(8,128)(2,1)S(1)} collective-permute-done((bf16[288,512]{1,0:T(8,128)(2,1)S(1)}, bf16[288,512]{1,0:T(8,128)(2,1)S(1)}, u32[]{:S(2)}, u32[]{:S(2)}) %collective-permute-start.29) | collective-permute-done | bytes 294944 | tf_op jit(solution)/shard_map/ppermute | solution.py:115
  108.1 3.8 %shard_map.239 = (bf16[1152,512]{1,0:T(8,128)(2,1)S(1)}, bf16[1152,1152]{1,0:T(8,128)(2,1)S(1)}, f32[256,1152]{1,0:T(8,128)S(1)}, f32[512,1152]{1,0:T(8,128)S(1)...) custom-call(s32[4]{0:T(128)S(1)} %pad_add_fusion.place, ...), custom_call_target="tpu_custom_call", output_to_operand_aliasing={{6}: (13, {})} | custom-call | flops 1 | bytes 1 | tf_op jit(solution)/shard_map/pallas_call | solution.py:85
  114.7 11.6 %collective-permute-done.33.refs_7_ = bf16[144,2304]{1,0:T(8,128)(2,1)S(1)} collective-permute-done((bf16[144,2304]{1,0:T(8,128)(2,1)S(1)}, bf16[144,2304]{1,0:T(8,128)(2,1)S(1)}, u32[]{:S(2)}, u32[]{:S(2)}) %collective-permute-start.33) | collective-permute-done | bytes 663584 | tf_op jit(solution)/shard_map/ppermute | solution.py:118
  127.8 4.9 %shard_map.242 = (bf16[512,1152]{1,0:T(8,128)(2,1)S(1)}, f32[512,1152]{1,0:T(8,128)S(1)}, f32[8,128]{1,0:T(8,128)S(1)}) custom-call(s32[4]{0:T(128)S(1)} %pad_add_fusion.place, bf16[512,1152]{1,0:T(8,128)(2,1)S(1)} %get-tuple-element.429.refs_0_, bf16[1152,1152]{1,0:T(8,128)(2,1)S(1)} %bitcast.18, ...), custom_call_target="tpu_custom_call", output_to_operand_aliasing={{2}: (4, {})} | custom-call | flops 1 | bytes 1 | tf_op jit(solution)/shard_map/pallas_call | solution.py:85
  132.7 3.4 %shard_map.243 = (bf16[512,1152]{1,0:T(8,128)(2,1)S(1)}, f32[1,1152]{1,0:T(1,128)S(1)}, f32[8,128]{1,0:T(8,128)S(1)}) custom-call(s32[4]{0:T(128)S(1)} %pad_add_fusion.place, bf16[512,1152]{1,0:T(8,128)(2,1)S(1)} %get-tuple-element.449.refs_0_.refs_1_, bf16[1152,1152]{1,0:T(8,128)(2,1)S(1)} %bitcast.22, ...), custom_call_target="tpu_custom_call", output_to_operand_aliasing={{2}: (4, {})} | custom-call | flops 1 | bytes 1 | tf_op jit(solution)/shard_map/pallas_call | solution.py:85
  136.1 4.5 %shard_map.244 = (bf16[512,1152]{1,0:T(8,128)(2,1)S(1)}, f32[512,1152]{1,0:T(8,128)S(1)}, f32[8,128]{1,0:T(8,128)S(1)}) custom-call(s32[4]{0:T(128)S(1)} %pad_add_fusion.place, bf16[512,1152]{1,0:T(8,128)(2,1)S(1)} %get-tuple-element.429.refs_0_, bf16[1152,1152]{1,0:T(8,128)(2,1)S(1)} %bitcast.20, ...), custom_call_target="tpu_custom_call", output_to_operand_aliasing={{2}: (4, {})} | custom-call | flops 1 | bytes 1 | tf_op jit(solution)/shard_map/pallas_call | solution.py:85
  140.6 3.4 %shard_map.245 = (bf16[512,1152]{1,0:T(8,128)(2,1)S(1)}, f32[1,1152]{1,0:T(1,128)S(1)}, f32[8,128]{1,0:T(8,128)S(1)}) custom-call(s32[4]{0:T(128)S(1)} %pad_add_fusion.place, bf16[512,1152]{1,0:T(8,128)(2,1)S(1)} %get-tuple-element.449.refs_0_.refs_1_, bf16[1152,1152]{1,0:T(8,128)(2,1)S(1)} %bitcast.24, ...), custom_call_target="tpu_custom_call", output_to_operand_aliasing={{2}: (4, {})} | custom-call | flops 1 | bytes 1 | tf_op jit(solution)/shard_map/pallas_call | solution.py:85
  144.0 5.1 %shard_map.246 = (bf16[512,1152]{1,0:T(8,128)(2,1)S(1)}, f32[8,128]{1,0:T(8,128)S(1)}) custom-call(s32[4]{0:T(128)S(1)} %pad_add_fusion.place, bf16[512,1152]{1,0:T(8,128)(2,1)S(1)} %get-tuple-element.462.refs_0_.refs_1_, bf16[1152,1152]{1,0:T(8,128)(2,1)S(1)} %bitcast.19, ...), custom_call_target="tpu_custom_call", output_to_operand_aliasing={{1}: (5, {})} | custom-call | flops 1 | bytes 1 | tf_op jit(solution)/shard_map/pallas_call | solution.py:85
  164.8 4.8 %collective-permute-done.40.refs_1_ = bf16[144,1152]{1,0:T(8,128)(2,1)S(1)} collective-permute-done((bf16[144,1152]{1,0:T(8,128)(2,1)S(1)}, bf16[144,1152]{1,0:T(8,128)(2,1)S(1)}, u32[]{:S(2)}, u32[]{:S(2)}) %collective-permute-start.40) | collective-permute-done | bytes 331808 | tf_op jit(solution)/shard_map/ppermute | solution.py:118
  172.0 5.6 %shard_map.252 = (f32[256,1152]{1,0:T(8,128)S(1)}, bf16[256,1152]{1,0:T(8,128)(2,1)S(1)}, f32[8,128]{1,0:T(8,128)S(1)}) custom-call(s32[4]{0:T(128)S(1)} %pad_add_fusion.place, bf16[512,1152]{1,0:T(8,128)(2,1)S(1)} %get-tuple-element.447.refs_0_, bf16[1152,1152]{1,0:T(8,128)(2,1)S(1)} %bitcast.23, ...), custom_call_target="tpu_custom_call", output_to_operand_aliasing={{2}: (5, {})} | custom-call | flops 1 | bytes 1 | tf_op jit(solution)/shard_map/pallas_call | solution.py:85
  187.0 5.8 %shard_map.256 = (bf16[512,864]{1,0:T(8,128)(2,1)S(1)}, f32[1,864]{1,0:T(1,128)S(1)}, f32[8,128]{1,0:T(8,128)S(1)}) custom-call(s32[4]{0:T(128)S(1)} %pad_add_fusion.place, bf16[12,72,512]{2,1,0:T(8,128)(2,1)S(1)} %get-tuple-element.503.refs_0_, bf16[1152,1152]{1,0:T(8,128)(2,1)S(1)} %get-tuple-element.489.refs_1_, ...), custom_call_target="tpu_custom_call", output_to_operand_aliasing={{2}: (4, {})} | custom-call | flops 1 | bytes 1 | tf_op jit(solution)/shard_map/pallas_call | solution.py:85
  193.5 2.8 shard_map.258
  206.6 5.8 %shard_map.259 = (bf16[512,864]{1,0:T(8,128)(2,1)S(1)}, f32[1,864]{1,0:T(1,128)S(1)}, f32[8,128]{1,0:T(8,128)S(1)}) custom-call(s32[4]{0:T(128)S(1)} %pad_add_fusion.place, bf16[12,72,512]{2,1,0:T(8,128)(2,1)S(1)} %get-tuple-element.488.refs_0_, bf16[1152,1152]{1,0:T(8,128)(2,1)S(1)} %get-tuple-element.489.refs_1_, ...), custom_call_target="tpu_custom_call", output_to_operand_aliasing={{2}: (4, {})} | custom-call | flops 1 | bytes 1 | tf_op jit(solution)/shard_map/pallas_call | solution.py:85
  214.8 2.9 shard_map.261
  220.8 5.3 %collective-permute-done.59.refs_1_ = bf16[144,1152]{1,0:T(8,128)(2,1)S(1)} collective-permute-done((bf16[144,1152]{1,0:T(8,128)(2,1)S(1)}, bf16[144,1152]{1,0:T(8,128)(2,1)S(1)}, u32[]{:S(2)}, u32[]{:S(2)}) %collective-permute-start.59) | collective-permute-done | bytes 331808 | tf_op jit(solution)/shard_map/ppermute | solution.py:121
  235.5 4.5 %shard_map.267 = (f32[256,1152]{1,0:T(8,128)S(1)}, bf16[256,1152]{1,0:T(8,128)(2,1)S(1)}, f32[2,1152]{1,0:T(2,128)S(1)}, f32[8,128]{1,0:T(8,128)S(1)}) custom-call(s32[4]{0:T(128)S(1)} %pad_add_fusion.place, bf16[512,864]{1,0:T(8,128)(2,1)S(1)} %get-tuple-element.532.refs_1_.refs_0_, ...), custom_call_target="tpu_custom_call", output_to_operand_aliasing={{3}: (11, {})} | custom-call | flops 1 | bytes 1 | tf_op jit(solution)/shard_map/pallas_call | solution.py:85
  251.5 2.9 collective-permute-start.76
  264.4 2.7 shard_map.274
  267.1 7.2 %collective-permute-done.79.refs_2_ = bf16[4,16,1152]{2,1,0:T(8,128)(2,1)S(1)} collective-permute-done((bf16[4,16,1152]{2,1,0:T(8,128)(2,1)S(1)}, bf16[4,16,1152]{2,1,0:T(8,128)(2,1)S(1)}, u32[]{:S(2)}, u32[]{:S(2)}) %collective-permute-start.79) | collective-permute-done | bytes 147488 | tf_op jit(solution)/shard_map/ppermute | solution.py:118
  282.6 2.7 collective-permute-done.85.refs_2_
  290.7 2.6 fusion
  (236 shorter events, 145.1 us)
Async XLA Ops:
  8.2 16.4 %collective-permute-start = (bf16[160,1440]{1,0:T(8,128)(2,1)S(1)}, bf16[160,1440]{1,0:T(8,128)(2,1)S(1)}, u32[]{:S(2)}, u32[]{:S(2)}) collective-permute-start(bf16[160,1440]{1,0:T(8,128)(2,1)S(1)} %get-tuple-element.350.refs_0_), channel_id=1, source_target_pairs={{0,8},{4,12},{8,16},{12,20},{16,24},{20,28},{24,0},{28,4},{1,9},{5... | collective-permute-start | bytes 1382408 | tf_op jit(solution)/shard_map/ppermute | solution.py:121
  11.3 13.3 %collective-permute-start.1 = (bf16[160,1440]{1,0:T(8,128)(2,1)S(1)}, bf16[160,1440]{1,0:T(8,128)(2,1)S(1)}, u32[]{:S(2)}, u32[]{:S(2)}) collective-permute-start(bf16[160,1440]{1,0:T(8,128)(2,1)S(1)} %get-tuple-element.350.refs_0_), channel_id=1, source_target_pairs={{0,4},{4,0},{8,12},{12,8},{16,20},{20,16},{24,28},{28,24},{1,5},{5... | collective-permute-start | bytes 1382408 | tf_op jit(solution)/shard_map/ppermute | solution.py:118
  24.5 14.2 %collective-permute-start.6 = (bf16[160,1440]{1,0:T(8,128)(2,1)S(1)}, bf16[160,1440]{1,0:T(8,128)(2,1)S(1)}, u32[]{:S(2)}, u32[]{:S(2)}) collective-permute-start(bf16[160,1440]{1,0:T(8,128)(2,1)S(1)} %collective-permute-done.refs_1_), channel_id=1, source_target_pairs={{0,8},{4,12},{8,16},{12,20},{16,24},{20,28},{24,0},{28,4},{1,9},{5... | collective-permute-start | bytes 1382408 | tf_op jit(solution)/shard_map/ppermute | solution.py:121
  25.5 13.2 %collective-permute-start.7 = (bf16[160,1440]{1,0:T(8,128)(2,1)S(1)}, bf16[160,1440]{1,0:T(8,128)(2,1)S(1)}, u32[]{:S(2)}, u32[]{:S(2)}) collective-permute-start(bf16[160,1440]{1,0:T(8,128)(2,1)S(1)} %collective-permute-done.refs_1_), channel_id=1, source_target_pairs={{0,4},{4,0},{8,12},{12,8},{16,20},{20,16},{24,28},{28,24},{1,5},{5... | collective-permute-start | bytes 1382408 | tf_op jit(solution)/shard_map/ppermute | solution.py:118
  38.8 13.4 %collective-permute-start.12 = (bf16[160,1440]{1,0:T(8,128)(2,1)S(1)}, bf16[160,1440]{1,0:T(8,128)(2,1)S(1)}, u32[]{:S(2)}, u32[]{:S(2)}) collective-permute-start(bf16[160,1440]{1,0:T(8,128)(2,1)S(1)} %collective-permute-done.6.refs_3_), channel_id=1, source_target_pairs={{0,8},{4,12},{8,16},{12,20},{16,24},{20,28},{24,0},{28,4},{1,9},{5... | collective-permute-start | bytes 1382408 | tf_op jit(solution)/shard_map/ppermute | solution.py:121
  53.8 29.4 %collective-permute-start.23 = (bf16[144,2304]{1,0:T(8,128)(2,1)S(1)}, bf16[144,2304]{1,0:T(8,128)(2,1)S(1)}, u32[]{:S(2)}, u32[]{:S(2)}) collective-permute-start(bf16[144,2304]{1,0:T(8,128)(2,1)S(1)} %get-tuple-element.404.refs_0_), channel_id=1, source_target_pairs={{0,8},{4,12},{8,16},{12,20},{16,24},{20,28},{24,0},{28,4},{1,9},{5... | collective-permute-start | bytes 1990664 | tf_op jit(solution)/shard_map/ppermute | solution.py:121
  64.2 19.0 %collective-permute-start.24 = (bf16[144,2304]{1,0:T(8,128)(2,1)S(1)}, bf16[144,2304]{1,0:T(8,128)(2,1)S(1)}, u32[]{:S(2)}, u32[]{:S(2)}) collective-permute-start(bf16[144,2304]{1,0:T(8,128)(2,1)S(1)} %get-tuple-element.404.refs_0_), channel_id=1, source_target_pairs={{0,4},{4,0},{8,12},{12,8},{16,20},{20,16},{24,28},{28,24},{1,5},{5... | collective-permute-start | bytes 1990664 | tf_op jit(solution)/shard_map/ppermute | solution.py:118
  67.4 16.8 %collective-permute-start.25 = (bf16[160,1440]{1,0:T(8,128)(2,1)S(1)}, bf16[160,1440]{1,0:T(8,128)(2,1)S(1)}, u32[]{:S(2)}, u32[]{:S(2)}) collective-permute-start(bf16[160,1440]{1,0:T(8,128)(2,1)S(1)} %collective-permute-done.16.refs_7_), channel_id=1, source_target_pairs={{0,1},{1,0},{2,3},{3,2},{4,5},{5,4},{6,7},{7,6},{8,9},{9,8},{10,11... | collective-permute-start | bytes 1382408 | tf_op jit(solution)/shard_map/ppermute | solution.py:112
  83.2 15.6 %collective-permute-start.27 = (bf16[144,2304]{1,0:T(8,128)(2,1)S(1)}, bf16[144,2304]{1,0:T(8,128)(2,1)S(1)}, u32[]{:S(2)}, u32[]{:S(2)}) collective-permute-start(bf16[144,2304]{1,0:T(8,128)(2,1)S(1)} %collective-permute-done.23.refs_1_), channel_id=1, source_target_pairs={{0,8},{4,12},{8,16},{12,20},{16,24},{20,28},{24,0},{28,4},{1,9},{5... | collective-permute-start | bytes 1990664 | tf_op jit(solution)/shard_map/ppermute | solution.py:121
  83.4 15.4 %collective-permute-start.28 = (bf16[144,2304]{1,0:T(8,128)(2,1)S(1)}, bf16[144,2304]{1,0:T(8,128)(2,1)S(1)}, u32[]{:S(2)}, u32[]{:S(2)}) collective-permute-start(bf16[144,2304]{1,0:T(8,128)(2,1)S(1)} %collective-permute-done.23.refs_1_), channel_id=1, source_target_pairs={{0,4},{4,0},{8,12},{12,8},{16,20},{20,16},{24,28},{28,24},{1,5},{5... | collective-permute-start | bytes 1990664 | tf_op jit(solution)/shard_map/ppermute | solution.py:118
  98.7 14.5 %collective-permute-start.31 = (bf16[144,2304]{1,0:T(8,128)(2,1)S(1)}, bf16[144,2304]{1,0:T(8,128)(2,1)S(1)}, u32[]{:S(2)}, u32[]{:S(2)}) collective-permute-start(bf16[144,2304]{1,0:T(8,128)(2,1)S(1)} %collective-permute-done.27.refs_3_), channel_id=1, source_target_pairs={{0,8},{4,12},{8,16},{12,20},{16,24},{20,28},{24,0},{28,4},{1,9},{5... | collective-permute-start | bytes 1990664 | tf_op jit(solution)/shard_map/ppermute | solution.py:121
  98.7 14.5 %collective-permute-start.32 = (bf16[144,2304]{1,0:T(8,128)(2,1)S(1)}, bf16[144,2304]{1,0:T(8,128)(2,1)S(1)}, u32[]{:S(2)}, u32[]{:S(2)}) collective-permute-start(bf16[144,2304]{1,0:T(8,128)(2,1)S(1)} %collective-permute-done.27.refs_3_), channel_id=1, source_target_pairs={{0,4},{4,0},{8,12},{12,8},{16,20},{20,16},{24,28},{28,24},{1,5},{5... | collective-permute-start | bytes 1990664 | tf_op jit(solution)/shard_map/ppermute | solution.py:118
  113.3 13.0 %collective-permute-start.33 = (bf16[144,2304]{1,0:T(8,128)(2,1)S(1)}, bf16[144,2304]{1,0:T(8,128)(2,1)S(1)}, u32[]{:S(2)}, u32[]{:S(2)}) collective-permute-start(bf16[144,2304]{1,0:T(8,128)(2,1)S(1)} %collective-permute-done.31.refs_5_), channel_id=1, source_target_pairs={{0,4},{4,0},{8,12},{12,8},{16,20},{20,16},{24,28},{28,24},{1,5},{5... | collective-permute-start | bytes 1990664 | tf_op jit(solution)/shard_map/ppermute | solution.py:118
  127.3 13.3 %collective-permute-start.35 = (bf16[8,144,1152]{2,1,0:T(8,128)(2,1)S(1)}, bf16[8,144,1152]{2,1,0:T(8,128)(2,1)S(1)}, u32[]{:S(2)}, u32[]{:S(2)}) collective-permute-start(bf16[8,144,1152]{2,1,0:T(8,128)(2,1)S(1)} %get-tuple-element.448), channel_id=1, source_target_pairs={{0,1},{1,0},{2,3},{3,2},{4,5},{5,4},{6,7},{7,6},{8,9},{9,8},{10,11... | collective-permute-start | bytes 7962632 | tf_op jit(solution)/shard_map/ppermute | solution.py:112
  154.8 28.0 %collective-permute-start.42 = (bf16[512,1152]{1,0:T(8,128)(2,1)S(1)}, bf16[512,1152]{1,0:T(8,128)(2,1)S(1)}, u32[]{:S(2)}, u32[]{:S(2)}) collective-permute-start(bf16[512,1152]{1,0:T(8,128)(2,1)S(1)} %get-tuple-element.490.refs_0_), channel_id=1, source_target_pairs={{0,2},{1,3},{2,0},{3,1},{4,6},{5,7},{6,4},{7,5},{8,10},{9,11},{10,... | collective-permute-start | bytes 3538952 | tf_op jit(solution)/shard_map/ppermute | solution.py:115
  162.7 14.9 %collective-permute-start.41 = (bf16[144,1152]{1,0:T(8,128)(2,1)S(1)}, bf16[144,1152]{1,0:T(8,128)(2,1)S(1)}, u32[]{:S(2)}, u32[]{:S(2)}) collective-permute-start(bf16[144,1152]{1,0:T(8,128)(2,1)S(1)} %get-tuple-element.493), channel_id=1, source_target_pairs={{0,4},{4,0},{8,12},{12,8},{16,20},{20,16},{24,28},{28,24},{1,5},{5... | collective-permute-start | bytes 995336 | tf_op jit(solution)/shard_map/ppermute | solution.py:118
  163.8 22.5 %collective-permute-start.44 = (bf16[144,1152]{1,0:T(8,128)(2,1)S(1)}, bf16[144,1152]{1,0:T(8,128)(2,1)S(1)}, u32[]{:S(2)}, u32[]{:S(2)}) collective-permute-start(bf16[144,1152]{1,0:T(8,128)(2,1)S(1)} %get-tuple-element.507), channel_id=1, source_target_pairs={{0,4},{4,0},{8,12},{12,8},{16,20},{20,16},{24,28},{28,24},{1,5},{5... | collective-permute-start | bytes 995336 | tf_op jit(solution)/shard_map/ppermute | solution.py:118
  170.2 16.1 %collective-permute-start.43 = (bf16[144,1152]{1,0:T(8,128)(2,1)S(1)}, bf16[144,1152]{1,0:T(8,128)(2,1)S(1)}, u32[]{:S(2)}, u32[]{:S(2)}) collective-permute-start(bf16[144,1152]{1,0:T(8,128)(2,1)S(1)} %get-tuple-element.506), channel_id=1, source_target_pairs={{0,8},{4,12},{8,16},{12,20},{16,24},{20,28},{24,0},{28,4},{1,9},{5... | collective-permute-start | bytes 995336 | tf_op jit(solution)/shard_map/ppermute | solution.py:121
  171.5 21.3 %collective-permute-start.46 = (bf16[144,1152]{1,0:T(8,128)(2,1)S(1)}, bf16[144,1152]{1,0:T(8,128)(2,1)S(1)}, u32[]{:S(2)}, u32[]{:S(2)}) collective-permute-start(bf16[144,1152]{1,0:T(8,128)(2,1)S(1)} %get-tuple-element.517), channel_id=1, source_target_pairs={{0,4},{4,0},{8,12},{12,8},{16,20},{20,16},{24,28},{28,24},{1,5},{5... | collective-permute-start | bytes 995336 | tf_op jit(solution)/shard_map/ppermute | solution.py:118
  178.3 14.5 %collective-permute-start.45 = (bf16[144,1152]{1,0:T(8,128)(2,1)S(1)}, bf16[144,1152]{1,0:T(8,128)(2,1)S(1)}, u32[]{:S(2)}, u32[]{:S(2)}) collective-permute-start(bf16[144,1152]{1,0:T(8,128)(2,1)S(1)} %get-tuple-element.516), channel_id=1, source_target_pairs={{0,8},{4,12},{8,16},{12,20},{16,24},{20,28},{24,0},{28,4},{1,9},{5... | collective-permute-start | bytes 995336 | tf_op jit(solution)/shard_map/ppermute | solution.py:121
  182.8 14.7 %collective-permute-start.56 = (bf16[144,1152]{1,0:T(8,128)(2,1)S(1)}, bf16[144,1152]{1,0:T(8,128)(2,1)S(1)}, u32[]{:S(2)}, u32[]{:S(2)}) collective-permute-start(bf16[144,1152]{1,0:T(8,128)(2,1)S(1)} %get-tuple-element.544), channel_id=1, source_target_pairs={{0,4},{4,0},{8,12},{12,8},{16,20},{20,16},{24,28},{28,24},{1,5},{5... | collective-permute-start | bytes 995336 | tf_op jit(solution)/shard_map/ppermute | solution.py:118
  200.2 14.1 %collective-permute-start.58 = (bf16[144,1152]{1,0:T(8,128)(2,1)S(1)}, bf16[144,1152]{1,0:T(8,128)(2,1)S(1)}, u32[]{:S(2)}, u32[]{:S(2)}) collective-permute-start(bf16[144,1152]{1,0:T(8,128)(2,1)S(1)} %get-tuple-element.551), channel_id=1, source_target_pairs={{0,4},{4,0},{8,12},{12,8},{16,20},{20,16},{24,28},{28,24},{1,5},{5... | collective-permute-start | bytes 995336 | tf_op jit(solution)/shard_map/ppermute | solution.py:118
  201.7 17.3 %collective-permute-start.57 = (bf16[144,1152]{1,0:T(8,128)(2,1)S(1)}, bf16[144,1152]{1,0:T(8,128)(2,1)S(1)}, u32[]{:S(2)}, u32[]{:S(2)}) collective-permute-start(bf16[144,1152]{1,0:T(8,128)(2,1)S(1)} %get-tuple-element.550), channel_id=1, source_target_pairs={{0,8},{4,12},{8,16},{12,20},{16,24},{20,28},{24,0},{28,4},{1,9},{5... | collective-permute-start | bytes 995336 | tf_op jit(solution)/shard_map/ppermute | solution.py:121
  204.0 15.7 %collective-permute-start.60 = (bf16[144,1152]{1,0:T(8,128)(2,1)S(1)}, bf16[144,1152]{1,0:T(8,128)(2,1)S(1)}, u32[]{:S(2)}, u32[]{:S(2)}) collective-permute-start(bf16[144,1152]{1,0:T(8,128)(2,1)S(1)} %get-tuple-element.557), channel_id=1, source_target_pairs={{0,4},{4,0},{8,12},{12,8},{16,20},{20,16},{24,28},{28,24},{1,5},{5... | collective-permute-start | bytes 995336 | tf_op jit(solution)/shard_map/ppermute | solution.py:118
  205.0 23.4 %collective-permute-start.61 = (bf16[256,1152]{1,0:T(8,128)(2,1)S(1)}, bf16[256,1152]{1,0:T(8,128)(2,1)S(1)}, u32[]{:S(2)}, u32[]{:S(2)}) collective-permute-start(bf16[256,1152]{1,0:T(8,128)(2,1)S(1)} %get-tuple-element.562), channel_id=1, source_target_pairs={{0,2},{1,3},{2,0},{3,1},{4,6},{5,7},{6,4},{7,5},{8,10},{9,11},{10,... | collective-permute-start | bytes 1769480 | tf_op jit(solution)/shard_map/ppermute | solution.py:115
  213.0 13.1 %collective-permute-start.59 = (bf16[144,1152]{1,0:T(8,128)(2,1)S(1)}, bf16[144,1152]{1,0:T(8,128)(2,1)S(1)}, u32[]{:S(2)}, u32[]{:S(2)}) collective-permute-start(bf16[144,1152]{1,0:T(8,128)(2,1)S(1)} %get-tuple-element.556), channel_id=1, source_target_pairs={{0,8},{4,12},{8,16},{12,20},{16,24},{20,28},{24,0},{28,4},{1,9},{5... | collective-permute-start | bytes 995336 | tf_op jit(solution)/shard_map/ppermute | solution.py:121
  214.3 14.1 %collective-permute-start.63 = (bf16[144,1152]{1,0:T(8,128)(2,1)S(1)}, bf16[144,1152]{1,0:T(8,128)(2,1)S(1)}, u32[]{:S(2)}, u32[]{:S(2)}) collective-permute-start(bf16[144,1152]{1,0:T(8,128)(2,1)S(1)} %get-tuple-element.571), channel_id=1, source_target_pairs={{0,4},{4,0},{8,12},{12,8},{16,20},{20,16},{24,28},{28,24},{1,5},{5... | collective-permute-start | bytes 995336 | tf_op jit(solution)/shard_map/ppermute | solution.py:118
  219.8 13.3 %collective-permute-start.64 = (bf16[144,1152]{1,0:T(8,128)(2,1)S(1)}, bf16[144,1152]{1,0:T(8,128)(2,1)S(1)}, u32[]{:S(2)}, u32[]{:S(2)}) collective-permute-start(bf16[144,1152]{1,0:T(8,128)(2,1)S(1)} %get-tuple-element.580), channel_id=1, source_target_pairs={{0,4},{4,0},{8,12},{12,8},{16,20},{20,16},{24,28},{28,24},{1,5},{5... | collective-permute-start | bytes 995336 | tf_op jit(solution)/shard_map/ppermute | solution.py:118
  228.4 14.4 %collective-permute-start.68 = (bf16[144,1152]{1,0:T(8,128)(2,1)S(1)}, bf16[144,1152]{1,0:T(8,128)(2,1)S(1)}, u32[]{:S(2)}, u32[]{:S(2)}) collective-permute-start(bf16[144,1152]{1,0:T(8,128)(2,1)S(1)} %get-tuple-element.599), channel_id=1, source_target_pairs={{0,4},{4,0},{8,12},{12,8},{16,20},{20,16},{24,28},{28,24},{1,5},{5... | collective-permute-start | bytes 995336 | tf_op jit(solution)/shard_map/ppermute | solution.py:118
  259.6 18.4 %collective-permute-start.84 = (bf16[256,1152]{1,0:T(8,128)(2,1)S(1)}, bf16[256,1152]{1,0:T(8,128)(2,1)S(1)}, u32[]{:S(2)}, u32[]{:S(2)}) collective-permute-start(bf16[256,1152]{1,0:T(8,128)(2,1)S(1)} %get-tuple-element.647), channel_id=1, source_target_pairs={{0,2},{1,3},{2,0},{3,1},{4,6},{5,7},{6,4},{7,5},{8,10},{9,11},{10,... | collective-permute-start | bytes 1769480 | tf_op jit(solution)/shard_map/ppermute | solution.py:115
  260.9 13.4 %collective-permute-start.81 = (bf16[144,1152]{1,0:T(8,128)(2,1)S(1)}, bf16[144,1152]{1,0:T(8,128)(2,1)S(1)}, u32[]{:S(2)}, u32[]{:S(2)}) collective-permute-start(bf16[144,1152]{1,0:T(8,128)(2,1)S(1)} %get-tuple-element.635), channel_id=1, source_target_pairs={{0,4},{4,0},{8,12},{12,8},{16,20},{20,16},{24,28},{28,24},{1,5},{5... | collective-permute-start | bytes 995336 | tf_op jit(solution)/shard_map/ppermute | solution.py:118
  280.0 17.7 %collective-permute-start.92 = (f32[128,1152]{1,0:T(8,128)}, f32[128,1152]{1,0:T(8,128)S(1)}, u32[]{:S(2)}, u32[]{:S(2)}) collective-permute-start(f32[128,1152]{1,0:T(8,128)} %get-tuple-element.665), channel_id=1, source_target_pairs={{0,1},{1,0},{2,3},{3,2},{4,5},{5,4},{6,7},{7,6},{8,9},{9,8},{10,11... | collective-permute-start | bytes 1769480 | tf_op jit(solution)/shard_map/ppermute | solution.py:112
  (71 other events, 555.3 us)

commit v4 on v3

--- a/solution.py
+++ b/solution.py
@@ -162,18 +162,17 @@
             self.copies += arrived[count:]
             self.send(arrived[:count])
 
-    def finish(self, widths, head=0, keep_head=False):
+    def finish(self, widths, keep_rest=False):
         while self.pending:
             self.turn()
-        return self.place(self.pieces, widths, head, keep_head)
-
-    def finish_near(self, widths, head=0):
-        return self.place(self.copies + [self.order.wait(*self.copied)], widths, head, False)
-
-    def place(self, pieces, widths, head, keep_head):
+        return self.place(self.pieces, widths, keep_rest)
+
+    def finish_near(self, widths):
+        return self.place(self.copies + [self.order.wait(*self.copied)], widths, False)
+
+    def place(self, pieces, widths, keep_rest):
         shards = self.here.shards
         rows, total = pieces[0].shape
-        rows -= head
 
         def kernel(place, *refs):
             targets = refs[shards:]
@@ -181,14 +180,14 @@
                 shard = piece_shard(place, index, shards)
                 start = 0
                 for target, columns in zip(targets, widths):
-                    target[shard] = refs[index][head:, start : start + columns]
+                    target[shard] = refs[index][:, start : start + columns]
                     start += columns
-                if keep_head:
-                    targets[-1][shard] = refs[index][:head, :]
+                if keep_rest:
+                    targets[-1][shard] = refs[index][:, start:]
 
         outs = [struct((shards, rows, columns), pieces[0].dtype) for columns in widths]
-        if keep_head:
-            outs.append(struct((shards, head, total), pieces[0].dtype))
+        if keep_rest:
+            outs.append(struct((shards, rows, total - sum(widths)), pieces[0].dtype))
         return self.order.run(kernel, outs, *pieces)
 
 
@@ -287,35 +286,37 @@
     rows, width = out_weight.shape
     columns = qkv_weight.shape[1] // 4
     total = columns + width // 2
+    lanes = -total % 128
     micros = condition.shape[0]
 
     def kernel(place, condition_ref, biases_ref, qkv_ref, out_ref, target, held):
         held[...] = jnp.zeros(held.shape, jnp.float32)
-        held[:micros, :width] = wide(condition_ref[...])
-        for row, start in enumerate(range(0, biases.shape[1], total)):
-            count = min(total, biases.shape[1] - start)
-            held[micros + row : micros + row + 1, :count] = wide(
-                biases_ref[:, start : start + count]
-            )
-        target[:HEAD, :] = low(held[...])
-        rest = target.at[HEAD:, :]
-        cut_columns(place, qkv_ref, rest, 0, place[SEAT], 4, 3)
-        cut_columns(place, out_ref, rest, columns, place[CORE], 2, 1)
+        row = 0
+        for source, index in [(condition_ref, micro) for micro in range(micros)] + [(biases_ref, 0)]:
+            size = source.shape[1]
+            for start in range(0, size, lanes):
+                count = min(lanes, size - start)
+                held[row : row + 1, :count] = wide(source[index : index + 1, start : start + count])
+                row += 1
+        target[:, total:] = low(held[...])
+        cut_columns(place, qkv_ref, target, 0, place[SEAT], 4, 3)
+        cut_columns(place, out_ref, target, columns, place[CORE], 2, 1)
 
     return order.run(
         kernel,
-        [struct((HEAD + rows, total), qkv_weight.dtype)],
+        [struct((rows, total + lanes), qkv_weight.dtype)],
         condition,
         biases,
         qkv_weight,
         out_weight,
-        scratch=(pltpu.VMEM((HEAD, total), jnp.float32),),
+        scratch=(pltpu.VMEM((rows, lanes), jnp.float32),),
     )
 
 
 def modulation_parts(order, heads, mod_weight, micros, width, hidden):
-    shards, head, total = heads.shape
+    shards, _, lanes = heads.shape
     rows, columns = mod_weight.shape
+    share_rows = width // lanes
     part = H // 4 * HD
     block = hidden // shards // 4
     sizes = {"mod": columns, "qv": 2 * width, "out": width, "up": hidden, "down": width}
@@ -325,9 +326,15 @@
         parts, (cond, mine, products) = refs[8:-3], refs[-3:]
         shard = 2 * place[LINE] + place[PAIR]
         for index in range(shards):
-            values = wide(heads_ref[index, :micros, :width])
-            values = wide(low(values / (1.0 + jnp.exp(-values))))
-            cond[index * micros : (index + 1) * micros, :] = values
+            for micro in range(micros):
+                goal = index * micros + micro
+                for part_row in range(share_rows):
+                    source = micro * share_rows + part_row
+                    cond[goal : goal + 1, part_row * lanes : (part_row + 1) * lanes] = wide(
+                        heads_ref[index, source : source + 1, :]
+                    )
+        values = cond[...]
+        cond[...] = wide(low(values / (1.0 + jnp.exp(-values))))
         for index in range(shards):
 
             @pl.when(shard == index)
@@ -351,9 +358,10 @@
             share = sizes[name] // shards
             while count > 0:
                 index, offset = divmod(start, share)
-                line, lane = divmod(base + offset, total)
-                length = min(count, share - offset, total - lane)
-                source = heads_ref[index, micros + line : micros + line + 1, lane : lane + length]
+                line, lane = divmod(base + offset, lanes)
+                line += micros * share_rows
+                length = min(count, share - offset, lanes - lane)
+                source = heads_ref[index, line : line + 1, lane : lane + length]
                 target[row : row + 1, column : column + length] = wide(source)
                 start, column, count = start + length, column + length, count - length
 
@@ -1159,7 +1167,7 @@
     lats = (lat_mine, lat_near, lat_far, lat_far_near)
     ring.turn()
     feed_ring = Gather(here, order, wait(feed_piece), hold=True)
-    qkv_mine, out_mine, heads_all = ring.finish(attention_widths, HEAD, True)
+    qkv_mine, out_mine, heads_all = ring.finish(attention_widths, True)
     feed_ring.release()
     (
         cond_rows,
@@ -1176,7 +1184,7 @@
     mod_sum.join()
     mod_parts = mod_sum.finish()
     feed_ring.turn()
-    qkv_near, out_near = ring.finish_near(attention_widths, HEAD)
+    qkv_near, out_near = ring.finish_near(attention_widths)
     mod, attn_in, attn_turned, means_one, inverses_one = norm_tokens(
         order, lats, mod_parts, mod_bias
     )

time: 306 us -> 305 us (level)
  starting transfers between devices: 77.4 us -> 66.4 us
  waiting for transfers between devices: 98.8 us -> 108 us
    ppermute x24, starting transfers between devices: 29.9 us -> 21.1 us  [to_line(): lax.ppermute(values, 'fsdp', [(i, (i + 2 * step) % self.shards) for i in...]
    ppermute x13, starting transfers between devices: 16.9 us -> 13 us  [to_side(): return lax.ppermute(values, 'seq', [(i, i ^ 2) for i in range(self.seats)])]
    ppermute x24, waiting for transfers between devices: 30.4 us -> 34.3 us  [to_line(): lax.ppermute(values, 'fsdp', [(i, (i + 2 * step) % self.shards) for i in...]
    ppermute x23, waiting for transfers between devices: 34.9 us -> 38.4 us  [to_pair(): lax.ppermute(values, 'fsdp', [(i, i ^ 1) for i in range(self.shards)])]
  transfers between devices with their start and end apart: 94 -> 94, of which waited for: 34 -> 35; matrix products, arithmetic and copies ran while one was open for 2% -> 2% of each run, Pallas kernels for 32% -> 32%
where the time goes in v4:
time: 305 us; the launch traced here: 300 us
  Pallas kernels  111 us (36%)
  waiting for transfers between devices  108 us (35%)
  starting transfers between devices  66.4 us (22%)
  local copies, waits for them, and re-layouts  8.65 us (3%)
    pallas_call x54, Pallas kernels, run(): pl.pallas_call(body, out_shape=tuple(outs) + (struct(self.token.shape, se...  111 us
    ppermute x23, waiting for transfers between devices, to_pair(): lax.ppermute(values, 'fsdp', [(i, i ^ 1) for i in range(self.shards)])  38.4 us
    ppermute x24, waiting for transfers between devices, to_line(): lax.ppermute(values, 'fsdp', [(i, (i + 2 * step) % self.shards) for i in...  34.3 us
    ppermute x13, waiting for transfers between devices, to_side(): return lax.ppermute(values, 'seq', [(i, i ^ 2) for i in range(self.seats)])  32.3 us
    ppermute x23, starting transfers between devices, to_pair(): lax.ppermute(values, 'fsdp', [(i, i ^ 1) for i in range(self.shards)])  24.9 us
    ppermute x24, starting transfers between devices, to_line(): lax.ppermute(values, 'fsdp', [(i, (i + 2 * step) % self.shards) for i in...  21.1 us
    ppermute x13, starting transfers between devices, to_side(): return lax.ppermute(values, 'seq', [(i, i ^ 2) for i in range(self.seats)])  13 us
    ppermute x34, starting transfers between devices, to_core(): return lax.ppermute(values, 'seq', [(i, i ^ 1) for i in range(self.seats)])  7.27 us
  transfers between devices with their start and end apart: 94, of which 35 were waited for; matrix products, arithmetic and copies ran while one was open for 2% of the time, Pallas kernels for 32%

profile of v4, /device:TPU:0, one launch (start us, length us, event | category | flops | bytes accessed | tf_op | source)
XLA Modules:
  0.0 300.2 jit_solution(8585534074606685112)
XLA Ops:
  0.7 3.6 %concatenate.3 = bf16[2016]{0:T(1024)(128)(2,1)S(1)} concatenate(bf16[864]{0:T(1024)(128)(2,1)} %param.16, bf16[288]{0:T(512)(128)(2,1)} %param.18, bf16[144]{0:T(256)(128)(2,1)} %param.20, bf16[576]{0:T(1024)(128)(2,1)} %param.22, bf16[144]{0:T(256)(128)(2,1)} %param.24), dimensions={0} | concatenate | bytes 8064 | tf_op jit(solution)/shard_map/concatenate | solution.py:1152
  8.3 3.1 %collective-permute-start = (bf16[144,1536]{1,0:T(8,128)(2,1)S(1)}, bf16[144,1536]{1,0:T(8,128)(2,1)S(1)}, u32[]{:S(2)}, u32[]{:S(2)}) collective-permute-start(bf16[144,1536]{1,0:T(8,128)(2,1)S(1)} %get-tuple-element.350.refs_0_), channel_id=1, source_target_pairs={{0,8},{4,12},{8,16},{12,20},{16,24},{20,28},{24,0},{28,4},{1,9},{5... | collective-permute-start | bytes 1327112 | tf_op jit(solution)/shard_map/ppermute | solution.py:121
  17.7 5.9 %collective-permute-done.refs_1_ = bf16[144,1536]{1,0:T(8,128)(2,1)S(1)} collective-permute-done((bf16[144,1536]{1,0:T(8,128)(2,1)S(1)}, bf16[144,1536]{1,0:T(8,128)(2,1)S(1)}, u32[]{:S(2)}, u32[]{:S(2)}) %collective-permute-start) | collective-permute-done | bytes 442400 | tf_op jit(solution)/shard_map/ppermute | solution.py:121
  27.2 4.6 %collective-permute-done.5.refs_5_.refs_9_.refs_6_ = bf16[128,1152]{1,0:T(8,128)(2,1)S(1)} collective-permute-done((bf16[128,1152]{1,0:T(8,128)(2,1)S(1)}, bf16[128,1152]{1,0:T(8,128)(2,1)S(1)}, u32[]{:S(2)}, u32[]{:S(2)}) %collective-permute-start.5) | collective-permute-done | bytes 294944 | tf_op jit(solution)/shard_map/ppermute | solution.py:115
  33.1 4.7 %collective-permute-done.6.refs_3_ = bf16[144,1536]{1,0:T(8,128)(2,1)S(1)} collective-permute-done((bf16[144,1536]{1,0:T(8,128)(2,1)S(1)}, bf16[144,1536]{1,0:T(8,128)(2,1)S(1)}, u32[]{:S(2)}, u32[]{:S(2)}) %collective-permute-start.6) | collective-permute-done | bytes 442400 | tf_op jit(solution)/shard_map/ppermute | solution.py:121
  40.5 8.4 %collective-permute-done.11.refs_6_.refs_10_.refs_7_ = bf16[128,1152]{1,0:T(8,128)(2,1)S(1)} collective-permute-done((bf16[128,1152]{1,0:T(8,128)(2,1)S(1)}, bf16[128,1152]{1,0:T(8,128)(2,1)S(1)}, u32[]{:S(2)}, u32[]{:S(2)}) %collective-permute-start.11) | collective-permute-done | bytes 294944 | tf_op jit(solution)/shard_map/ppermute | solution.py:115
  51.7 8.5 %collective-permute-done.16.refs_7_ = bf16[144,1536]{1,0:T(8,128)(2,1)S(1)} collective-permute-done((bf16[144,1536]{1,0:T(8,128)(2,1)S(1)}, bf16[144,1536]{1,0:T(8,128)(2,1)S(1)}, u32[]{:S(2)}, u32[]{:S(2)}) %collective-permute-start.16) | collective-permute-done | bytes 442400 | tf_op jit(solution)/shard_map/ppermute | solution.py:118
  64.3 3.7 %collective-permute-start.20 = (f32[2,6912]{1,0:T(2,128)S(1)}, f32[2,6912]{1,0:T(2,128)S(1)}, u32[]{:S(2)}, u32[]{:S(2)}) collective-permute-start(f32[2,6912]{1,0:T(2,128)S(1)} %get-tuple-element.383), channel_id=1, source_target_pairs={{0,16},{4,20},{8,24},{12,28},{16,0},{20,4},{24,8},{28,12},{1,17},{... | collective-permute-start | bytes 165896 | tf_op jit(solution)/shard_map/ppermute | solution.py:121
  68.8 3.8 %collective-permute-done.19.refs_1_ = f32[2,6912]{1,0:T(2,128)S(1)} collective-permute-done((f32[2,6912]{1,0:T(2,128)S(1)}, f32[2,6912]{1,0:T(2,128)S(1)}, u32[]{:S(2)}, u32[]{:S(2)}) %collective-permute-start.19) | collective-permute-done | bytes 55328 | tf_op jit(solution)/shard_map/ppermute | solution.py:121
  75.1 3.4 %collective-permute-done.22.refs_0_ = f32[1,6912]{1,0:T(1,128)S(1)} collective-permute-done((f32[1,6912]{1,0:T(1,128)S(1)}, f32[1,6912]{1,0:T(1,128)S(1)}, u32[]{:S(2)}, u32[]{:S(2)}) %collective-permute-start.22) | collective-permute-done | bytes 27680 | tf_op jit(solution)/shard_map/ppermute | solution.py:118
  83.9 4.3 %shard_map.237 = (bf16[12,72,512]{2,1,0:T(8,128)(2,1)S(1)}, bf16[288,512]{1,0:T(8,128)(2,1)S(1)}, f32[8,128]{1,0:T(8,128)S(1)}) custom-call(s32[4]{0:T(128)S(1)} %pad_add_fusion.place, bf16[512,1152]{1,0:T(8,128)(2,1)S(1)} %get-tuple-element.409.refs_0_, bf16[1152,864]{1,0:T(8,128)(2,1)S(1)} %bitcast.26, ...), custom_call_target="tpu_custom_call", output_to_operand_aliasing={{2}: (4, {})} | custom-call | flops 1 | bytes 1 | tf_op jit(solution)/shard_map/pallas_call | solution.py:85
  89.3 4.3 %shard_map.238 = (bf16[12,72,512]{2,1,0:T(8,128)(2,1)S(1)}, bf16[288,512]{1,0:T(8,128)(2,1)S(1)}, f32[8,128]{1,0:T(8,128)S(1)}) custom-call(s32[4]{0:T(128)S(1)} %pad_add_fusion.place, bf16[512,1152]{1,0:T(8,128)(2,1)S(1)} %get-tuple-element.409.refs_0_, bf16[1152,864]{1,0:T(8,128)(2,1)S(1)} %bitcast.28, ...), custom_call_target="tpu_custom_call", output_to_operand_aliasing={{2}: (4, {})} | custom-call | flops 1 | bytes 1 | tf_op jit(solution)/shard_map/pallas_call | solution.py:85
  99.5 7.2 %collective-permute-done.29.refs_3_ = bf16[288,512]{1,0:T(8,128)(2,1)S(1)} collective-permute-done((bf16[288,512]{1,0:T(8,128)(2,1)S(1)}, bf16[288,512]{1,0:T(8,128)(2,1)S(1)}, u32[]{:S(2)}, u32[]{:S(2)}) %collective-permute-start.29) | collective-permute-done | bytes 294944 | tf_op jit(solution)/shard_map/ppermute | solution.py:115
  106.6 3.8 %shard_map.239 = (bf16[1152,512]{1,0:T(8,128)(2,1)S(1)}, bf16[1152,1152]{1,0:T(8,128)(2,1)S(1)}, f32[256,1152]{1,0:T(8,128)S(1)}, f32[512,1152]{1,0:T(8,128)S(1)...) custom-call(s32[4]{0:T(128)S(1)} %pad_add_fusion.place, ...), custom_call_target="tpu_custom_call", output_to_operand_aliasing={{6}: (13, {})} | custom-call | flops 1 | bytes 1 | tf_op jit(solution)/shard_map/pallas_call | solution.py:85
  113.1 13.2 %collective-permute-done.33.refs_7_ = bf16[144,2304]{1,0:T(8,128)(2,1)S(1)} collective-permute-done((bf16[144,2304]{1,0:T(8,128)(2,1)S(1)}, bf16[144,2304]{1,0:T(8,128)(2,1)S(1)}, u32[]{:S(2)}, u32[]{:S(2)}) %collective-permute-start.33) | collective-permute-done | bytes 663584 | tf_op jit(solution)/shard_map/ppermute | solution.py:118
  127.8 4.9 %shard_map.242 = (bf16[512,1152]{1,0:T(8,128)(2,1)S(1)}, f32[512,1152]{1,0:T(8,128)S(1)}, f32[8,128]{1,0:T(8,128)S(1)}) custom-call(s32[4]{0:T(128)S(1)} %pad_add_fusion.place, bf16[512,1152]{1,0:T(8,128)(2,1)S(1)} %get-tuple-element.429.refs_0_, bf16[1152,1152]{1,0:T(8,128)(2,1)S(1)} %bitcast.18, ...), custom_call_target="tpu_custom_call", output_to_operand_aliasing={{2}: (4, {})} | custom-call | flops 1 | bytes 1 | tf_op jit(solution)/shard_map/pallas_call | solution.py:85
  132.7 3.4 %shard_map.243 = (bf16[512,1152]{1,0:T(8,128)(2,1)S(1)}, f32[1,1152]{1,0:T(1,128)S(1)}, f32[8,128]{1,0:T(8,128)S(1)}) custom-call(s32[4]{0:T(128)S(1)} %pad_add_fusion.place, bf16[512,1152]{1,0:T(8,128)(2,1)S(1)} %get-tuple-element.449.refs_0_.refs_1_, bf16[1152,1152]{1,0:T(8,128)(2,1)S(1)} %bitcast.22, ...), custom_call_target="tpu_custom_call", output_to_operand_aliasing={{2}: (4, {})} | custom-call | flops 1 | bytes 1 | tf_op jit(solution)/shard_map/pallas_call | solution.py:85
  136.1 4.5 %shard_map.244 = (bf16[512,1152]{1,0:T(8,128)(2,1)S(1)}, f32[512,1152]{1,0:T(8,128)S(1)}, f32[8,128]{1,0:T(8,128)S(1)}) custom-call(s32[4]{0:T(128)S(1)} %pad_add_fusion.place, bf16[512,1152]{1,0:T(8,128)(2,1)S(1)} %get-tuple-element.429.refs_0_, bf16[1152,1152]{1,0:T(8,128)(2,1)S(1)} %bitcast.20, ...), custom_call_target="tpu_custom_call", output_to_operand_aliasing={{2}: (4, {})} | custom-call | flops 1 | bytes 1 | tf_op jit(solution)/shard_map/pallas_call | solution.py:85
  140.6 3.4 %shard_map.245 = (bf16[512,1152]{1,0:T(8,128)(2,1)S(1)}, f32[1,1152]{1,0:T(1,128)S(1)}, f32[8,128]{1,0:T(8,128)S(1)}) custom-call(s32[4]{0:T(128)S(1)} %pad_add_fusion.place, bf16[512,1152]{1,0:T(8,128)(2,1)S(1)} %get-tuple-element.449.refs_0_.refs_1_, bf16[1152,1152]{1,0:T(8,128)(2,1)S(1)} %bitcast.24, ...), custom_call_target="tpu_custom_call", output_to_operand_aliasing={{2}: (4, {})} | custom-call | flops 1 | bytes 1 | tf_op jit(solution)/shard_map/pallas_call | solution.py:85
  144.0 5.1 %shard_map.246 = (bf16[512,1152]{1,0:T(8,128)(2,1)S(1)}, f32[8,128]{1,0:T(8,128)S(1)}) custom-call(s32[4]{0:T(128)S(1)} %pad_add_fusion.place, bf16[512,1152]{1,0:T(8,128)(2,1)S(1)} %get-tuple-element.462.refs_0_.refs_1_, bf16[1152,1152]{1,0:T(8,128)(2,1)S(1)} %bitcast.19, ...), custom_call_target="tpu_custom_call", output_to_operand_aliasing={{1}: (5, {})} | custom-call | flops 1 | bytes 1 | tf_op jit(solution)/shard_map/pallas_call | solution.py:85
  164.8 4.8 %collective-permute-done.40.refs_1_ = bf16[144,1152]{1,0:T(8,128)(2,1)S(1)} collective-permute-done((bf16[144,1152]{1,0:T(8,128)(2,1)S(1)}, bf16[144,1152]{1,0:T(8,128)(2,1)S(1)}, u32[]{:S(2)}, u32[]{:S(2)}) %collective-permute-start.40) | collective-permute-done | bytes 331808 | tf_op jit(solution)/shard_map/ppermute | solution.py:118
  170.6 5.6 %shard_map.252 = (f32[256,1152]{1,0:T(8,128)S(1)}, bf16[256,1152]{1,0:T(8,128)(2,1)S(1)}, f32[8,128]{1,0:T(8,128)S(1)}) custom-call(s32[4]{0:T(128)S(1)} %pad_add_fusion.place, bf16[512,1152]{1,0:T(8,128)(2,1)S(1)} %get-tuple-element.447.refs_0_, bf16[1152,1152]{1,0:T(8,128)(2,1)S(1)} %bitcast.23, ...), custom_call_target="tpu_custom_call", output_to_operand_aliasing={{2}: (5, {})} | custom-call | flops 1 | bytes 1 | tf_op jit(solution)/shard_map/pallas_call | solution.py:85
  178.6 4.1 %collective-permute-done.42.refs_1_ = bf16[512,1152]{1,0:T(8,128)(2,1)S(1)} collective-permute-done((bf16[512,1152]{1,0:T(8,128)(2,1)S(1)}, bf16[512,1152]{1,0:T(8,128)(2,1)S(1)}, u32[]{:S(2)}, u32[]{:S(2)}) %collective-permute-start.42) | collective-permute-done | bytes 1179680 | tf_op jit(solution)/shard_map/ppermute | solution.py:115
  186.2 5.8 %shard_map.256 = (bf16[512,864]{1,0:T(8,128)(2,1)S(1)}, f32[1,864]{1,0:T(1,128)S(1)}, f32[8,128]{1,0:T(8,128)S(1)}) custom-call(s32[4]{0:T(128)S(1)} %pad_add_fusion.place, bf16[12,72,512]{2,1,0:T(8,128)(2,1)S(1)} %get-tuple-element.503.refs_0_, bf16[1152,1152]{1,0:T(8,128)(2,1)S(1)} %get-tuple-element.489.refs_1_, ...), custom_call_target="tpu_custom_call", output_to_operand_aliasing={{2}: (4, {})} | custom-call | flops 1 | bytes 1 | tf_op jit(solution)/shard_map/pallas_call | solution.py:85
  192.7 2.8 shard_map.258
  203.2 5.8 %shard_map.259 = (bf16[512,864]{1,0:T(8,128)(2,1)S(1)}, f32[1,864]{1,0:T(1,128)S(1)}, f32[8,128]{1,0:T(8,128)S(1)}) custom-call(s32[4]{0:T(128)S(1)} %pad_add_fusion.place, bf16[12,72,512]{2,1,0:T(8,128)(2,1)S(1)} %get-tuple-element.488.refs_0_, bf16[1152,1152]{1,0:T(8,128)(2,1)S(1)} %get-tuple-element.489.refs_1_, ...), custom_call_target="tpu_custom_call", output_to_operand_aliasing={{2}: (4, {})} | custom-call | flops 1 | bytes 1 | tf_op jit(solution)/shard_map/pallas_call | solution.py:85
  213.7 2.9 shard_map.261
  220.8 4.5 %collective-permute-done.59.refs_1_ = bf16[144,1152]{1,0:T(8,128)(2,1)S(1)} collective-permute-done((bf16[144,1152]{1,0:T(8,128)(2,1)S(1)}, bf16[144,1152]{1,0:T(8,128)(2,1)S(1)}, u32[]{:S(2)}, u32[]{:S(2)}) %collective-permute-start.59) | collective-permute-done | bytes 331808 | tf_op jit(solution)/shard_map/ppermute | solution.py:121
  234.3 4.5 %shard_map.267 = (f32[256,1152]{1,0:T(8,128)S(1)}, bf16[256,1152]{1,0:T(8,128)(2,1)S(1)}, f32[2,1152]{1,0:T(2,128)S(1)}, f32[8,128]{1,0:T(8,128)S(1)}) custom-call(s32[4]{0:T(128)S(1)} %pad_add_fusion.place, bf16[512,864]{1,0:T(8,128)(2,1)S(1)} %get-tuple-element.532.refs_1_.refs_0_, ...), custom_call_target="tpu_custom_call", output_to_operand_aliasing={{3}: (11, {})} | custom-call | flops 1 | bytes 1 | tf_op jit(solution)/shard_map/pallas_call | solution.py:85
  249.2 4.0 %collective-permute-start.76 = (bf16[16,1152]{1,0:T(8,128)(2,1)S(1)}, bf16[16,1152]{1,0:T(8,128)(2,1)S(1)}, u32[]{:S(2)}, u32[]{:S(2)}) collective-permute-start(bf16[16,1152]{1,0:T(8,128)(2,1)S(1)} %get-tuple-element.610.refs_0_), channel_id=1, source_target_pairs={{0,16},{4,20},{8,24},{12,28},{16,0},{20,4},{24,8},{28,12},{1,17},{... | collective-permute-start | bytes 110600 | tf_op jit(solution)/shard_map/ppermute | solution.py:121
  265.8 7.4 %collective-permute-done.79.refs_2_ = bf16[4,16,1152]{2,1,0:T(8,128)(2,1)S(1)} collective-permute-done((bf16[4,16,1152]{2,1,0:T(8,128)(2,1)S(1)}, bf16[4,16,1152]{2,1,0:T(8,128)(2,1)S(1)}, u32[]{:S(2)}, u32[]{:S(2)}) %collective-permute-start.79) | collective-permute-done | bytes 147488 | tf_op jit(solution)/shard_map/ppermute | solution.py:118
  281.5 2.7 collective-permute-done.85.refs_2_
  (236 shorter events, 139.6 us)
Async XLA Ops:
  8.3 15.3 %collective-permute-start = (bf16[144,1536]{1,0:T(8,128)(2,1)S(1)}, bf16[144,1536]{1,0:T(8,128)(2,1)S(1)}, u32[]{:S(2)}, u32[]{:S(2)}) collective-permute-start(bf16[144,1536]{1,0:T(8,128)(2,1)S(1)} %get-tuple-element.350.refs_0_), channel_id=1, source_target_pairs={{0,8},{4,12},{8,16},{12,20},{16,24},{20,28},{24,0},{28,4},{1,9},{5... | collective-permute-start | bytes 1327112 | tf_op jit(solution)/shard_map/ppermute | solution.py:121
  11.4 13.8 %collective-permute-start.1 = (bf16[144,1536]{1,0:T(8,128)(2,1)S(1)}, bf16[144,1536]{1,0:T(8,128)(2,1)S(1)}, u32[]{:S(2)}, u32[]{:S(2)}) collective-permute-start(bf16[144,1536]{1,0:T(8,128)(2,1)S(1)} %get-tuple-element.350.refs_0_), channel_id=1, source_target_pairs={{0,4},{4,0},{8,12},{12,8},{16,20},{20,16},{24,28},{28,24},{1,5},{5... | collective-permute-start | bytes 1327112 | tf_op jit(solution)/shard_map/ppermute | solution.py:118
  25.1 12.7 %collective-permute-start.6 = (bf16[144,1536]{1,0:T(8,128)(2,1)S(1)}, bf16[144,1536]{1,0:T(8,128)(2,1)S(1)}, u32[]{:S(2)}, u32[]{:S(2)}) collective-permute-start(bf16[144,1536]{1,0:T(8,128)(2,1)S(1)} %collective-permute-done.refs_1_), channel_id=1, source_target_pairs={{0,8},{4,12},{8,16},{12,20},{16,24},{20,28},{24,0},{28,4},{1,9},{5... | collective-permute-start | bytes 1327112 | tf_op jit(solution)/shard_map/ppermute | solution.py:121
  25.1 12.7 %collective-permute-start.7 = (bf16[144,1536]{1,0:T(8,128)(2,1)S(1)}, bf16[144,1536]{1,0:T(8,128)(2,1)S(1)}, u32[]{:S(2)}, u32[]{:S(2)}) collective-permute-start(bf16[144,1536]{1,0:T(8,128)(2,1)S(1)} %collective-permute-done.refs_1_), channel_id=1, source_target_pairs={{0,4},{4,0},{8,12},{12,8},{16,20},{20,16},{24,28},{28,24},{1,5},{5... | collective-permute-start | bytes 1327112 | tf_op jit(solution)/shard_map/ppermute | solution.py:118
  51.7 26.8 %collective-permute-start.23 = (bf16[144,2304]{1,0:T(8,128)(2,1)S(1)}, bf16[144,2304]{1,0:T(8,128)(2,1)S(1)}, u32[]{:S(2)}, u32[]{:S(2)}) collective-permute-start(bf16[144,2304]{1,0:T(8,128)(2,1)S(1)} %get-tuple-element.404.refs_0_), channel_id=1, source_target_pairs={{0,8},{4,12},{8,16},{12,20},{16,24},{20,28},{24,0},{28,4},{1,9},{5... | collective-permute-start | bytes 1990664 | tf_op jit(solution)/shard_map/ppermute | solution.py:121
  61.7 16.8 %collective-permute-start.24 = (bf16[144,2304]{1,0:T(8,128)(2,1)S(1)}, bf16[144,2304]{1,0:T(8,128)(2,1)S(1)}, u32[]{:S(2)}, u32[]{:S(2)}) collective-permute-start(bf16[144,2304]{1,0:T(8,128)(2,1)S(1)} %get-tuple-element.404.refs_0_), channel_id=1, source_target_pairs={{0,4},{4,0},{8,12},{12,8},{16,20},{20,16},{24,28},{28,24},{1,5},{5... | collective-permute-start | bytes 1990664 | tf_op jit(solution)/shard_map/ppermute | solution.py:118
  78.5 17.6 %collective-permute-start.27 = (bf16[144,2304]{1,0:T(8,128)(2,1)S(1)}, bf16[144,2304]{1,0:T(8,128)(2,1)S(1)}, u32[]{:S(2)}, u32[]{:S(2)}) collective-permute-start(bf16[144,2304]{1,0:T(8,128)(2,1)S(1)} %collective-permute-done.23.refs_1_), channel_id=1, source_target_pairs={{0,8},{4,12},{8,16},{12,20},{16,24},{20,28},{24,0},{28,4},{1,9},{5... | collective-permute-start | bytes 1990664 | tf_op jit(solution)/shard_map/ppermute | solution.py:121
  80.4 15.7 %collective-permute-start.28 = (bf16[144,2304]{1,0:T(8,128)(2,1)S(1)}, bf16[144,2304]{1,0:T(8,128)(2,1)S(1)}, u32[]{:S(2)}, u32[]{:S(2)}) collective-permute-start(bf16[144,2304]{1,0:T(8,128)(2,1)S(1)} %collective-permute-done.23.refs_1_), channel_id=1, source_target_pairs={{0,4},{4,0},{8,12},{12,8},{16,20},{20,16},{24,28},{28,24},{1,5},{5... | collective-permute-start | bytes 1990664 | tf_op jit(solution)/shard_map/ppermute | solution.py:118
  96.1 16.5 %collective-permute-start.31 = (bf16[144,2304]{1,0:T(8,128)(2,1)S(1)}, bf16[144,2304]{1,0:T(8,128)(2,1)S(1)}, u32[]{:S(2)}, u32[]{:S(2)}) collective-permute-start(bf16[144,2304]{1,0:T(8,128)(2,1)S(1)} %collective-permute-done.27.refs_3_), channel_id=1, source_target_pairs={{0,8},{4,12},{8,16},{12,20},{16,24},{20,28},{24,0},{28,4},{1,9},{5... | collective-permute-start | bytes 1990664 | tf_op jit(solution)/shard_map/ppermute | solution.py:121
  96.1 16.4 %collective-permute-start.32 = (bf16[144,2304]{1,0:T(8,128)(2,1)S(1)}, bf16[144,2304]{1,0:T(8,128)(2,1)S(1)}, u32[]{:S(2)}, u32[]{:S(2)}) collective-permute-start(bf16[144,2304]{1,0:T(8,128)(2,1)S(1)} %collective-permute-done.27.refs_3_), channel_id=1, source_target_pairs={{0,4},{4,0},{8,12},{12,8},{16,20},{20,16},{24,28},{28,24},{1,5},{5... | collective-permute-start | bytes 1990664 | tf_op jit(solution)/shard_map/ppermute | solution.py:118
  98.0 12.5 %collective-permute-start.30 = (bf16[128,1152]{1,0:T(8,128)(2,1)S(1)}, bf16[128,1152]{1,0:T(8,128)(2,1)S(1)}, u32[]{:S(2)}, u32[]{:S(2)}) collective-permute-start(bf16[128,1152]{1,0:T(8,128)(2,1)S(1)} %collective-permute-done.4.refs_1_.refs_5_.refs_7_), channel_id=1, source_target_pairs={{0,2},{1,3},{2,0},{3,1},{4,6},{5,7},{6,4},{7,5},{8,10},{9,11},{10,... | collective-permute-start | bytes 884744 | tf_op jit(solution)/shard_map/ppermute | solution.py:115
  112.6 13.7 %collective-permute-start.33 = (bf16[144,2304]{1,0:T(8,128)(2,1)S(1)}, bf16[144,2304]{1,0:T(8,128)(2,1)S(1)}, u32[]{:S(2)}, u32[]{:S(2)}) collective-permute-start(bf16[144,2304]{1,0:T(8,128)(2,1)S(1)} %collective-permute-done.31.refs_5_), channel_id=1, source_target_pairs={{0,4},{4,0},{8,12},{12,8},{16,20},{20,16},{24,28},{28,24},{1,5},{5... | collective-permute-start | bytes 1990664 | tf_op jit(solution)/shard_map/ppermute | solution.py:118
  127.3 13.3 %collective-permute-start.35 = (bf16[8,144,1152]{2,1,0:T(8,128)(2,1)S(1)}, bf16[8,144,1152]{2,1,0:T(8,128)(2,1)S(1)}, u32[]{:S(2)}, u32[]{:S(2)}) collective-permute-start(bf16[8,144,1152]{2,1,0:T(8,128)(2,1)S(1)} %get-tuple-element.448), channel_id=1, source_target_pairs={{0,1},{1,0},{2,3},{3,2},{4,5},{5,4},{6,7},{7,6},{8,9},{9,8},{10,11... | collective-permute-start | bytes 7962632 | tf_op jit(solution)/shard_map/ppermute | solution.py:112
  154.8 28.0 %collective-permute-start.42 = (bf16[512,1152]{1,0:T(8,128)(2,1)S(1)}, bf16[512,1152]{1,0:T(8,128)(2,1)S(1)}, u32[]{:S(2)}, u32[]{:S(2)}) collective-permute-start(bf16[512,1152]{1,0:T(8,128)(2,1)S(1)} %get-tuple-element.490.refs_0_), channel_id=1, source_target_pairs={{0,2},{1,3},{2,0},{3,1},{4,6},{5,7},{6,4},{7,5},{8,10},{9,11},{10,... | collective-permute-start | bytes 3538952 | tf_op jit(solution)/shard_map/ppermute | solution.py:115
  162.7 14.0 %collective-permute-start.41 = (bf16[144,1152]{1,0:T(8,128)(2,1)S(1)}, bf16[144,1152]{1,0:T(8,128)(2,1)S(1)}, u32[]{:S(2)}, u32[]{:S(2)}) collective-permute-start(bf16[144,1152]{1,0:T(8,128)(2,1)S(1)} %get-tuple-element.493), channel_id=1, source_target_pairs={{0,4},{4,0},{8,12},{12,8},{16,20},{20,16},{24,28},{28,24},{1,5},{5... | collective-permute-start | bytes 995336 | tf_op jit(solution)/shard_map/ppermute | solution.py:118
  163.6 22.0 %collective-permute-start.44 = (bf16[144,1152]{1,0:T(8,128)(2,1)S(1)}, bf16[144,1152]{1,0:T(8,128)(2,1)S(1)}, u32[]{:S(2)}, u32[]{:S(2)}) collective-permute-start(bf16[144,1152]{1,0:T(8,128)(2,1)S(1)} %get-tuple-element.507), channel_id=1, source_target_pairs={{0,4},{4,0},{8,12},{12,8},{16,20},{20,16},{24,28},{28,24},{1,5},{5... | collective-permute-start | bytes 995336 | tf_op jit(solution)/shard_map/ppermute | solution.py:118
  170.2 15.3 %collective-permute-start.43 = (bf16[144,1152]{1,0:T(8,128)(2,1)S(1)}, bf16[144,1152]{1,0:T(8,128)(2,1)S(1)}, u32[]{:S(2)}, u32[]{:S(2)}) collective-permute-start(bf16[144,1152]{1,0:T(8,128)(2,1)S(1)} %get-tuple-element.506), channel_id=1, source_target_pairs={{0,8},{4,12},{8,16},{12,20},{16,24},{20,28},{24,0},{28,4},{1,9},{5... | collective-permute-start | bytes 995336 | tf_op jit(solution)/shard_map/ppermute | solution.py:121
  170.3 21.7 %collective-permute-start.46 = (bf16[144,1152]{1,0:T(8,128)(2,1)S(1)}, bf16[144,1152]{1,0:T(8,128)(2,1)S(1)}, u32[]{:S(2)}, u32[]{:S(2)}) collective-permute-start(bf16[144,1152]{1,0:T(8,128)(2,1)S(1)} %get-tuple-element.517), channel_id=1, source_target_pairs={{0,4},{4,0},{8,12},{12,8},{16,20},{20,16},{24,28},{28,24},{1,5},{5... | collective-permute-start | bytes 995336 | tf_op jit(solution)/shard_map/ppermute | solution.py:118
  177.3 14.7 %collective-permute-start.45 = (bf16[144,1152]{1,0:T(8,128)(2,1)S(1)}, bf16[144,1152]{1,0:T(8,128)(2,1)S(1)}, u32[]{:S(2)}, u32[]{:S(2)}) collective-permute-start(bf16[144,1152]{1,0:T(8,128)(2,1)S(1)} %get-tuple-element.516), channel_id=1, source_target_pairs={{0,8},{4,12},{8,16},{12,20},{16,24},{20,28},{24,0},{28,4},{1,9},{5... | collective-permute-start | bytes 995336 | tf_op jit(solution)/shard_map/ppermute | solution.py:121
  182.8 14.5 %collective-permute-start.56 = (bf16[144,1152]{1,0:T(8,128)(2,1)S(1)}, bf16[144,1152]{1,0:T(8,128)(2,1)S(1)}, u32[]{:S(2)}, u32[]{:S(2)}) collective-permute-start(bf16[144,1152]{1,0:T(8,128)(2,1)S(1)} %get-tuple-element.544), channel_id=1, source_target_pairs={{0,4},{4,0},{8,12},{12,8},{16,20},{20,16},{24,28},{28,24},{1,5},{5... | collective-permute-start | bytes 995336 | tf_op jit(solution)/shard_map/ppermute | solution.py:118
  199.2 12.9 %collective-permute-start.58 = (bf16[144,1152]{1,0:T(8,128)(2,1)S(1)}, bf16[144,1152]{1,0:T(8,128)(2,1)S(1)}, u32[]{:S(2)}, u32[]{:S(2)}) collective-permute-start(bf16[144,1152]{1,0:T(8,128)(2,1)S(1)} %get-tuple-element.551), channel_id=1, source_target_pairs={{0,4},{4,0},{8,12},{12,8},{16,20},{20,16},{24,28},{28,24},{1,5},{5... | collective-permute-start | bytes 995336 | tf_op jit(solution)/shard_map/ppermute | solution.py:118
  200.9 17.3 %collective-permute-start.57 = (bf16[144,1152]{1,0:T(8,128)(2,1)S(1)}, bf16[144,1152]{1,0:T(8,128)(2,1)S(1)}, u32[]{:S(2)}, u32[]{:S(2)}) collective-permute-start(bf16[144,1152]{1,0:T(8,128)(2,1)S(1)} %get-tuple-element.550), channel_id=1, source_target_pairs={{0,8},{4,12},{8,16},{12,20},{16,24},{20,28},{24,0},{28,4},{1,9},{5... | collective-permute-start | bytes 995336 | tf_op jit(solution)/shard_map/ppermute | solution.py:121
  201.6 17.4 %collective-permute-start.60 = (bf16[144,1152]{1,0:T(8,128)(2,1)S(1)}, bf16[144,1152]{1,0:T(8,128)(2,1)S(1)}, u32[]{:S(2)}, u32[]{:S(2)}) collective-permute-start(bf16[144,1152]{1,0:T(8,128)(2,1)S(1)} %get-tuple-element.557), channel_id=1, source_target_pairs={{0,4},{4,0},{8,12},{12,8},{16,20},{20,16},{24,28},{28,24},{1,5},{5... | collective-permute-start | bytes 995336 | tf_op jit(solution)/shard_map/ppermute | solution.py:118
  202.7 24.7 %collective-permute-start.61 = (bf16[256,1152]{1,0:T(8,128)(2,1)S(1)}, bf16[256,1152]{1,0:T(8,128)(2,1)S(1)}, u32[]{:S(2)}, u32[]{:S(2)}) collective-permute-start(bf16[256,1152]{1,0:T(8,128)(2,1)S(1)} %get-tuple-element.562), channel_id=1, source_target_pairs={{0,2},{1,3},{2,0},{3,1},{4,6},{5,7},{6,4},{7,5},{8,10},{9,11},{10,... | collective-permute-start | bytes 1769480 | tf_op jit(solution)/shard_map/ppermute | solution.py:115
  211.8 13.6 %collective-permute-start.59 = (bf16[144,1152]{1,0:T(8,128)(2,1)S(1)}, bf16[144,1152]{1,0:T(8,128)(2,1)S(1)}, u32[]{:S(2)}, u32[]{:S(2)}) collective-permute-start(bf16[144,1152]{1,0:T(8,128)(2,1)S(1)} %get-tuple-element.556), channel_id=1, source_target_pairs={{0,8},{4,12},{8,16},{12,20},{16,24},{20,28},{24,0},{28,4},{1,9},{5... | collective-permute-start | bytes 995336 | tf_op jit(solution)/shard_map/ppermute | solution.py:121
  212.1 15.3 %collective-permute-start.63 = (bf16[144,1152]{1,0:T(8,128)(2,1)S(1)}, bf16[144,1152]{1,0:T(8,128)(2,1)S(1)}, u32[]{:S(2)}, u32[]{:S(2)}) collective-permute-start(bf16[144,1152]{1,0:T(8,128)(2,1)S(1)} %get-tuple-element.571), channel_id=1, source_target_pairs={{0,4},{4,0},{8,12},{12,8},{16,20},{20,16},{24,28},{28,24},{1,5},{5... | collective-permute-start | bytes 995336 | tf_op jit(solution)/shard_map/ppermute | solution.py:118
  218.9 12.7 %collective-permute-start.62 = (bf16[144,1152]{1,0:T(8,128)(2,1)S(1)}, bf16[144,1152]{1,0:T(8,128)(2,1)S(1)}, u32[]{:S(2)}, u32[]{:S(2)}) collective-permute-start(bf16[144,1152]{1,0:T(8,128)(2,1)S(1)} %get-tuple-element.570), channel_id=1, source_target_pairs={{0,8},{4,12},{8,16},{12,20},{16,24},{20,28},{24,0},{28,4},{1,9},{5... | collective-permute-start | bytes 995336 | tf_op jit(solution)/shard_map/ppermute | solution.py:121
  219.0 13.3 %collective-permute-start.64 = (bf16[144,1152]{1,0:T(8,128)(2,1)S(1)}, bf16[144,1152]{1,0:T(8,128)(2,1)S(1)}, u32[]{:S(2)}, u32[]{:S(2)}) collective-permute-start(bf16[144,1152]{1,0:T(8,128)(2,1)S(1)} %get-tuple-element.580), channel_id=1, source_target_pairs={{0,4},{4,0},{8,12},{12,8},{16,20},{20,16},{24,28},{28,24},{1,5},{5... | collective-permute-start | bytes 995336 | tf_op jit(solution)/shard_map/ppermute | solution.py:118
  227.4 14.3 %collective-permute-start.68 = (bf16[144,1152]{1,0:T(8,128)(2,1)S(1)}, bf16[144,1152]{1,0:T(8,128)(2,1)S(1)}, u32[]{:S(2)}, u32[]{:S(2)}) collective-permute-start(bf16[144,1152]{1,0:T(8,128)(2,1)S(1)} %get-tuple-element.599), channel_id=1, source_target_pairs={{0,4},{4,0},{8,12},{12,8},{16,20},{20,16},{24,28},{28,24},{1,5},{5... | collective-permute-start | bytes 995336 | tf_op jit(solution)/shard_map/ppermute | solution.py:118
  259.0 18.4 %collective-permute-start.84 = (bf16[256,1152]{1,0:T(8,128)(2,1)S(1)}, bf16[256,1152]{1,0:T(8,128)(2,1)S(1)}, u32[]{:S(2)}, u32[]{:S(2)}) collective-permute-start(bf16[256,1152]{1,0:T(8,128)(2,1)S(1)} %get-tuple-element.647), channel_id=1, source_target_pairs={{0,2},{1,3},{2,0},{3,1},{4,6},{5,7},{6,4},{7,5},{8,10},{9,11},{10,... | collective-permute-start | bytes 1769480 | tf_op jit(solution)/shard_map/ppermute | solution.py:115
  259.9 13.4 %collective-permute-start.81 = (bf16[144,1152]{1,0:T(8,128)(2,1)S(1)}, bf16[144,1152]{1,0:T(8,128)(2,1)S(1)}, u32[]{:S(2)}, u32[]{:S(2)}) collective-permute-start(bf16[144,1152]{1,0:T(8,128)(2,1)S(1)} %get-tuple-element.635), channel_id=1, source_target_pairs={{0,4},{4,0},{8,12},{12,8},{16,20},{20,16},{24,28},{28,24},{1,5},{5... | collective-permute-start | bytes 995336 | tf_op jit(solution)/shard_map/ppermute | solution.py:118
  279.4 17.2 %collective-permute-start.92 = (f32[128,1152]{1,0:T(8,128)}, f32[128,1152]{1,0:T(8,128)S(1)}, u32[]{:S(2)}, u32[]{:S(2)}) collective-permute-start(f32[128,1152]{1,0:T(8,128)} %get-tuple-element.665), channel_id=1, source_target_pairs={{0,1},{1,0},{2,3},{3,2},{4,5},{5,4},{6,7},{7,6},{8,9},{9,8},{10,11... | collective-permute-start | bytes 1769480 | tf_op jit(solution)/shard_map/ppermute | solution.py:112
  (71 other events, 544.3 us)
